TPU v7x, 512 devices: a whole 4x8x8 slice. The times are simulated.
512 devices in a mesh: section: 4 (over z_hi), blk: 8 (over y), uly: 16 (over z_lo, x, core).
Axes of the slice: x: 4, y: 8, z: 8 (z_hi: 4, z_lo: 2; z = z_hi * 2 + z_lo), core: 2. Of those that a mesh axis runs over, the one named last changes fastest.
Arguments:
- stale: bfloat16 [4, 1280, 6144], P('section', ('blk', 'uly')), may hold values from -6 to 6
- layer_of_section: int32 [4], P('section'), may hold values from 0 to 15, as said below
- mod_table: float32 [16, 2, 6144], replicated, may hold values from -3 to 3
- w_qkv: bfloat16 [4, 6144, 48, 3, 128], P('section', 'blk', 'uly'), may hold values from -0.076546554 to 0.076546554
- q_gain: float32 [4, 48, 128], P('section', 'uly'), may hold values from 0.25 to 5.2
- k_gain: float32 [4, 48, 128], P('section', 'uly'), may hold values from 0.25 to 5.2
- counts: int32 [8], P('blk'), may hold values from 1 to 160, as said below
Outputs:
- mixed: bfloat16 [4, 1280, 6144], P('section', ('blk', 'uly'))
Inputs may be any that keep to these rules, and one draw needn't show every extreme that they name: `layer_of_section`: each section runs a different layer; the first and the last layer are both run. `counts`: the valid tokens of a subgroup are its first ones; some subgroup is full.
All inputs are finite; a program needn't handle non-finite values.
Results may differ from a plain program's by a relative error of at most 0.029.
Values may be sent and summed in bfloat16 or wider, within the bound.
No kernel may reach another device: no remote copies, remote signals or barrier semaphores. Data moves between devices by JAX's collectives and lax.ppermute only.
A program may use at most 64 MiB of HBM per device.

v0:
```python
import jax
import jax.numpy as jnp
from jax import lax
from jax.sharding import PartitionSpec as P


def from_behind(value, axis, steps):
    count = lax.axis_size(axis)
    pairs = [(source, (source + steps) % count) for source in range(count)]
    return lax.ppermute(value, axis, pairs)


def head_norm(values, gain):
    scale = jnp.sqrt(jnp.mean(values * values, axis=-1, keepdims=True) + 1e-06)
    return values / scale * gain[None]


def on_device(stale, layer_of_section, mod_table, w_qkv, q_gain, k_gain, counts):
    tok_rows = stale.shape[1]
    width = stale.shape[2]
    groups = lax.axis_size("uly")
    slice_width = w_qkv.shape[1]
    heads_dev = w_qkv.shape[2]
    head_size = w_qkv.shape[4]
    columns = heads_dev * 3 * head_size
    received = from_behind(stale[0], "section", 1)
    source = received.astype(jnp.float32)
    pick = (jnp.arange(mod_table.shape[0]) == layer_of_section[0]).astype(jnp.float32)
    modul = jnp.einsum("l,lcd->cd", pick, mod_table, precision=lax.Precision.HIGHEST)
    spread = jnp.sqrt(jnp.mean(source * source, axis=-1, keepdims=True) + 1e-06)
    normed = (source / spread * (1.0 + modul[1]) + modul[0]).astype(jnp.bfloat16)
    weights = w_qkv[0].reshape(slice_width, columns)
    sub_rows = tok_rows * groups
    subgroup = lax.all_gather(normed, "uly", axis=0, tiled=True)
    empty = jnp.zeros((sub_rows, columns), jnp.float32)
    total = empty
    piece = lax.all_gather(weights, "blk", axis=0, tiled=True)
    for index in range(piece.shape[0] // slice_width):
        block = lax.dynamic_slice_in_dim(piece, index * slice_width, slice_width, 0)
        feats = lax.dynamic_slice_in_dim(subgroup, index * slice_width, slice_width, 1)
        product = jnp.dot(feats, block, preferred_element_type=jnp.float32)
        total = total + lax.optimization_barrier(product.astype(jnp.bfloat16)).astype(jnp.float32)
    qkv = total
    qkv = qkv.reshape(sub_rows, heads_dev, 3, head_size)
    query = head_norm(qkv[:, :, 0], q_gain[0]).astype(jnp.bfloat16)
    key_part = head_norm(qkv[:, :, 1], k_gain[0]).astype(jnp.bfloat16)
    value = qkv[:, :, 2].astype(jnp.bfloat16)
    keys, values, all_counts = (
        lax.all_gather(key_part, "blk", axis=0, tiled=True),
        lax.all_gather(value, "blk", axis=0, tiled=True),
        lax.all_gather(counts, "blk", axis=0, tiled=True),
    )
    total_keys = keys.shape[0]
    position = jnp.arange(total_keys) % sub_rows
    limit = jnp.repeat(all_counts, sub_rows)
    valid = position < limit
    scores = jnp.einsum("qhd,khd->hqk", query, keys, preferred_element_type=jnp.float32) / jnp.sqrt(
        jnp.float32(head_size)
    )
    scores = jnp.where(valid[None, None, :], scores, -1e30)
    top = jnp.max(scores, axis=-1, keepdims=True)
    expo = jnp.exp(scores - top)
    denom = jnp.sum(expo, axis=-1)
    probs = expo.astype(jnp.bfloat16)
    mixed = jnp.einsum("hqk,khd->qhd", probs, values, preferred_element_type=jnp.float32)
    mixed = (mixed / jnp.transpose(denom)[:, :, None]).astype(jnp.bfloat16)
    returned = lax.all_to_all(mixed, "uly", split_axis=0, concat_axis=1, tiled=True)
    return returned.reshape(1, tok_rows, width)


def solution(mesh):
    in_specs = (
        P("section", ("blk", "uly"), None),
        P("section"),
        P(),
        P("section", "blk", "uly", None, None),
        P("section", "uly", None),
        P("section", "uly", None),
        P("blk"),
    )
    out_specs = P("section", ("blk", "uly"), None)
    return jax.shard_map(
        on_device, mesh=mesh, in_specs=in_specs, out_specs=out_specs, check_vma=False
    )
```

profile of v0, /device:TPU:6, one launch (start us, length us, event | category | flops | bytes accessed | tf_op | source)
XLA Modules:
  0.0 314.5 jit_solution(8141140409822076245)
XLA Ops:
  6.5 0.0 copy-start
  6.5 0.0 copy-start.1
  6.5 0.0 all-gather.7.cloned.1.call-start
  6.5 6.2 %collective-permute-start = (bf16[10,6144]{1,0:T(8,128)(2,1)}, bf16[10,6144]{1,0:T(8,128)(2,1)S(1)}, u32[]{:S(2)}, u32[]{:S(2)}) collective-permute-start(bf16[10,6144]{1,0:T(8,128)(2,1)} %bitcast.63), channel_id=1, source_target_pairs={{0,128},{128,256},{256,384},{384,0},{1,129},{129,257},{257,385},{3... | collective-permute-start | bytes 368648 | tf_op jit(solution)/shard_map/ppermute | solution.py:10
  13.4 0.0 copy-done
  13.4 0.8 fusion.24
  14.3 8.5 %collective-permute-done = bf16[10,6144]{1,0:T(8,128)(2,1)S(1)} collective-permute-done((bf16[10,6144]{1,0:T(8,128)(2,1)}, bf16[10,6144]{1,0:T(8,128)(2,1)S(1)}, u32[]{:S(2)}, u32[]{:S(2)}) %collective-permute-start) | collective-permute-done | bytes 122912 | tf_op jit(solution)/shard_map/ppermute | solution.py:10
  22.8 0.2 fusion.26
  23.0 0.8 fusion.41
  23.9 0.0 all-gather.7.cloned.1.call-update
  23.9 0.0 copy-start.2
  23.9 0.0 copy-start.3
  23.9 0.0 all-gather.5.cloned.1.call-start
  24.0 0.0 copy-done.1
  24.0 2.2 copy.23
  26.2 0.0 all-gather.5.cloned.1.call-update
  26.8 1.3 dynamic-slice
  28.1 0.7 dynamic-update-slice
  28.8 14.1 %all-reduce = s32[8]{0:T(128)S(1)} all-reduce(s32[8]{0:T(128)S(1)} %dynamic-update-slice), channel_id=1, replica_groups=mesh['section'=4,'blk'=8,'uly'=16] {'blk'}, use_global_device_ids=true, to_apply=%add | all-reduce | flops 8 | bytes 64
  42.9 0.0 copy-done.2
  42.9 0.1 broadcast_in_dim.14
  42.9 0.1 reshape.52
  43.0 0.0 copy-done.3
  43.0 24.9 %all-gather.7.cloned.1.call-done = bf16[16,10,6144]{2,1,0:T(8,128)(2,1)} async-done(((bf16[1,10,6144]{2,1,0:T(8,128)(2,1)}), bf16[16,10,6144]{2,1,0:T(8,128)(2,1)}) %all-gather.7.cloned.1.call-update) | async-done | bytes 1966096 | tf_op jit(solution)/shard_map/all_gather | solution.py:34
  67.9 2.9 reshape.59
  70.9 150.5 %all-gather.5.cloned.1.call-done = bf16[6144,1152]{0,1:T(8,128)(2,1)} async-done(((bf16[768,1152]{0,1:T(8,128)(2,1)}), bf16[6144,1152]{0,1:T(8,128)(2,1)}) %all-gather.5.cloned.1.call-update) | async-done | bytes 14155792 | tf_op jit(solution)/shard_map/all_gather | solution.py:37
  221.4 2.2 convolution_convert_fusion.7
  223.6 2.2 convolution_convert_fusion.6
  225.8 2.2 convolution_convert_fusion.5
  228.0 2.2 convolution_convert_fusion.4
  230.2 2.2 convolution_convert_fusion.3
  232.4 2.2 convolution_convert_fusion.2
  234.6 2.2 convolution_convert_fusion.1
  236.8 2.2 convolution_convert_fusion
  239.0 0.4 convert_add_fusion
  239.4 0.3 reshape.51
  239.7 0.4 fusion.53
  240.1 0.3 slice.25
  240.3 0.2 multiply_reduce_fusion
  240.5 0.1 multiply_convert_fusion
  240.7 26.8 %all_gather.19 = bf16[1280,3,128]{2,0,1:T(8,128)(2,1)S(1)} all-gather(bf16[160,3,128]{2,0,1:T(8,128)(2,1)S(1)} %multiply_convert_fusion), channel_id=1, replica_groups=mesh['section'=4,'blk'=8,'uly'=16] {'blk'}, dimensions={0}, use_global_device_ids=true | all-gather | bytes 1105920 | tf_op jit(solution)/shard_map/all_gather | solution.py:49
  267.5 0.2 fusion.38
  267.7 26.5 %all-gather = bf16[1280,3,1,128]{3,0,1,2:T(8,128)(2,1)S(1)} all-gather(bf16[160,3,1,128]{3,0,1,2:T(8,128)(2,1)S(1)} %copy.52), channel_id=2, replica_groups=mesh['section'=4,'blk'=8,'uly'=16] {'blk'}, dimensions={0}, use_global_device_ids=true | all-gather | bytes 1105920 | tf_op jit(solution)/shard_map/all_gather | solution.py:50
  294.2 0.7 fusion.54
  294.9 0.5 fusion.1
  295.4 0.6 fusion.20
  296.0 0.1 copy.27
  296.1 10.6 %all_to_all.15 = bf16[160,3,128]{2,1,0:T(4,128)(2,1)S(1)} all-to-all(bf16[160,3,128]{2,1,0:T(4,128)(2,1)S(1)} %copy.27), channel_id=1, replica_groups=mesh['section'=4,'blk'=8,'uly'=16] {'uly'}, dimensions={0} | all-to-all | bytes 245760 | tf_op jit(solution)/shard_map/all_to_all | solution.py:67
  306.8 0.1 copy.29
  306.9 0.8 reshape.53
  (11 shorter events, 0.2 us)
Async XLA Ops:
  6.5 6.9 %copy-start = (f32[16,2,6144]{2,1,0:T(2,128)S(1)}, f32[16,2,6144]{2,1,0:T(2,128)}, u32[]{:S(2)}) copy-start(f32[16,2,6144]{2,1,0:T(2,128)} %param.9) | copy-start | bytes 2359300
  6.5 17.4 %copy-start.1 = (bf16[1,768,3,3,128]{4,1,3,2,0:T(8,128)(2,1)S(1)}, bf16[1,768,3,3,128]{4,1,3,2,0:T(8,128)(2,1)}, u32[]{:S(2)}) copy-start(bf16[1,768,3,3,128]{4,1,3,2,0:T(8,128)(2,1)} %param.10) | copy-start | bytes 5308420
  6.5 61.4 %all-gather.7.cloned.1.call-start = ((), (), s32[]{:S(2)}) async-start(), calls=%async_computation.2 | async-start | bytes 3342336 | tf_op jit(solution)/shard_map/all_gather | solution.py:34
  6.5 16.3 %collective-permute-start = (bf16[10,6144]{1,0:T(8,128)(2,1)}, bf16[10,6144]{1,0:T(8,128)(2,1)S(1)}, u32[]{:S(2)}, u32[]{:S(2)}) collective-permute-start(bf16[10,6144]{1,0:T(8,128)(2,1)} %bitcast.63), channel_id=1, source_target_pairs={{0,128},{128,256},{256,384},{384,0},{1,129},{129,257},{257,385},{3... | collective-permute-start | bytes 368648 | tf_op jit(solution)/shard_map/ppermute | solution.py:10
  23.9 19.0 %copy-start.2 = (f32[1,3,128]{2,0,1:T(1,128)S(1)}, f32[1,3,128]{2,0,1:T(1,128)}, u32[]{:S(2)}) copy-start(f32[1,3,128]{2,0,1:T(1,128)} %param.12) | copy-start | bytes 4612
  23.9 19.1 %copy-start.3 = (f32[1,3,128]{2,0,1:T(1,128)S(1)}, f32[1,3,128]{2,0,1:T(1,128)}, u32[]{:S(2)}) copy-start(f32[1,3,128]{2,0,1:T(1,128)} %param.11) | copy-start | bytes 4612
  23.9 197.5 %all-gather.5.cloned.1.call-start = ((), (), s32[]{:S(2)}) async-start(), calls=%async_computation.1 | async-start | bytes 15925248 | tf_op jit(solution)/shard_map/all_gather | solution.py:37
Sparse Core Ops, SparseCore 0:
  24.0 43.8 all-gather.6
  70.0 151.3 all-gather.4
where the time goes:
time: 318 us; the launch traced here: 315 us
  waiting for transfers between devices  184 us (58%)
  blocking collectives  78 us (25%)
  matrix products  19.6 us (6%)
  between operations  14.9 us (5%)
  local copies, waits for them, and re-layouts  9.29 us (3%)
  starting transfers between devices  6.25 us (2%)
    all_gather x1, waiting for transfers between devices, on_device(): piece = lax.all_gather(weights, 'blk', axis=0, tiled=True)  151 us
    all_gather x1, blocking collectives, on_device(): lax.all_gather(key_part, 'blk', axis=0, tiled=True)  26.8 us
    all_gather x1, blocking collectives, on_device(): lax.all_gather(value, 'blk', axis=0, tiled=True)  26.5 us
    all_gather x1, waiting for transfers between devices, on_device(): subgroup = lax.all_gather(normed, 'uly', axis=0, tiled=True)  24.9 us
    dot_general x8, matrix products, on_device(): product = jnp.dot(feats, block, preferred_element_type=jnp.float32)  17.5 us
    unnamed x1, blocking collectives  14.1 us
    all_to_all x1, blocking collectives, on_device(): lax.all_to_all(mixed, 'uly', split_axis=0, concat_axis=1, tiled=True)  10.6 us
    ppermute x1, waiting for transfers between devices, from_behind(): return lax.ppermute(value, axis, pairs)  8.5 us
  transfers between devices with their start and end apart: 3, of which 3 were waited for; matrix products, arithmetic and copies ran while one was open for 3% of the time, Pallas kernels for 0%

commit v1 on v0

v1 whole, which is shorter than its diff:
```python
import jax
import jax.numpy as jnp
from jax import lax
from jax.sharding import Mesh
from jax.sharding import PartitionSpec as P

AXES = ("section", "blk", "zlo", "x", "core")
CHIPS = ("zlo", "x")


def shifted(value, axis, steps):
    count = lax.axis_size(axis)
    pairs = [(source, (source + steps) % count) for source in range(count)]
    return lax.ppermute(value, axis, pairs)


def head_norm(values, gain):
    scale = jnp.sqrt(jnp.mean(values * values, axis=-1, keepdims=True) + 1e-06)
    return values / scale * gain


def on_device(stale, layer_of_section, mod_table, w_qkv, q_gain, k_gain, counts):
    tok_rows, width = stale.shape[1:]
    blks = lax.axis_size("blk")
    cores = lax.axis_size("core")
    chips = lax.axis_size("zlo") * lax.axis_size("x")
    slice_width, heads_dev = w_qkv.shape[1:3]
    head_size = w_qkv.shape[4]
    part = 3 * head_size
    heads_chip = cores * heads_dev
    sub_rows = tok_rows * chips * cores
    core = lax.axis_index("core")
    row = lax.axis_index("blk")

    weights = w_qkv[0].reshape(slice_width, heads_dev * part)
    weights = lax.all_gather(weights, "core", axis=0, tiled=False)
    gains = jnp.stack([q_gain[0], k_gain[0]])
    other = shifted(gains, "core", 1)
    gains = jnp.where(core == 0, jnp.stack([gains, other]), jnp.stack([other, gains]))
    owned = jnp.minimum(row, heads_chip - 1)
    gain = lax.dynamic_index_in_dim(
        gains.transpose(0, 2, 1, 3).reshape(heads_chip, 2, head_size), owned, 0, keepdims=False
    )

    received = shifted(stale[0], "section", 1)
    source = received.astype(jnp.float32)
    modul = lax.dynamic_index_in_dim(mod_table, layer_of_section[0], 0, keepdims=False)
    spread = jnp.sqrt(jnp.mean(source * source, axis=-1, keepdims=True) + 1e-06)
    normed = (source / spread * (1.0 + modul[1]) + modul[0]).astype(jnp.bfloat16)
    count_row = jnp.broadcast_to(counts.astype(jnp.bfloat16)[:, None], (6, width))
    sent = jnp.concatenate([normed, count_row], axis=0)
    sent = sent.reshape(sent.shape[0], blks, slice_width).transpose(1, 0, 2)
    sliced = lax.all_to_all(sent, "blk", 0, 0, tiled=False)
    all_counts = sliced[:, tok_rows, 0].astype(jnp.int32)
    mine = sliced[:, :tok_rows].reshape(blks * tok_rows, slice_width)
    copies = jnp.broadcast_to(mine[None], (chips,) + mine.shape)
    tokens = lax.all_to_all(copies, CHIPS, 0, 0, tiled=False)
    tokens = tokens.reshape(chips * blks * tok_rows, slice_width)
    rows = tokens.shape[0]

    products = []
    for index in range(cores):
        product = jnp.dot(tokens, weights[index], preferred_element_type=jnp.float32)
        product = product.astype(jnp.bfloat16).reshape(rows, heads_dev, part)
        products.append(product.transpose(1, 0, 2))
    products.append(jnp.zeros((blks - heads_chip, rows, part), jnp.bfloat16))
    products = jnp.concatenate(products, axis=0)
    qkv = lax.psum_scatter(products, "blk", scatter_dimension=0, tiled=False)
    qkv = qkv.astype(jnp.float32)
    query = head_norm(qkv[:, :head_size], gain[0]).astype(jnp.bfloat16)
    key_part = head_norm(qkv[:, head_size : 2 * head_size], gain[1]).astype(jnp.bfloat16)
    value = qkv[:, 2 * head_size :].astype(jnp.bfloat16)
    pair = jnp.concatenate([key_part, value], axis=1)
    pairs = jnp.concatenate([pair, shifted(pair, "core", 1)], axis=0)
    keys, values = pairs[:, :head_size], pairs[:, head_size:]

    lane = jnp.arange(cores)[:, None, None, None]
    lane = jnp.where(lane == 0, core, 1 - core)
    chip = jnp.arange(chips)[None, :, None, None]
    token = jnp.arange(tok_rows)[None, None, None, :]
    position = (chip * cores + lane) * tok_rows + token
    valid = (position < all_counts[None, None, :, None]).reshape(1, cores * rows)
    scores = jnp.dot(query, keys.T, preferred_element_type=jnp.float32) / jnp.sqrt(
        jnp.float32(head_size)
    )
    scores = jnp.where(valid, scores, -1e30)
    top = jnp.max(scores, axis=-1, keepdims=True)
    expo = jnp.exp(scores - top)
    denom = jnp.sum(expo, axis=-1, keepdims=True)
    mixed = jnp.dot(expo.astype(jnp.bfloat16), values, preferred_element_type=jnp.float32)
    mixed = (mixed / denom).astype(jnp.bfloat16)

    mixed = mixed.reshape(chips, blks, tok_rows, head_size).transpose(1, 0, 2, 3)
    mixed = mixed.reshape(blks * chips, tok_rows, head_size)
    returned = lax.all_to_all(mixed, ("blk",) + CHIPS, 0, 0, tiled=False)
    returned = returned.reshape(blks, chips, tok_rows, head_size)[:heads_chip]
    return returned.transpose(2, 1, 0, 3).reshape(1, tok_rows, width)


def solution(mesh):
    sizes = mesh.shape
    fine = Mesh(mesh.devices.reshape(sizes["section"], sizes["blk"], 2, 4, 2), AXES)
    uly = CHIPS + ("core",)
    in_specs = (
        P("section", ("blk",) + uly, None),
        P("section"),
        P(),
        P("section", "blk", uly, None, None),
        P("section", uly, None),
        P("section", uly, None),
        P("blk"),
    )
    out_specs = P("section", ("blk",) + uly, None)
    return jax.shard_map(
        on_device, mesh=fine, in_specs=in_specs, out_specs=out_specs, check_vma=False
    )
```

time: 318 us -> 162 us (0.51)
  waiting for transfers between devices: 184 us -> 60 us
  blocking collectives: 78 us -> 38.3 us
  starting transfers between devices: 6.25 us -> 20.4 us
  matrix products: 19.6 us -> 8.72 us
  local copies, waits for them, and re-layouts: 9.29 us -> 14 us
    all_gather x2 -> x1, waiting for transfers between devices: 175 us -> 0.01 us  [on_device(): weights = lax.all_gather(weights, 'core', axis=0, tiled=False)]
    all_gather x2 -> x0, blocking collectives: 53.3 us -> none  [the longest x1 26.8 us: on_device(): lax.all_gather(key_part, 'blk', axis=0, tiled=True)]
    reduce_scatter x0 -> x1, waiting for transfers between devices: none -> 43.6 us  [on_device(): qkv = lax.psum_scatter(products, 'blk', scatter_dimension=0, tiled=False)]
    all_to_all x1 -> x2, blocking collectives: 10.6 us -> 38.3 us  [the longest x1 21.5 us: on_device(): returned = lax.all_to_all(mixed, ('blk',) + CHIPS, 0, 0, tiled=False)]
    unnamed x1 -> x0, blocking collectives: 14.1 us -> none
    all_to_all x0 -> x1, waiting for transfers between devices: none -> 11.1 us  [on_device(): tokens = lax.all_to_all(copies, CHIPS, 0, 0, tiled=False)]
    dot_general x11 -> x4, matrix products: 19.6 us -> 8.72 us  [the longest x2 7.26 us: on_device(): jnp.dot(tokens, weights[index], preferred_element_type=jnp.float32)]
    all_to_all x0 -> x1, starting transfers between devices: none -> 10.5 us  [on_device(): tokens = lax.all_to_all(copies, CHIPS, 0, 0, tiled=False)]
  transfers between devices with their start and end apart: 3 -> 6, of which waited for: 3 -> 5; matrix products, arithmetic and copies ran while one was open for 3% -> 5% of each run, Pallas kernels for 0% -> 0%
where the time goes in v1:
time: 162 us
  waiting for transfers between devices  60 us (37%)
  blocking collectives  38.3 us (24%)
  starting transfers between devices  20.4 us (13%)
  between operations  14.9 us (9%)
  local copies, waits for them, and re-layouts  14 us (9%)
  matrix products  8.72 us (5%)
  other arithmetic  5.34 us (3%)
    reduce_scatter x1, waiting for transfers between devices, on_device(): qkv = lax.psum_scatter(products, 'blk', scatter_dimension=0, tiled=False)  43.6 us
    all_to_all x1, blocking collectives, on_device(): returned = lax.all_to_all(mixed, ('blk',) + CHIPS, 0, 0, tiled=False)  21.5 us
    all_to_all x1, blocking collectives, on_device(): sliced = lax.all_to_all(sent, 'blk', 0, 0, tiled=False)  16.8 us
    all_to_all x1, waiting for transfers between devices, on_device(): tokens = lax.all_to_all(copies, CHIPS, 0, 0, tiled=False)  11.1 us
    all_to_all x1, starting transfers between devices, on_device(): tokens = lax.all_to_all(copies, CHIPS, 0, 0, tiled=False)  10.5 us
    ppermute x3, starting transfers between devices, shifted(): return lax.ppermute(value, axis, pairs)  9.92 us
    dot_general x2, matrix products, on_device(): jnp.dot(tokens, weights[index], preferred_element_type=jnp.float32)  7.26 us
    ppermute x3, waiting for transfers between devices, shifted(): return lax.ppermute(value, axis, pairs)  5.26 us
  transfers between devices with their start and end apart: 6, of which 5 were waited for; matrix products, arithmetic and copies ran while one was open for 5% of the time, Pallas kernels for 0%

profile of v1, /device:TPU:6, one launch (start us, length us, event | category | flops | bytes accessed | tf_op | source)
XLA Modules:
  0.0 161.7 jit_solution(17847927041842915466)
XLA Ops:
  6.5 0.0 all-gather.2.cloned.1.call-start
  6.5 6.1 %collective-permute-start = (bf16[10,6144]{1,0:T(8,128)(2,1)}, bf16[10,6144]{1,0:T(8,128)(2,1)S(1)}, u32[]{:S(2)}, u32[]{:S(2)}) collective-permute-start(bf16[10,6144]{1,0:T(8,128)(2,1)} %bitcast.70), channel_id=1, source_target_pairs={{0,128},{128,256},{256,384},{384,0},{1,129},{129,257},{257,385},{3... | collective-permute-start | bytes 368648 | tf_op jit(solution)/shard_map/ppermute | solution.py:14
  12.6 2.6 %copy.24 = bf16[1,768,3,3,128]{1,4,3,2,0:T(8,128)(2,1)S(1)} copy(bf16[1,768,3,3,128]{4,1,3,2,0:T(8,128)(2,1)} %param.10) | data formatting | bytes 3538944 | tf_op args[3]
  15.3 2.2 %copy.25 = bf16[1,768,1152]{2,1,0:T(8,128)(2,1)} copy(bf16[1,768,1152]{1,2,0:T(8,128)(2,1)S(1)} %bitcast.54) | data formatting | bytes 3538944 | tf_op jit(solution)/shard_map/all_gather;reshape;squeeze | solution.py:36
  17.5 0.0 all-gather.2.cloned.1.call-update
  18.2 0.9 dynamic-slice_add_fusion
  19.7 3.0 %collective-permute-done = bf16[10,6144]{1,0:T(8,128)(2,1)S(1)} collective-permute-done((bf16[10,6144]{1,0:T(8,128)(2,1)}, bf16[10,6144]{1,0:T(8,128)(2,1)S(1)}, u32[]{:S(2)}, u32[]{:S(2)}) %collective-permute-start) | collective-permute-done | bytes 122912 | tf_op jit(solution)/shard_map/ppermute | solution.py:14
  22.7 0.2 fusion.12
  22.9 0.1 fusion.15
  23.1 16.8 %all_to_all.15 = bf16[8,16,768]{2,1,0:T(8,128)(2,1)S(1)} all-to-all(bf16[8,16,768]{2,1,0:T(8,128)(2,1)S(1)} %bitcast.63), channel_id=1, replica_groups=mesh['section'=4,'blk'=8,'zlo'=2,'x'=4,'core'=2] {'blk'}, dimensions={0} | all-to-all | bytes 393216 | tf_op jit(solution)/shard_map/all_to_all | solution.py:53
  40.0 1.1 broadcast_in_dim.51
  41.0 10.5 %all-to-all-start.1 = ((bf16[8,80,768]{2,1,0:T(8,128)(2,1)}), bf16[8,80,768]{2,1,0:T(8,128)(2,1)S(1)}, u32[]{:S(2)}, u32[]{:S(2)}) async-start(bf16[8,80,768]{2,1,0:T(8,128)(2,1)} %broadcast_in_dim.51), calls=%async_computation.1 | async-start | bytes 1966080 | tf_op jit(solution)/shard_map/all_to_all | solution.py:57
  51.5 0.0 reduce-scatter.2.cloned.1.call-start
  51.5 0.1 pad.14.clone
  51.6 11.1 %all-to-all-done.1 = bf16[8,80,768]{2,1,0:T(8,128)(2,1)S(1)} async-done(((bf16[8,80,768]{2,1,0:T(8,128)(2,1)}), bf16[8,80,768]{2,1,0:T(8,128)(2,1)S(1)}, u32[]{:S(2)}, u32[]{:S(2)}) %all-to-all-start.1) | async-done | bytes 983072 | tf_op jit(solution)/shard_map/all_to_all | solution.py:57
  62.7 0.0 copy-start
  62.7 0.0 all-gather.2.cloned.1.call-done
  62.7 1.0 copy-done
  63.7 2.9 %convolution_convert_fusion.1 = bf16[640,1152]{1,0:T(8,128)(2,1)S(1)} fusion(bf16[640,768]{1,0:T(8,128)(2,1)S(1)} %bitcast.59, bf16[2,768,1152]{2,1,0:T(8,128)(2,1)} %all-gather.2.cloned.1.call-done), kind=kOutput, calls=%fused_computation.5 | convolution fusion | flops 1133199360 | bytes 4227072 | tf_op jit(solution)/shard_map/dot_general | solution.py:63
  66.6 1.0 copy.26
  67.6 4.3 %convolution_convert_fusion = bf16[640,1152]{1,0:T(8,128)(2,1)} fusion(bf16[640,768]{1,0:T(8,128)(2,1)} %bitcast.60, bf16[2,768,1152]{2,1,0:T(8,128)(2,1)} %all-gather.2.cloned.1.call-done), kind=kOutput, calls=%fused_computation.4 | convolution fusion | flops 1133199360 | bytes 4227072 | tf_op jit(solution)/shard_map/dot_general | solution.py:63
  71.9 2.6 %copy.27 = bf16[640,1152]{0,1:T(8,128)(2,1)S(1)} copy(bf16[640,1152]{1,0:T(8,128)(2,1)} %convolution_convert_fusion) | data formatting | bytes 2949120 | tf_op jit(solution)/shard_map/convert_element_type | solution.py:64
  74.5 2.4 %maximum_maximum_fusion = bf16[8,640,384]{1,2,0:T(8,128)(2,1)} fusion(bf16[3,640,384]{1,2,0:T(8,128)(2,1)S(1)} %bitcast.56, bf16[3,640,384]{1,2,0:T(8,128)(2,1)S(1)} %bitcast.55, bf16[8]{0:T(256)(128)(2,1)S(1)} %pad.14.clone), kind=kLoop, calls=%fused_computation | loop fusion | flops 3932160 | bytes 6881296 | tf_op jit(solution)/shard_map/concatenate | solution.py:67
  76.9 0.0 copy-start.1
  76.9 0.0 copy-start.2
  76.9 0.0 reduce-scatter.2.cloned.1.call-update
  76.9 0.7 copy-done.1
  77.5 0.0 copy-done.2
  77.6 1.9 %collective-permute-start.1 = (f32[2,3,128]{2,0,1:T(2,128)S(1)}, f32[2,3,128]{2,0,1:T(2,128)S(1)}, u32[]{:S(2)}, u32[]{:S(2)}) collective-permute-start(f32[2,3,128]{2,0,1:T(2,128)S(1)} %get-tuple-element.10), channel_id=1, source_target_pairs={{0,1},{1,0},{2,3},{3,2},{4,5},{5,4},{6,7},{7,6},{8,9},{9,8},{10,11... | collective-permute-start | bytes 9224 | tf_op jit(solution)/shard_map/ppermute | solution.py:14
  79.5 0.1 add_multiply_fusion
  79.6 0.1 iota_add_fusion
  79.7 0.9 collective-permute-done.1
  80.6 0.2 fusion.20
  80.9 43.6 %reduce-scatter.2.cloned.1.call-done = bf16[1,640,384]{1,2,0:T(8,128)(2,1)} async-done(((bf16[8,640,384]{1,2,0:T(8,128)(2,1)}), bf16[1,640,384]{1,2,0:T(8,128)(2,1)}) %reduce-scatter.2.cloned.1.call-update) | async-done | bytes 491536 | tf_op jit(solution)/shard_map/reduce_scatter | solution.py:68
  124.5 1.3 copy.28
  125.8 0.1 bitcast_convert_fusion
  125.9 0.2 multiply_reduce_fusion.1
  126.2 0.2 multiply_convert_fusion
  126.4 1.9 %collective-permute-start.2 = (bf16[640,256]{1,0:T(8,128)(2,1)S(1)}, bf16[640,256]{1,0:T(8,128)(2,1)S(1)}, u32[]{:S(2)}, u32[]{:S(2)}) collective-permute-start(bf16[640,256]{1,0:T(8,128)(2,1)S(1)} %pad_maximum_fusion.1), channel_id=1, source_target_pairs={{0,1},{1,0},{2,3},{3,2},{4,5},{5,4},{6,7},{7,6},{8,9},{9,8},{10,11... | collective-permute-start | bytes 983048 | tf_op jit(solution)/shard_map/ppermute | solution.py:14
  128.3 0.1 broadcast_compare_fusion
  128.4 0.1 lt.32
  128.6 1.3 collective-permute-done.2
  129.9 0.1 pad_maximum_fusion
  130.0 0.8 fusion.22
  130.8 0.6 fusion.1
  131.4 0.7 fusion.9
  132.1 0.1 reshape.151
  132.2 0.1 copy.39
  132.3 0.1 copy.30
  132.4 21.5 %all_to_all.16 = bf16[64,10,128]{2,1,0:T(8,128)(2,1)S(1)} all-to-all(bf16[64,10,128]{2,1,0:T(8,128)(2,1)S(1)} %copy.30), channel_id=1, replica_groups=mesh['section'=4,'blk'=8,'zlo'=2,'x'=4,'core'=2] {'blk','zlo','x'}, dimensions={0} | all-to-all | bytes 327680 | tf_op jit(solution)/shard_map/all_to_all | solution.py:95
  153.9 0.1 copy.32
  154.0 0.8 reshape.153
  (16 shorter events, 0.2 us)
Async XLA Ops:
  6.5 56.1 %all-gather.2.cloned.1.call-start = ((), (), s32[]{:S(2)}) async-start(), calls=%async_computation.4 | async-start | bytes 5308416 | tf_op jit(solution)/shard_map/all_gather | solution.py:36
  6.5 16.2 %collective-permute-start = (bf16[10,6144]{1,0:T(8,128)(2,1)}, bf16[10,6144]{1,0:T(8,128)(2,1)S(1)}, u32[]{:S(2)}, u32[]{:S(2)}) collective-permute-start(bf16[10,6144]{1,0:T(8,128)(2,1)} %bitcast.70), channel_id=1, source_target_pairs={{0,128},{128,256},{256,384},{384,0},{1,129},{129,257},{257,385},{3... | collective-permute-start | bytes 368648 | tf_op jit(solution)/shard_map/ppermute | solution.py:14
  41.0 21.6 %all-to-all-start.1 = ((bf16[8,80,768]{2,1,0:T(8,128)(2,1)}), bf16[8,80,768]{2,1,0:T(8,128)(2,1)S(1)}, u32[]{:S(2)}, u32[]{:S(2)}) async-start(bf16[8,80,768]{2,1,0:T(8,128)(2,1)} %broadcast_in_dim.51), calls=%async_computation.1 | async-start | bytes 1966080 | tf_op jit(solution)/shard_map/all_to_all | solution.py:57
  51.5 73.0 %reduce-scatter.2.cloned.1.call-start = ((), (), s32[]{:S(2)}) async-start(), calls=%async_computation.5 | async-start | bytes 4423680 | tf_op jit(solution)/shard_map/reduce_scatter | solution.py:68
  62.7 1.0 copy-start
  76.9 0.7 copy-start.1
  76.9 0.7 copy-start.2
  77.6 3.1 %collective-permute-start.1 = (f32[2,3,128]{2,0,1:T(2,128)S(1)}, f32[2,3,128]{2,0,1:T(2,128)S(1)}, u32[]{:S(2)}, u32[]{:S(2)}) collective-permute-start(f32[2,3,128]{2,0,1:T(2,128)S(1)} %get-tuple-element.10), channel_id=1, source_target_pairs={{0,1},{1,0},{2,3},{3,2},{4,5},{5,4},{6,7},{7,6},{8,9},{9,8},{10,11... | collective-permute-start | bytes 9224 | tf_op jit(solution)/shard_map/ppermute | solution.py:14
  126.4 3.5 %collective-permute-start.2 = (bf16[640,256]{1,0:T(8,128)(2,1)S(1)}, bf16[640,256]{1,0:T(8,128)(2,1)S(1)}, u32[]{:S(2)}, u32[]{:S(2)}) collective-permute-start(bf16[640,256]{1,0:T(8,128)(2,1)S(1)} %pad_maximum_fusion.1), channel_id=1, source_target_pairs={{0,1},{1,0},{2,3},{3,2},{4,5},{5,4},{6,7},{7,6},{8,9},{9,8},{10,11... | collective-permute-start | bytes 983048 | tf_op jit(solution)/shard_map/ppermute | solution.py:14
Sparse Core Ops, SparseCore 0:
  17.6 23.5 all-gather.1
  77.0 47.4 reduce-scatter.1

commit v2 on v1

v2 whole, which is shorter than its diff:
```python
import jax
import jax.numpy as jnp
from jax import lax
from jax.experimental import pallas as pl
from jax.experimental.pallas import tpu as pltpu
from jax.sharding import Mesh
from jax.sharding import PartitionSpec as P

AXES = ("section", "quad", "pair", "zlo", "x", "core")
ROWS = ("quad", "pair")
CHIPS = ("zlo", "x")


def swapped(value, axis):
    return lax.ppermute(value, axis, [(0, 1), (1, 0)])


def head_norm(values, gain):
    scale = jnp.sqrt(jnp.mean(values * values, axis=-1, keepdims=True) + 1e-06)
    return values / scale * gain


def product_kernel(tokens, held, other, out):
    heads, parts, depth, size = held.shape
    for head in range(heads):
        near = jnp.concatenate([held[head, part] for part in range(parts)], axis=1)
        far = jnp.concatenate([other[head, part] for part in range(parts)], axis=1)
        total = jnp.dot(tokens[:, :depth], near, preferred_element_type=jnp.float32)
        total += jnp.dot(tokens[:, depth:], far, preferred_element_type=jnp.float32)
        out[head] = total.astype(out.dtype)
    for head in range(heads, out.shape[0]):
        out[head] = jnp.zeros(out.shape[1:], out.dtype)


def products(tokens, held, other, blocks):
    heads, parts, depth, size = held.shape
    rows = tokens.shape[0]
    whole = pl.BlockSpec(memory_space=pltpu.VMEM)
    return pl.pallas_call(
        product_kernel,
        out_shape=jax.ShapeDtypeStruct((blocks, rows, parts * size), jnp.bfloat16),
        in_specs=[whole] * 3,
        out_specs=whole,
        compiler_params=pltpu.CompilerParams(vmem_limit_bytes=32 * 2**20),
        cost_estimate=pl.CostEstimate(
            flops=4 * rows * depth * heads * parts * size, bytes_accessed=8 * 2**20, transcendentals=0
        ),
    )(tokens, held, other)


def on_device(stale, layer_of_section, mod_table, w_qkv, q_gain, k_gain, counts):
    tok_rows, width = stale.shape[1:]
    quads = lax.axis_size("quad")
    pairs = lax.axis_size("pair")
    cores = lax.axis_size("core")
    chips = lax.axis_size("zlo") * lax.axis_size("x")
    slice_width, heads_dev = w_qkv.shape[1:3]
    head_size = w_qkv.shape[4]
    blks = quads * pairs
    core = lax.axis_index("core")
    pair = lax.axis_index("pair")
    quad = lax.axis_index("quad")
    same = core == pair

    received = lax.ppermute(stale[0], "section", [(i, (i + 1) % 4) for i in range(4)])

    weights = w_qkv[0].transpose(1, 2, 0, 3)
    moved = lax.ppermute(weights, ("pair", "core"), [(1, 2), (2, 1)])
    held = jnp.where(same, weights, moved)
    other = swapped(held, "core")
    gains = jnp.stack([q_gain[0], k_gain[0]])
    gains = jnp.where(same, gains, swapped(gains, "core"))
    owned = jnp.minimum(quad, heads_dev - 1)
    gain = lax.dynamic_index_in_dim(gains, owned, 1, keepdims=False)

    source = received.astype(jnp.float32)
    modul = lax.dynamic_index_in_dim(mod_table, layer_of_section[0], 0, keepdims=False)
    spread = jnp.sqrt(jnp.mean(source * source, axis=-1, keepdims=True) + 1e-06)
    normed = (source / spread * (1.0 + modul[1]) + modul[0]).astype(jnp.bfloat16)
    count_rows = jnp.broadcast_to(counts.astype(jnp.bfloat16)[:, None], (6, width))
    sent = jnp.concatenate([normed, count_rows], axis=0)
    sent = sent.reshape(sent.shape[0], quads, 2, slice_width)
    sent = jnp.where(core == 0, sent, sent[:, :, ::-1])
    sent = sent.reshape(sent.shape[0], quads, 1, 2 * slice_width).transpose(1, 2, 0, 3)
    sent = jnp.broadcast_to(sent, (quads, pairs) + sent.shape[2:])
    sent = sent.reshape((blks,) + sent.shape[2:])
    sliced = lax.all_to_all(sent, ROWS, 0, 0, tiled=False)
    all_counts = sliced[:, tok_rows, 0].astype(jnp.int32)
    mine = sliced[:, :tok_rows].reshape(blks * tok_rows, 2 * slice_width)
    copies = jnp.broadcast_to(mine[None], (chips,) + mine.shape)
    tokens = lax.all_to_all(copies, CHIPS, 0, 0, tiled=False)
    tokens = tokens.reshape(chips * blks * tok_rows, 2 * slice_width)
    rows = tokens.shape[0]

    partial = products(tokens, held, other, quads)
    partial = lax.all_to_all(partial, "quad", 0, 0, tiled=False)
    qkv = jnp.sum(partial.astype(jnp.float32), axis=0)
    query = head_norm(qkv[:, :head_size], gain[0]).astype(jnp.bfloat16)
    key_part = head_norm(qkv[:, head_size : 2 * head_size], gain[1]).astype(jnp.bfloat16)
    value = qkv[:, 2 * head_size :].astype(jnp.bfloat16)
    near = jnp.concatenate([key_part, value], axis=1)
    both = jnp.concatenate([near, swapped(near, "core")], axis=0)
    keys, values = both[:, :head_size], both[:, head_size:]

    lane = jnp.arange(cores)[:, None, None, None]
    lane = jnp.where(lane == 0, core, 1 - core)
    chip = jnp.arange(chips)[None, :, None, None]
    token = jnp.arange(tok_rows)[None, None, None, :]
    position = (chip * cores + lane) * tok_rows + token
    valid = (position < all_counts[None, None, :, None]).reshape(1, cores * rows)
    scores = jnp.dot(query, keys.T, preferred_element_type=jnp.float32) / jnp.sqrt(
        jnp.float32(head_size)
    )
    scores = jnp.where(valid, scores, -1e30)
    top = jnp.max(scores, axis=-1, keepdims=True)
    expo = jnp.exp(scores - top)
    denom = jnp.sum(expo, axis=-1, keepdims=True)
    mixed = jnp.dot(expo.astype(jnp.bfloat16), values, preferred_element_type=jnp.float32)
    mixed = (mixed / denom).astype(jnp.bfloat16)

    mixed = mixed.reshape(chips, blks, tok_rows, head_size).transpose(1, 0, 2, 3)
    mixed = mixed.reshape(blks * chips, tok_rows, head_size)
    returned = lax.all_to_all(mixed, ROWS + CHIPS, 0, 0, tiled=False)
    returned = returned.reshape(quads, pairs, chips, tok_rows, head_size)[:heads_dev]
    return returned.transpose(3, 2, 1, 0, 4).reshape(1, tok_rows, width)


def solution(mesh):
    sizes = mesh.shape
    fine = Mesh(mesh.devices.reshape(sizes["section"], 4, 2, 2, 4, 2), AXES)
    uly = CHIPS + ("core",)
    in_specs = (
        P("section", ROWS + uly, None),
        P("section"),
        P(),
        P("section", ROWS, uly, None, None),
        P("section", uly, None),
        P("section", uly, None),
        P(ROWS),
    )
    out_specs = P("section", ROWS + uly, None)
    return jax.shard_map(
        on_device, mesh=fine, in_specs=in_specs, out_specs=out_specs, check_vma=False
    )
```

time: 162 us -> 161 us (level)
  waiting for transfers between devices: 60 us -> 77.6 us
  starting transfers between devices: 20.4 us -> 37.5 us
  blocking collectives: 38.3 us -> 22.2 us
  between operations: 14.9 us -> 1.57 us
  matrix products: 8.72 us -> 1.47 us
  Pallas kernels: 0 us -> 4.49 us
  local copies, waits for them, and re-layouts: 14 us -> 10.5 us
    all_to_all x0 -> x2, waiting for transfers between devices: none -> 53.8 us  [the longest x1 40.6 us: on_device(): partial = lax.all_to_all(partial, 'quad', 0, 0, tiled=False)]
    reduce_scatter x1 -> x0, waiting for transfers between devices: 43.6 us -> none  [on_device(): qkv = lax.psum_scatter(products, 'blk', scatter_dimension=0, tiled=False)]
    all_to_all x2 -> x1, blocking collectives: 38.3 us -> 22.2 us  [on_device(): returned = lax.all_to_all(mixed, ROWS + CHIPS, 0, 0, tiled=False)]
    all_to_all x0 -> x2, starting transfers between devices: none -> 10.8 us  [the longest x1 7.1 us: on_device(): sliced = lax.all_to_all(sent, ROWS, 0, 0, tiled=False)]
    dot_general x2 -> x0, matrix products: 7.26 us -> none  [on_device(): jnp.dot(tokens, weights[index], preferred_element_type=jnp.float32)]
    ppermute x3 -> x5, starting transfers between devices: 9.92 us -> 17.1 us  [the longest x3 9.2 us: swapped(): return lax.ppermute(value, axis, [(0, 1), (1, 0)])]
    ppermute x3 -> x5, waiting for transfers between devices: 5.26 us -> 12.2 us  [the longest x1 7.85 us: on_device(): lax.ppermute(stale[0], 'section', [(i, (i + 1) % 4) for i in range(4)])]
    pallas_call x0 -> x1, Pallas kernels: none -> 4.49 us  [products(): pl.pallas_call(product_kernel, out_shape=jax.ShapeDtypeStruct((blocks, ro...]
  transfers between devices with their start and end apart: 6 -> 8, of which waited for: 5 -> 7; matrix products, arithmetic and copies ran while one was open for 5% -> 3% of each run, Pallas kernels for 0% -> 0%
where the time goes in v2:
time: 161 us; the launch traced here: 160 us
  waiting for transfers between devices  77.6 us (48%)
  starting transfers between devices  37.5 us (23%)
  blocking collectives  22.2 us (14%)
  local copies, waits for them, and re-layouts  10.5 us (7%)
  other arithmetic  4.85 us (3%)
  Pallas kernels  4.49 us (3%)
    all_to_all x1, waiting for transfers between devices, on_device(): partial = lax.all_to_all(partial, 'quad', 0, 0, tiled=False)  40.6 us
    all_to_all x1, blocking collectives, on_device(): returned = lax.all_to_all(mixed, ROWS + CHIPS, 0, 0, tiled=False)  22.2 us
    all_to_all x1, waiting for transfers between devices, on_device(): sliced = lax.all_to_all(sent, ROWS, 0, 0, tiled=False)  13.2 us
    all_to_all x1, waiting for transfers between devices, on_device(): tokens = lax.all_to_all(copies, CHIPS, 0, 0, tiled=False)  11.5 us
    all_to_all x1, starting transfers between devices, on_device(): tokens = lax.all_to_all(copies, CHIPS, 0, 0, tiled=False)  9.55 us
    ppermute x3, starting transfers between devices, swapped(): return lax.ppermute(value, axis, [(0, 1), (1, 0)])  9.2 us
    ppermute x1, waiting for transfers between devices, on_device(): lax.ppermute(stale[0], 'section', [(i, (i + 1) % 4) for i in range(4)])  7.85 us
    all_to_all x1, starting transfers between devices, on_device(): sliced = lax.all_to_all(sent, ROWS, 0, 0, tiled=False)  7.1 us
  transfers between devices with their start and end apart: 8, of which 7 were waited for; matrix products, arithmetic and copies ran while one was open for 3% of the time, Pallas kernels for 0%

profile of v2, /device:TPU:6, one launch (start us, length us, event | category | flops | bytes accessed | tf_op | source)
XLA Modules:
  0.0 160.1 jit_solution(6872601818849400272)
XLA Ops:
  0.0 6.1 %collective-permute-start = (bf16[10,6144]{1,0:T(8,128)(2,1)}, bf16[10,6144]{1,0:T(8,128)(2,1)S(1)}, u32[]{:S(2)}, u32[]{:S(2)}) collective-permute-start(bf16[10,6144]{1,0:T(8,128)(2,1)} %bitcast.48), channel_id=1, source_target_pairs={{0,128},{128,256},{256,384},{384,0},{1,129},{129,257},{257,385},{3... | collective-permute-start | bytes 368648 | tf_op jit(solution)/shard_map/ppermute | solution.py:65
  6.7 0.9 dynamic-slice_add_fusion
  8.3 7.8 %collective-permute-done = bf16[10,6144]{1,0:T(8,128)(2,1)S(1)} collective-permute-done((bf16[10,6144]{1,0:T(8,128)(2,1)}, bf16[10,6144]{1,0:T(8,128)(2,1)S(1)}, u32[]{:S(2)}, u32[]{:S(2)}) %collective-permute-start) | collective-permute-done | bytes 122912 | tf_op jit(solution)/shard_map/ppermute | solution.py:65
  16.2 0.2 fusion.12
  16.4 0.1 fusion.15
  16.5 0.1 reshape.141
  16.7 1.1 rev.3
  17.8 0.1 reshape.149
  18.0 0.8 broadcast_in_dim.54
  18.7 7.1 %all-to-all-start = ((bf16[8,16,1536]{2,1,0:T(8,128)(2,1)}), bf16[8,16,1536]{2,1,0:T(8,128)(2,1)S(1)}, u32[]{:S(2)}, u32[]{:S(2)}) async-start(bf16[8,16,1536]{2,1,0:T(8,128)(2,1)} %bitcast.7), calls=%async_computation | async-start | bytes 786432 | tf_op jit(solution)/shard_map/all_to_all | solution.py:87
  25.8 1.9 %collective-permute-start.1 = (bf16[3,3,768,128]{3,2,1,0:T(8,128)(2,1)}, bf16[3,3,768,128]{3,2,1,0:T(8,128)(2,1)}, u32[]{:S(2)}, u32[]{:S(2)}) collective-permute-start(bf16[3,3,768,128]{3,2,1,0:T(8,128)(2,1)} %bitcast.10), channel_id=1, source_target_pairs={{1,16},{16,1},{3,18},{18,3},{5,20},{20,5},{7,22},{22,7},{9,24},{24... | collective-permute-start | bytes 5308424 | tf_op jit(solution)/shard_map/ppermute | solution.py:68
  27.7 13.2 %all-to-all-done = bf16[8,16,1536]{2,1,0:T(8,128)(2,1)S(1)} async-done(((bf16[8,16,1536]{2,1,0:T(8,128)(2,1)}), bf16[8,16,1536]{2,1,0:T(8,128)(2,1)S(1)}, u32[]{:S(2)}, u32[]{:S(2)}) %all-to-all-start) | async-done | bytes 393248 | tf_op jit(solution)/shard_map/all_to_all | solution.py:87
  40.9 0.1 broadcast_in_dim.56
  41.0 1.4 broadcast_in_dim.57
  42.5 9.6 %all-to-all-start.1 = ((bf16[8,80,1536]{2,1,0:T(8,128)(2,1)}), bf16[8,80,1536]{2,1,0:T(8,128)(2,1)S(1)}, u32[]{:S(2)}, u32[]{:S(2)}) async-start(bf16[8,80,1536]{2,1,0:T(8,128)(2,1)} %broadcast_in_dim.57), calls=%async_computation.1 | async-start | bytes 3932160 | tf_op jit(solution)/shard_map/all_to_all | solution.py:91
  52.0 0.0 collective-permute-done.1
  52.0 1.7 %broadcast_select_fusion.held = bf16[3,3,768,128]{3,2,1,0:T(8,128)(2,1)S(1)} fusion(bf16[3,3,768,128]{3,2,1,0:T(8,128)(2,1)} %collective-permute-done.1, pred[]{:T(512)S(6)} %eq.16, bf16[1,768,3,3,128]{4,1,3,2,0:T(8,128)(2,1)} %param.10), kind=kLoop, calls=%fused_computation.6 | loop fusion | flops 884736 | bytes 5308417 | tf_op jit(solution)/shard_map/jit(_where)/select_n | solution.py:69
  53.7 5.4 %collective-permute-start.2 = (bf16[3,3,768,128]{3,2,1,0:T(8,128)(2,1)S(1)}, bf16[3,3,768,128]{3,2,1,0:T(8,128)(2,1)S(1)}, u32[]{:S(2)}, u32[]{:S(2)}) collective-permute-start(bf16[3,3,768,128]{3,2,1,0:T(8,128)(2,1)S(1)} %broadcast_select_fusion.held), channel_id=1, source_target_pairs={{0,1},{1,0},{2,3},{3,2},{4,5},{5,4},{6,7},{7,6},{8,9},{9,8},{10,11... | collective-permute-start | bytes 5308424 | tf_op jit(solution)/shard_map/ppermute | solution.py:15
  59.1 0.0 copy-start
  59.1 1.2 copy-done
  60.3 2.1 %collective-permute-done.2.other = bf16[3,3,768,128]{3,2,1,0:T(8,128)(2,1)S(1)} collective-permute-done((bf16[3,3,768,128]{3,2,1,0:T(8,128)(2,1)S(1)}, bf16[3,3,768,128]{3,2,1,0:T(8,128)(2,1)S(1)}, u32[]{:S(2)}, u32[]{:S(2)}) %collective-permute-start.2) | collective-permute-done | bytes 1769504 | tf_op jit(solution)/shard_map/ppermute | solution.py:15
  62.4 0.0 copy-start.2
  62.4 1.2 copy-done.2
  63.6 11.5 %all-to-all-done.1 = bf16[8,80,1536]{2,1,0:T(8,128)(2,1)S(1)} async-done(((bf16[8,80,1536]{2,1,0:T(8,128)(2,1)}), bf16[8,80,1536]{2,1,0:T(8,128)(2,1)S(1)}, u32[]{:S(2)}, u32[]{:S(2)}) %all-to-all-start.1) | async-done | bytes 1966112 | tf_op jit(solution)/shard_map/all_to_all | solution.py:91
  75.1 0.0 copy-start.1
  75.1 1.5 copy-done.1
  76.6 0.0 copy-start.3
  76.6 1.5 copy-done.3
  78.0 4.5 %shard_map.73 = bf16[4,640,384]{2,1,0:T(8,128)(2,1)} custom-call(bf16[640,1536]{1,0:T(8,128)(2,1)S(1)} %bitcast.37, bf16[3,3,768,128]{3,2,1,0:T(8,128)(2,1)S(1)} %copy-done.1, bf16[3,3,768,128]{3,2,1,0:T(8,128)(2,1)S(1)} %copy-done.3), custom_call_target="tpu_custom_call" | custom-call | flops 2264924160 | bytes 8388608 | tf_op jit(solution)/shard_map/pallas_call | solution.py:39
  82.5 0.0 copy-start.4
  82.5 0.0 copy-start.5
  82.5 3.7 %all-to-all-start.2 = ((bf16[4,640,384]{2,1,0:T(8,128)(2,1)}), bf16[4,640,384]{2,1,0:T(8,128)(2,1)S(1)}, u32[]{:S(2)}, u32[]{:S(2)}) async-start(bf16[4,640,384]{2,1,0:T(8,128)(2,1)} %shard_map.73), calls=%async_computation.2 | async-start | bytes 3932160 | tf_op jit(solution)/shard_map/all_to_all | solution.py:96
  86.3 0.0 copy-done.4
  86.3 0.0 copy-done.5
  86.3 1.9 %collective-permute-start.3 = (f32[2,3,128]{2,0,1:T(2,128)S(1)}, f32[2,3,128]{2,0,1:T(2,128)S(1)}, u32[]{:S(2)}, u32[]{:S(2)}) collective-permute-start(f32[2,3,128]{2,0,1:T(2,128)S(1)} %pad_maximum_fusion.2), channel_id=1, source_target_pairs={{0,1},{1,0},{2,3},{3,2},{4,5},{5,4},{6,7},{7,6},{8,9},{9,8},{10,11... | collective-permute-start | bytes 9224 | tf_op jit(solution)/shard_map/ppermute | solution.py:15
  88.3 0.1 add_multiply_fusion
  88.3 0.1 iota_add_fusion
  88.4 1.0 collective-permute-done.3
  89.4 0.2 fusion.20
  89.6 40.6 %all-to-all-done.2 = bf16[4,640,384]{2,1,0:T(8,128)(2,1)S(1)} async-done(((bf16[4,640,384]{2,1,0:T(8,128)(2,1)}), bf16[4,640,384]{2,1,0:T(8,128)(2,1)S(1)}, u32[]{:S(2)}, u32[]{:S(2)}) %all-to-all-start.2) | async-done | bytes 1966112 | tf_op jit(solution)/shard_map/all_to_all | solution.py:96
  130.2 0.3 convert_reduce_fusion
  130.5 0.2 multiply_reduce_fusion.1
  130.8 0.2 multiply_convert_fusion
  131.0 1.9 %collective-permute-start.4 = (bf16[640,256]{1,0:T(8,128)(2,1)S(1)}, bf16[640,256]{1,0:T(8,128)(2,1)S(1)}, u32[]{:S(2)}, u32[]{:S(2)}) collective-permute-start(bf16[640,256]{1,0:T(8,128)(2,1)S(1)} %pad_maximum_fusion.1), channel_id=1, source_target_pairs={{0,1},{1,0},{2,3},{3,2},{4,5},{5,4},{6,7},{7,6},{8,9},{9,8},{10,11... | collective-permute-start | bytes 983048 | tf_op jit(solution)/shard_map/ppermute | solution.py:15
  132.9 0.1 broadcast_compare_fusion
  133.0 0.1 lt.32
  133.2 1.3 collective-permute-done.4
  134.5 0.1 pad_maximum_fusion
  134.6 0.8 fusion.23
  135.4 0.6 fusion.1
  136.0 0.7 fusion.9
  136.7 0.1 reshape.145
  136.8 0.1 copy.31
  136.9 0.1 copy.22
  137.0 22.2 %all_to_all.20 = bf16[64,10,128]{2,1,0:T(8,128)(2,1)S(1)} all-to-all(bf16[64,10,128]{2,1,0:T(8,128)(2,1)S(1)} %copy.22), channel_id=1, replica_groups=mesh['section'=4,'quad'=4,'pair'=2,'zlo'=2,'x'=4,'core'=2] {'quad','pair..., dimensions={0} | all-to-all | bytes 327680 | tf_op jit(solution)/shard_map/all_to_all | solution.py:123
  159.2 0.1 copy.24
  159.3 0.8 reshape.147
  (14 shorter events, 0.2 us)
Async XLA Ops:
  0.0 16.2 %collective-permute-start = (bf16[10,6144]{1,0:T(8,128)(2,1)}, bf16[10,6144]{1,0:T(8,128)(2,1)S(1)}, u32[]{:S(2)}, u32[]{:S(2)}) collective-permute-start(bf16[10,6144]{1,0:T(8,128)(2,1)} %bitcast.48), channel_id=1, source_target_pairs={{0,128},{128,256},{256,384},{384,0},{1,129},{129,257},{257,385},{3... | collective-permute-start | bytes 368648 | tf_op jit(solution)/shard_map/ppermute | solution.py:65
  18.7 22.2 %all-to-all-start = ((bf16[8,16,1536]{2,1,0:T(8,128)(2,1)}), bf16[8,16,1536]{2,1,0:T(8,128)(2,1)S(1)}, u32[]{:S(2)}, u32[]{:S(2)}) async-start(bf16[8,16,1536]{2,1,0:T(8,128)(2,1)} %bitcast.7), calls=%async_computation | async-start | bytes 786432 | tf_op jit(solution)/shard_map/all_to_all | solution.py:87
  25.8 26.2 %collective-permute-start.1 = (bf16[3,3,768,128]{3,2,1,0:T(8,128)(2,1)}, bf16[3,3,768,128]{3,2,1,0:T(8,128)(2,1)}, u32[]{:S(2)}, u32[]{:S(2)}) collective-permute-start(bf16[3,3,768,128]{3,2,1,0:T(8,128)(2,1)} %bitcast.10), channel_id=1, source_target_pairs={{1,16},{16,1},{3,18},{18,3},{5,20},{20,5},{7,22},{22,7},{9,24},{24... | collective-permute-start | bytes 5308424 | tf_op jit(solution)/shard_map/ppermute | solution.py:68
  42.5 32.6 %all-to-all-start.1 = ((bf16[8,80,1536]{2,1,0:T(8,128)(2,1)}), bf16[8,80,1536]{2,1,0:T(8,128)(2,1)S(1)}, u32[]{:S(2)}, u32[]{:S(2)}) async-start(bf16[8,80,1536]{2,1,0:T(8,128)(2,1)} %broadcast_in_dim.57), calls=%async_computation.1 | async-start | bytes 3932160 | tf_op jit(solution)/shard_map/all_to_all | solution.py:91
  53.7 8.7 %collective-permute-start.2 = (bf16[3,3,768,128]{3,2,1,0:T(8,128)(2,1)S(1)}, bf16[3,3,768,128]{3,2,1,0:T(8,128)(2,1)S(1)}, u32[]{:S(2)}, u32[]{:S(2)}) collective-permute-start(bf16[3,3,768,128]{3,2,1,0:T(8,128)(2,1)S(1)} %broadcast_select_fusion.held), channel_id=1, source_target_pairs={{0,1},{1,0},{2,3},{3,2},{4,5},{5,4},{6,7},{7,6},{8,9},{9,8},{10,11... | collective-permute-start | bytes 5308424 | tf_op jit(solution)/shard_map/ppermute | solution.py:15
  59.1 1.2 copy-start
  62.4 1.2 copy-start.2
  75.1 1.5 copy-start.1
  76.6 1.5 copy-start.3
  82.5 3.7 %copy-start.4 = (f32[1,3,128]{2,0,1:T(1,128)S(1)}, f32[1,3,128]{2,0,1:T(1,128)}, u32[]{:S(2)}) copy-start(f32[1,3,128]{2,0,1:T(1,128)} %param.12) | copy-start | bytes 4612
  82.5 3.7 %copy-start.5 = (f32[1,3,128]{2,0,1:T(1,128)S(1)}, f32[1,3,128]{2,0,1:T(1,128)}, u32[]{:S(2)}) copy-start(f32[1,3,128]{2,0,1:T(1,128)} %param.11) | copy-start | bytes 4612
  82.5 47.7 %all-to-all-start.2 = ((bf16[4,640,384]{2,1,0:T(8,128)(2,1)}), bf16[4,640,384]{2,1,0:T(8,128)(2,1)S(1)}, u32[]{:S(2)}, u32[]{:S(2)}) async-start(bf16[4,640,384]{2,1,0:T(8,128)(2,1)} %shard_map.73), calls=%async_computation.2 | async-start | bytes 3932160 | tf_op jit(solution)/shard_map/all_to_all | solution.py:96
  86.3 3.1 %collective-permute-start.3 = (f32[2,3,128]{2,0,1:T(2,128)S(1)}, f32[2,3,128]{2,0,1:T(2,128)S(1)}, u32[]{:S(2)}, u32[]{:S(2)}) collective-permute-start(f32[2,3,128]{2,0,1:T(2,128)S(1)} %pad_maximum_fusion.2), channel_id=1, source_target_pairs={{0,1},{1,0},{2,3},{3,2},{4,5},{5,4},{6,7},{7,6},{8,9},{9,8},{10,11... | collective-permute-start | bytes 9224 | tf_op jit(solution)/shard_map/ppermute | solution.py:15
  131.0 3.5 %collective-permute-start.4 = (bf16[640,256]{1,0:T(8,128)(2,1)S(1)}, bf16[640,256]{1,0:T(8,128)(2,1)S(1)}, u32[]{:S(2)}, u32[]{:S(2)}) collective-permute-start(bf16[640,256]{1,0:T(8,128)(2,1)S(1)} %pad_maximum_fusion.1), channel_id=1, source_target_pairs={{0,1},{1,0},{2,3},{3,2},{4,5},{5,4},{6,7},{7,6},{8,9},{9,8},{10,11... | collective-permute-start | bytes 983048 | tf_op jit(solution)/shard_map/ppermute | solution.py:15

commit v3 on v1

v3 whole, which is shorter than its diff:
```python
import jax
import jax.numpy as jnp
from jax import lax
from jax.experimental import pallas as pl
from jax.experimental.pallas import tpu as pltpu
from jax.sharding import Mesh
from jax.sharding import PartitionSpec as P

AXES = ("section", "blk", "zlo", "x", "core")
CHIPS = ("zlo", "x")
SMALL = pl.BlockSpec(memory_space=pltpu.SMEM)
WHOLE = pl.BlockSpec(memory_space=pltpu.VMEM)
DISTANT = pl.BlockSpec(memory_space=pltpu.HBM)
LIMIT = pltpu.CompilerParams(vmem_limit_bytes=12 * 2**20)


def shifted(value, axis, steps):
    count = lax.axis_size(axis)
    pairs = [(source, (source + steps) % count) for source in range(count)]
    return lax.ppermute(value, axis, pairs)


def head_norm(values, gain):
    scale = jnp.sqrt(jnp.mean(values * values, axis=-1, keepdims=True) + 1e-06)
    return values / scale * gain


def pack_kernel(counts, stale, modul, out):
    rows, width = stale.shape
    blks, padded, slice_width = out.shape
    source = stale[...].astype(jnp.float32)
    spread = jnp.sqrt(jnp.mean(source * source, axis=-1, keepdims=True) + 1e-06)
    normed = source / spread * (1.0 + modul[1:2]) + modul[0:1]
    count = jnp.full((padded - rows, width), counts[0], jnp.int32).astype(jnp.float32)
    normed = jnp.concatenate([normed, count], axis=0).astype(out.dtype)
    for blk in range(blks):
        out[blk] = normed[:, blk * slice_width : (blk + 1) * slice_width]


def packed(counts, stale, modul, shape):
    return pl.pallas_call(
        pack_kernel,
        out_shape=jax.ShapeDtypeStruct(shape, jnp.bfloat16),
        in_specs=[SMALL, WHOLE, WHOLE],
        out_specs=WHOLE,
        compiler_params=LIMIT,
        cost_estimate=pl.CostEstimate(flops=10**6, bytes_accessed=10**6, transcendentals=0),
    )(counts, stale, modul)


def product_kernel(steps, place, tokens, own, other, *refs):
    outs, block, sems = refs[: len(steps)], refs[-2], refs[-1]
    row, core = place[0], place[1]
    heads, parts = own.shape[:2]

    def fetch(number):
        owner = lax.rem(row + steps[number], lax.axis_size("blk"))
        head = jnp.minimum(owner, 2 * heads - 1)
        lane = jnp.where(head >= heads, 1, 0)
        slot = number % 2

        @pl.when(lane == core)
        def _():
            pltpu.make_async_copy(own.at[head - lane * heads], block.at[slot], sems.at[slot]).start()

        @pl.when(lane != core)
        def _():
            pltpu.make_async_copy(other.at[head - lane * heads], block.at[slot], sems.at[slot]).start()

    fetch(0)
    for number, out in enumerate(outs):
        slot = number % 2
        if number + 1 < len(outs):
            fetch(number + 1)
        pltpu.make_async_copy(own.at[0], block.at[slot], sems.at[slot]).wait()
        weights = jnp.concatenate([block[slot, part] for part in range(parts)], axis=1)
        total = jnp.dot(tokens[...], weights, preferred_element_type=jnp.float32)
        out[...] = total.astype(out.dtype)


def products(steps, place, tokens, own, other):
    rows, depth = tokens.shape
    parts, size = own.shape[1], own.shape[3]
    shape = jax.ShapeDtypeStruct((rows, parts * size), jnp.bfloat16)
    return pl.pallas_call(
        lambda *refs: product_kernel(steps, *refs),
        out_shape=[shape] * len(steps),
        in_specs=[SMALL, WHOLE, DISTANT, DISTANT],
        out_specs=[WHOLE] * len(steps),
        scratch_shapes=[
            pltpu.VMEM((2,) + own.shape[1:], jnp.bfloat16),
            pltpu.SemaphoreType.DMA((2,)),
        ],
        compiler_params=LIMIT,
        cost_estimate=pl.CostEstimate(
            flops=2 * rows * depth * parts * size * len(steps), bytes_accessed=4 * 2**20, transcendentals=0
        ),
    )(place, tokens, own, other)


def add_kernel(begin, first, second, out):
    rows = second.shape[0]
    total = first[begin : begin + rows].astype(jnp.float32) + second[...].astype(jnp.float32)
    out[begin : begin + rows] = total.astype(out.dtype)
    for low, high in ((0, begin), (begin + rows, out.shape[0])):
        if high > low:
            out[low:high] = first[low:high]


def added(first, second, begin=0):
    return pl.pallas_call(
        lambda *refs: add_kernel(begin, *refs),
        out_shape=jax.ShapeDtypeStruct(first.shape, first.dtype),
        in_specs=[WHOLE, WHOLE],
        out_specs=WHOLE,
        compiler_params=LIMIT,
        cost_estimate=pl.CostEstimate(flops=first.size, bytes_accessed=3 * 2**19, transcendentals=0),
    )(first, second)


def head_kernel(first, second, third, gain, query, pair):
    size = query.shape[1]
    total = first[...].astype(jnp.float32) + second[...].astype(jnp.float32)
    total = total + third[...].astype(jnp.float32)
    query[...] = head_norm(total[:, :size], gain[0:1]).astype(query.dtype)
    pair[:, :size] = head_norm(total[:, size : 2 * size], gain[1:2]).astype(pair.dtype)
    pair[:, size:] = total[:, 2 * size :].astype(pair.dtype)


def headed(first, second, third, gain):
    rows, size = first.shape[0], gain.shape[1]
    return pl.pallas_call(
        head_kernel,
        out_shape=[
            jax.ShapeDtypeStruct((rows, size), jnp.bfloat16),
            jax.ShapeDtypeStruct((rows, 2 * size), jnp.bfloat16),
        ],
        in_specs=[WHOLE] * 4,
        out_specs=[WHOLE] * 2,
        compiler_params=LIMIT,
        cost_estimate=pl.CostEstimate(flops=10 * first.size, bytes_accessed=4 * 2**19, transcendentals=0),
    )(first, second, third, gain)


def merge_kernel(blocks, out):
    blks, chips = blocks.shape[:2]
    size = blocks.shape[3]
    heads = out.shape[2] // (chips * size)
    for chip in range(chips):
        for blk in range(heads):
            begin = (chip * heads + blk) * size
            out[0, :, begin : begin + size] = blocks[blk, chip]


def merged(blocks, shape):
    return pl.pallas_call(
        merge_kernel,
        out_shape=jax.ShapeDtypeStruct(shape, blocks.dtype),
        in_specs=[WHOLE],
        out_specs=WHOLE,
        compiler_params=LIMIT,
        cost_estimate=pl.CostEstimate(flops=0, bytes_accessed=2**19, transcendentals=0),
    )(blocks)


def on_device(stale, layer_of_section, mod_table, w_qkv, q_gain, k_gain, counts):
    tok_rows, width = stale.shape[1:]
    blks = lax.axis_size("blk")
    cores = lax.axis_size("core")
    chips = lax.axis_size("zlo") * lax.axis_size("x")
    slice_width, heads_dev = w_qkv.shape[1:3]
    head_size = w_qkv.shape[4]
    heads_chip = cores * heads_dev
    core = lax.axis_index("core")
    row = lax.axis_index("blk")

    received = shifted(stale[0], "section", 1)
    modul = lax.dynamic_index_in_dim(mod_table, layer_of_section[0], 0, keepdims=False)
    own = w_qkv[0].transpose(1, 2, 0, 3)
    gains = jnp.concatenate([q_gain, k_gain], axis=0)
    other = shifted(own, "core", 1)
    theirs = shifted(gains, "core", 1)
    owned = jnp.minimum(row, heads_chip - 1)
    lane = owned // heads_dev
    gain = jnp.where(lane == core, gains, theirs)
    gain = lax.dynamic_index_in_dim(gain, owned - lane * heads_dev, 1, keepdims=False)

    sent = packed(counts, received, modul, (blks, 16, slice_width))
    sliced = lax.all_to_all(sent, "blk", 0, 0, tiled=False)
    all_counts = sliced[:, tok_rows, 0].astype(jnp.int32)
    mine = sliced[:, :tok_rows].reshape(blks * tok_rows, slice_width)
    copies = jnp.broadcast_to(mine[None], (chips,) + mine.shape)
    tokens = lax.all_to_all(copies, CHIPS, 0, 0, tiled=False)
    tokens = tokens.reshape(chips * blks * tok_rows, slice_width)
    rows = tokens.shape[0]
    half = rows // 2

    place = jnp.stack([row, core]).astype(jnp.int32)
    (far,) = products((4,), place, tokens, own, other)
    up, down = shifted(far[:half], "blk", 1), shifted(far[half:], "blk", -1)
    three, five = products((3, 5), place, tokens, own, other)
    up, down = shifted(added(three, up), "blk", 1), shifted(added(five, down, half), "blk", -1)
    two, six = products((2, 6), place, tokens, own, other)
    up, down = shifted(added(two, up), "blk", 1), shifted(added(six, down), "blk", -1)
    one, seven, zero = products((1, 7, 0), place, tokens, own, other)
    up, down = shifted(added(one, up), "blk", 1), shifted(added(seven, down), "blk", -1)
    query, near = headed(zero, up, down, gain)
    both = jnp.concatenate([near, shifted(near, "core", 1)], axis=0)
    keys, values = both[:, :head_size], both[:, head_size:]

    lane = jnp.arange(cores)[:, None, None, None]
    lane = jnp.where(lane == 0, core, 1 - core)
    chip = jnp.arange(chips)[None, :, None, None]
    token = jnp.arange(tok_rows)[None, None, None, :]
    position = (chip * cores + lane) * tok_rows + token
    valid = (position < all_counts[None, None, :, None]).reshape(1, cores * rows)
    scores = jnp.dot(query, keys.T, preferred_element_type=jnp.float32) / jnp.sqrt(
        jnp.float32(head_size)
    )
    scores = jnp.where(valid, scores, -1e30)
    top = jnp.max(scores, axis=-1, keepdims=True)
    expo = jnp.exp(scores - top)
    denom = jnp.sum(expo, axis=-1, keepdims=True)
    mixed = jnp.dot(expo.astype(jnp.bfloat16), values, preferred_element_type=jnp.float32)
    mixed = (mixed / denom).astype(jnp.bfloat16)

    mixed = mixed.reshape(chips, blks, tok_rows, head_size).transpose(1, 0, 2, 3)
    mixed = mixed.reshape(blks * chips, tok_rows, head_size)
    returned = lax.all_to_all(mixed, ("blk",) + CHIPS, 0, 0, tiled=False)
    return merged(returned.reshape(blks, chips, tok_rows, head_size), (1, tok_rows, width))


def solution(mesh):
    sizes = mesh.shape
    fine = Mesh(mesh.devices.reshape(sizes["section"], sizes["blk"], 2, 4, 2), AXES)
    uly = CHIPS + ("core",)
    in_specs = (
        P("section", ("blk",) + uly, None),
        P("section"),
        P(),
        P("section", "blk", uly, None, None),
        P("section", uly, None),
        P("section", uly, None),
        P("blk"),
    )
    out_specs = P("section", ("blk",) + uly, None)
    return jax.shard_map(
        on_device, mesh=fine, in_specs=in_specs, out_specs=out_specs, check_vma=False
    )
```

time: 162 us -> 149 us (0.920)
  starting transfers between devices: 20.4 us -> 55.7 us
  Pallas kernels: 0 us -> 17.3 us
  blocking collectives: 38.3 us -> 21.2 us
  waiting for transfers between devices: 60 us -> 45.6 us
  between operations: 14.9 us -> 1.63 us
  local copies, waits for them, and re-layouts: 14 us -> 2.43 us
  matrix products: 8.72 us -> 1.39 us
  other arithmetic: 5.34 us -> 2.59 us
    reduce_scatter x1 -> x0, waiting for transfers between devices: 43.6 us -> none  [on_device(): qkv = lax.psum_scatter(products, 'blk', scatter_dimension=0, tiled=False)]
    ppermute x3 -> x12, starting transfers between devices: 9.92 us -> 38.1 us  [shifted(): return lax.ppermute(value, axis, pairs)]
    ppermute x3 -> x12, waiting for transfers between devices: 5.26 us -> 26.5 us  [shifted(): return lax.ppermute(value, axis, pairs)]
    pallas_call x0 -> x13, Pallas kernels: none -> 17.3 us  [the longest x4 10.9 us: products(): pl.pallas_call(lambda *refs: product_kernel(steps, *refs), out_shape=[sha...]
    all_to_all x1 -> x0, blocking collectives: 16.8 us -> none  [on_device(): sliced = lax.all_to_all(sent, 'blk', 0, 0, tiled=False)]
    all_to_all x0 -> x1, waiting for transfers between devices: none -> 8 us  [on_device(): sliced = lax.all_to_all(sent, 'blk', 0, 0, tiled=False)]
    dot_general x2 -> x0, matrix products: 7.26 us -> none  [on_device(): jnp.dot(tokens, weights[index], preferred_element_type=jnp.float32)]
    all_to_all x0 -> x1, starting transfers between devices: none -> 7.1 us  [on_device(): sliced = lax.all_to_all(sent, 'blk', 0, 0, tiled=False)]
  transfers between devices with their start and end apart: 6 -> 14, of which waited for: 5 -> 7; matrix products, arithmetic and copies ran while one was open for 5% -> 2% of each run, Pallas kernels for 0% -> 9%
where the time goes in v3:
time: 149 us; the launch traced here: 148 us
  starting transfers between devices  55.7 us (37%)
  waiting for transfers between devices  45.6 us (31%)
  blocking collectives  21.2 us (14%)
  Pallas kernels  17.3 us (12%)
  other arithmetic  2.59 us (2%)
  local copies, waits for them, and re-layouts  2.43 us (2%)
  between operations  1.63 us (1%)
    ppermute x12, starting transfers between devices, shifted(): return lax.ppermute(value, axis, pairs)  38.1 us
    ppermute x12, waiting for transfers between devices, shifted(): return lax.ppermute(value, axis, pairs)  26.5 us
    all_to_all x1, blocking collectives, on_device(): returned = lax.all_to_all(mixed, ('blk',) + CHIPS, 0, 0, tiled=False)  21.2 us
    all_to_all x1, waiting for transfers between devices, on_device(): tokens = lax.all_to_all(copies, CHIPS, 0, 0, tiled=False)  11.1 us
    pallas_call x4, Pallas kernels, products(): pl.pallas_call(lambda *refs: product_kernel(steps, *refs), out_shape=[sha...  10.9 us
    all_to_all x1, starting transfers between devices, on_device(): tokens = lax.all_to_all(copies, CHIPS, 0, 0, tiled=False)  10.5 us
    all_to_all x1, waiting for transfers between devices, on_device(): sliced = lax.all_to_all(sent, 'blk', 0, 0, tiled=False)  8 us
    all_to_all x1, starting transfers between devices, on_device(): sliced = lax.all_to_all(sent, 'blk', 0, 0, tiled=False)  7.1 us
  transfers between devices with their start and end apart: 14, of which 7 were waited for; matrix products, arithmetic and copies ran while one was open for 2% of the time, Pallas kernels for 9%

profile of v3, /device:TPU:6, one launch (start us, length us, event | category | flops | bytes accessed | tf_op | source)
XLA Modules:
  0.0 147.8 jit_solution(7929517837923450738)
XLA Ops:
  0.0 0.0 copy-start
  0.0 6.2 %collective-permute-start = (bf16[10,6144]{1,0:T(8,128)(2,1)}, bf16[10,6144]{1,0:T(8,128)(2,1)S(1)}, u32[]{:S(2)}, u32[]{:S(2)}) collective-permute-start(bf16[10,6144]{1,0:T(8,128)(2,1)} %bitcast.37), channel_id=1, source_target_pairs={{0,128},{128,256},{256,384},{384,0},{1,129},{129,257},{257,385},{3... | collective-permute-start | bytes 368648 | tf_op jit(solution)/shard_map/ppermute | solution.py:20
  7.5 8.8 %collective-permute-done.stale = bf16[10,6144]{1,0:T(8,128)(2,1)S(1)} collective-permute-done((bf16[10,6144]{1,0:T(8,128)(2,1)}, bf16[10,6144]{1,0:T(8,128)(2,1)S(1)}, u32[]{:S(2)}, u32[]{:S(2)}) %collective-permute-start) | collective-permute-done | bytes 122912 | tf_op jit(solution)/shard_map/ppermute | solution.py:20
  16.3 0.9 shard_map.73
  17.2 7.1 %all-to-all-start = ((bf16[8,16,768]{2,1,0:T(8,128)(2,1)}), bf16[8,16,768]{2,1,0:T(8,128)(2,1)S(1)}, u32[]{:S(2)}, u32[]{:S(2)}) async-start(bf16[8,16,768]{2,1,0:T(8,128)(2,1)} %shard_map.73), calls=%async_computation | async-start | bytes 393216 | tf_op jit(solution)/shard_map/all_to_all | solution.py:189
  24.3 1.9 %collective-permute-start.1 = (bf16[3,3,768,128]{3,2,1,0:T(8,128)(2,1)}, bf16[3,3,768,128]{3,2,1,0:T(8,128)(2,1)}, u32[]{:S(2)}, u32[]{:S(2)}) collective-permute-start(bf16[3,3,768,128]{3,2,1,0:T(8,128)(2,1)} %bitcast.24), channel_id=1, source_target_pairs={{0,1},{1,0},{2,3},{3,2},{4,5},{5,4},{6,7},{7,6},{8,9},{9,8},{10,11... | collective-permute-start | bytes 5308424 | tf_op jit(solution)/shard_map/ppermute | solution.py:20
  26.2 8.0 %all-to-all-done = bf16[8,16,768]{2,1,0:T(8,128)(2,1)S(1)} async-done(((bf16[8,16,768]{2,1,0:T(8,128)(2,1)}), bf16[8,16,768]{2,1,0:T(8,128)(2,1)S(1)}, u32[]{:S(2)}, u32[]{:S(2)}) %all-to-all-start) | async-done | bytes 196640 | tf_op jit(solution)/shard_map/all_to_all | solution.py:189
  34.3 1.0 broadcast_in_dim.37
  35.3 10.5 %all-to-all-start.1 = ((bf16[8,80,768]{2,1,0:T(8,128)(2,1)}), bf16[8,80,768]{2,1,0:T(8,128)(2,1)S(1)}, u32[]{:S(2)}, u32[]{:S(2)}) async-start(bf16[8,80,768]{2,1,0:T(8,128)(2,1)} %broadcast_in_dim.37), calls=%async_computation.1 | async-start | bytes 1966080 | tf_op jit(solution)/shard_map/all_to_all | solution.py:193
  45.8 0.1 pad_add_fusion.refs_0_
  45.9 0.0 collective-permute-done.1.refs_3_
  45.9 11.1 %all-to-all-done.1 = bf16[8,80,768]{2,1,0:T(8,128)(2,1)S(1)} async-done(((bf16[8,80,768]{2,1,0:T(8,128)(2,1)}), bf16[8,80,768]{2,1,0:T(8,128)(2,1)S(1)}, u32[]{:S(2)}, u32[]{:S(2)}) %all-to-all-start.1) | async-done | bytes 983072 | tf_op jit(solution)/shard_map/all_to_all | solution.py:193
  57.0 2.3 %shard_map.77 = bf16[640,384]{1,0:T(8,128)(2,1)S(1)} custom-call(s32[2]{0:T(128)S(1)} %pad_add_fusion.refs_0_, bf16[640,768]{1,0:T(8,128)(2,1)S(1)} %bitcast.29, bf16[3,3,768,128]{3,2,1,0:T(8,128)(2,1)S(1)} %bitcast.25, bf16[3,3,768,128]{3,2,1,0:T(8,128)(2,1)} %collective-permute-done.1.refs_3_), custom_call_target="tpu_custom_call" | custom-call | flops 377487360 | bytes 4194304 | tf_op jit(solution)/shard_map/pallas_call | solution.py:85
  59.3 0.1 fusion.18
  59.4 1.9 %collective-permute-start.6 = (bf16[320,384]{1,0:T(8,128)(2,1)S(1)}, bf16[320,384]{1,0:T(8,128)(2,1)S(1)}, u32[]{:S(2)}, u32[]{:S(2)}) collective-permute-start(bf16[320,384]{1,0:T(8,128)(2,1)S(1)} %get-tuple-element.23), channel_id=1, source_target_pairs={{0,112},{16,0},{32,16},{48,32},{64,48},{80,64},{96,80},{112,96},{1... | collective-permute-start | bytes 737288 | tf_op jit(solution)/shard_map/ppermute | solution.py:20
  61.3 3.9 %collective-permute-start.2 = (bf16[320,384]{1,0:T(8,128)(2,1)S(1)}, bf16[320,384]{1,0:T(8,128)(2,1)S(1)}, u32[]{:S(2)}, u32[]{:S(2)}) collective-permute-start(bf16[320,384]{1,0:T(8,128)(2,1)S(1)} %get-tuple-element.24), channel_id=1, source_target_pairs={{0,16},{16,32},{32,48},{48,64},{64,80},{80,96},{96,112},{112,0},{1... | collective-permute-start | bytes 737288 | tf_op jit(solution)/shard_map/ppermute | solution.py:20
  65.2 3.0 %shard_map.76 = (bf16[640,384]{1,0:T(8,128)(2,1)S(1)}, bf16[640,384]{1,0:T(8,128)(2,1)S(1)}) custom-call(s32[2]{0:T(128)S(1)} %pad_add_fusion.refs_0_, bf16[640,768]{1,0:T(8,128)(2,1)S(1)} %bitcast.30, bf16[3,3,768,128]{3,2,1,0:T(8,128)(2,1)S(1)} %bitcast.26, bf16[3,3,768,128]{3,2,1,0:T(8,128)(2,1)} %collective-permute-done.1.refs_3_), custom_call_target="tpu_custom_call" | custom-call | flops 754974720 | bytes 4194304 | tf_op jit(solution)/shard_map/pallas_call | solution.py:85
  68.2 0.0 collective-permute-done.6.refs_1_
  68.2 0.1 shard_map.81
  68.3 2.6 %collective-permute-start.7 = (bf16[640,384]{1,0:T(8,128)(2,1)S(1)}, bf16[640,384]{1,0:T(8,128)(2,1)S(1)}, u32[]{:S(2)}, u32[]{:S(2)}) collective-permute-start(bf16[640,384]{1,0:T(8,128)(2,1)S(1)} %shard_map.81), channel_id=1, source_target_pairs={{0,112},{16,0},{32,16},{48,32},{64,48},{80,64},{96,80},{112,96},{1... | collective-permute-start | bytes 1474568 | tf_op jit(solution)/shard_map/ppermute | solution.py:20
  70.9 0.0 collective-permute-done.2.refs_1_
  70.9 0.1 shard_map.78
  71.0 0.0 copy-start.5
  71.0 0.0 copy-start.6
  71.0 3.3 %collective-permute-start.3 = (bf16[640,384]{1,0:T(8,128)(2,1)S(1)}, bf16[640,384]{1,0:T(8,128)(2,1)S(1)}, u32[]{:S(2)}, u32[]{:S(2)}) collective-permute-start(bf16[640,384]{1,0:T(8,128)(2,1)S(1)} %shard_map.78), channel_id=1, source_target_pairs={{0,16},{16,32},{32,48},{48,64},{64,80},{80,96},{96,112},{112,0},{1... | collective-permute-start | bytes 1474568 | tf_op jit(solution)/shard_map/ppermute | solution.py:20
  74.3 2.4 %shard_map.75 = (bf16[640,384]{1,0:T(8,128)(2,1)S(1)}, bf16[640,384]{1,0:T(8,128)(2,1)S(1)}) custom-call(s32[2]{0:T(128)S(1)} %pad_add_fusion.refs_0_, bf16[640,768]{1,0:T(8,128)(2,1)S(1)} %bitcast.31, bf16[3,3,768,128]{3,2,1,0:T(8,128)(2,1)S(1)} %bitcast.27, bf16[3,3,768,128]{3,2,1,0:T(8,128)(2,1)} %collective-permute-done.1.refs_3_), custom_call_target="tpu_custom_call" | custom-call | flops 754974720 | bytes 4194304 | tf_op jit(solution)/shard_map/pallas_call | solution.py:85
  76.7 3.1 %collective-permute-done.7.refs_1_ = bf16[640,384]{1,0:T(8,128)(2,1)S(1)} collective-permute-done((bf16[640,384]{1,0:T(8,128)(2,1)S(1)}, bf16[640,384]{1,0:T(8,128)(2,1)S(1)}, u32[]{:S(2)}, u32[]{:S(2)}) %collective-permute-start.7) | collective-permute-done | bytes 491552 | tf_op jit(solution)/shard_map/ppermute | solution.py:20
  79.8 0.9 shard_map.82
  80.7 5.4 %collective-permute-start.8 = (bf16[640,384]{1,0:T(8,128)(2,1)}, bf16[640,384]{1,0:T(8,128)(2,1)}, u32[]{:S(2)}, u32[]{:S(2)}) collective-permute-start(bf16[640,384]{1,0:T(8,128)(2,1)} %shard_map.82), channel_id=1, source_target_pairs={{0,112},{16,0},{32,16},{48,32},{64,48},{80,64},{96,80},{112,96},{1... | collective-permute-start | bytes 1474568 | tf_op jit(solution)/shard_map/ppermute | solution.py:20
  86.1 0.0 collective-permute-done.3.refs_1_
  86.1 0.9 shard_map.79
  87.0 1.9 %collective-permute-start.4 = (bf16[640,384]{1,0:T(8,128)(2,1)}, bf16[640,384]{1,0:T(8,128)(2,1)}, u32[]{:S(2)}, u32[]{:S(2)}) collective-permute-start(bf16[640,384]{1,0:T(8,128)(2,1)} %shard_map.79), channel_id=1, source_target_pairs={{0,16},{16,32},{32,48},{48,64},{64,80},{80,96},{96,112},{112,0},{1... | collective-permute-start | bytes 1474568 | tf_op jit(solution)/shard_map/ppermute | solution.py:20
  88.9 0.0 copy-done.5
  89.0 0.0 copy-done.6
  89.0 1.9 %collective-permute-start.10 = (f32[2,3,128]{2,0,1:T(2,128)S(1)}, f32[2,3,128]{2,0,1:T(2,128)}, u32[]{:S(2)}, u32[]{:S(2)}) collective-permute-start(f32[2,3,128]{2,0,1:T(2,128)S(1)} %pad_maximum_fusion), channel_id=1, source_target_pairs={{0,1},{1,0},{2,3},{3,2},{4,5},{5,4},{6,7},{7,6},{8,9},{9,8},{10,11... | collective-permute-start | bytes 9224 | tf_op jit(solution)/shard_map/ppermute | solution.py:20
  90.9 3.1 %shard_map.74 = (bf16[640,384]{1,0:T(8,128)(2,1)S(1)}, bf16[640,384]{1,0:T(8,128)(2,1)S(1)}, bf16[640,384]{1,0:T(8,128)(2,1)S(1)}) custom-call(s32[2]{0:T(128)S(1)} %pad_add_fusion.refs_0_, bf16[640,768]{1,0:T(8,128)(2,1)S(1)} %bitcast.32, bf16[3,3,768,128]{3,2,1,0:T(8,128)(2,1)S(1)} %bitcast.28, bf16[3,3,768,128]{3,2,1,0:T(8,128)(2,1)} %collective-permute-done.1.refs_3_), custom_call_target="tpu_custom_call" | custom-call | flops 1132462080 | bytes 4194304 | tf_op jit(solution)/shard_map/pallas_call | solution.py:85
  94.1 0.0 copy-start.2
  94.1 0.8 copy-done.2
  94.9 0.0 collective-permute-done.8.refs_1_
  94.9 1.2 shard_map.83
  96.1 5.2 %collective-permute-start.9 = (bf16[640,384]{1,0:T(8,128)(2,1)S(1)}, bf16[640,384]{1,0:T(8,128)(2,1)S(1)}, u32[]{:S(2)}, u32[]{:S(2)}) collective-permute-start(bf16[640,384]{1,0:T(8,128)(2,1)S(1)} %shard_map.83), channel_id=1, source_target_pairs={{0,112},{16,0},{32,16},{48,32},{64,48},{80,64},{96,80},{112,96},{1... | collective-permute-start | bytes 1474568 | tf_op jit(solution)/shard_map/ppermute | solution.py:20
  101.3 0.0 collective-permute-done.4.refs_1_
  101.3 1.2 shard_map.80
  102.4 1.9 %collective-permute-start.5 = (bf16[640,384]{1,0:T(8,128)(2,1)S(1)}, bf16[640,384]{1,0:T(8,128)(2,1)S(1)}, u32[]{:S(2)}, u32[]{:S(2)}) collective-permute-start(bf16[640,384]{1,0:T(8,128)(2,1)S(1)} %shard_map.80), channel_id=1, source_target_pairs={{0,16},{16,32},{32,48},{48,64},{64,80},{80,96},{96,112},{112,0},{1... | collective-permute-start | bytes 1474568 | tf_op jit(solution)/shard_map/ppermute | solution.py:20
  104.3 0.1 add_multiply_fusion
  104.4 0.1 iota_add_fusion
  104.5 0.0 collective-permute-done.10
  104.5 0.7 fusion.17.gain
  105.2 1.0 fusion.14
  106.1 6.6 %collective-permute-done.9.third = bf16[640,384]{1,0:T(8,128)(2,1)S(1)} collective-permute-done((bf16[640,384]{1,0:T(8,128)(2,1)S(1)}, bf16[640,384]{1,0:T(8,128)(2,1)S(1)}, u32[]{:S(2)}, u32[]{:S(2)}) %collective-permute-start.9) | collective-permute-done | bytes 491552 | tf_op jit(solution)/shard_map/ppermute | solution.py:20
  112.7 6.8 %collective-permute-done.5.second = bf16[640,384]{1,0:T(8,128)(2,1)S(1)} collective-permute-done((bf16[640,384]{1,0:T(8,128)(2,1)S(1)}, bf16[640,384]{1,0:T(8,128)(2,1)S(1)}, u32[]{:S(2)}, u32[]{:S(2)}) %collective-permute-start.5) | collective-permute-done | bytes 491552 | tf_op jit(solution)/shard_map/ppermute | solution.py:20
  119.5 0.5 shard_map.84
  120.0 1.9 %collective-permute-start.11 = (bf16[640,256]{1,0:T(8,128)(2,1)S(1)}, bf16[640,256]{1,0:T(8,128)(2,1)S(1)}, u32[]{:S(2)}, u32[]{:S(2)}) collective-permute-start(bf16[640,256]{1,0:T(8,128)(2,1)S(1)} %get-tuple-element.22), channel_id=1, source_target_pairs={{0,1},{1,0},{2,3},{3,2},{4,5},{5,4},{6,7},{7,6},{8,9},{9,8},{10,11... | collective-permute-start | bytes 983048 | tf_op jit(solution)/shard_map/ppermute | solution.py:20
  121.9 0.1 broadcast_compare_fusion
  122.0 0.1 lt.32
  122.2 1.3 collective-permute-done.11
  123.6 0.7 fusion.19
  124.3 0.6 fusion.1
  124.9 0.7 fusion.9
  125.6 0.1 reshape.91
  125.7 0.1 copy.14
  125.8 0.1 copy.12
  125.9 21.2 %all_to_all.15 = bf16[64,10,128]{2,1,0:T(8,128)(2,1)S(1)} all-to-all(bf16[64,10,128]{2,1,0:T(8,128)(2,1)S(1)} %copy.12), channel_id=1, replica_groups=mesh['section'=4,'blk'=8,'zlo'=2,'x'=4,'core'=2] {'blk','zlo','x'}, dimensions={0} | all-to-all | bytes 327680 | tf_op jit(solution)/shard_map/all_to_all | solution.py:229
  147.1 0.7 shard_map.85
  (14 shorter events, 0.1 us)
Async XLA Ops:
  0.0 6.9 %copy-start = (f32[16,2,6144]{2,1,0:T(2,128)S(1)}, f32[16,2,6144]{2,1,0:T(2,128)}, u32[]{:S(2)}) copy-start(f32[16,2,6144]{2,1,0:T(2,128)} %param.9) | copy-start | bytes 2359300
  0.0 57.0 %copy-start.1 = (bf16[1,768,3,3,128]{4,1,3,2,0:T(8,128)(2,1)S(1)}, bf16[1,768,3,3,128]{4,1,3,2,0:T(8,128)(2,1)}, u32[]{:S(2)}) copy-start(bf16[1,768,3,3,128]{4,1,3,2,0:T(8,128)(2,1)} %param.10) | copy-start | bytes 5308420
  0.0 16.3 %collective-permute-start = (bf16[10,6144]{1,0:T(8,128)(2,1)}, bf16[10,6144]{1,0:T(8,128)(2,1)S(1)}, u32[]{:S(2)}, u32[]{:S(2)}) collective-permute-start(bf16[10,6144]{1,0:T(8,128)(2,1)} %bitcast.37), channel_id=1, source_target_pairs={{0,128},{128,256},{256,384},{384,0},{1,129},{129,257},{257,385},{3... | collective-permute-start | bytes 368648 | tf_op jit(solution)/shard_map/ppermute | solution.py:20
  17.2 17.0 %all-to-all-start = ((bf16[8,16,768]{2,1,0:T(8,128)(2,1)}), bf16[8,16,768]{2,1,0:T(8,128)(2,1)S(1)}, u32[]{:S(2)}, u32[]{:S(2)}) async-start(bf16[8,16,768]{2,1,0:T(8,128)(2,1)} %shard_map.73), calls=%async_computation | async-start | bytes 393216 | tf_op jit(solution)/shard_map/all_to_all | solution.py:189
  24.3 21.6 %collective-permute-start.1 = (bf16[3,3,768,128]{3,2,1,0:T(8,128)(2,1)}, bf16[3,3,768,128]{3,2,1,0:T(8,128)(2,1)}, u32[]{:S(2)}, u32[]{:S(2)}) collective-permute-start(bf16[3,3,768,128]{3,2,1,0:T(8,128)(2,1)} %bitcast.24), channel_id=1, source_target_pairs={{0,1},{1,0},{2,3},{3,2},{4,5},{5,4},{6,7},{7,6},{8,9},{9,8},{10,11... | collective-permute-start | bytes 5308424 | tf_op jit(solution)/shard_map/ppermute | solution.py:20
  34.2 1.1 copy-start.4
  35.3 21.6 %all-to-all-start.1 = ((bf16[8,80,768]{2,1,0:T(8,128)(2,1)}), bf16[8,80,768]{2,1,0:T(8,128)(2,1)S(1)}, u32[]{:S(2)}, u32[]{:S(2)}) async-start(bf16[8,80,768]{2,1,0:T(8,128)(2,1)} %broadcast_in_dim.37), calls=%async_computation.1 | async-start | bytes 1966080 | tf_op jit(solution)/shard_map/all_to_all | solution.py:193
  59.4 8.9 %collective-permute-start.6 = (bf16[320,384]{1,0:T(8,128)(2,1)S(1)}, bf16[320,384]{1,0:T(8,128)(2,1)S(1)}, u32[]{:S(2)}, u32[]{:S(2)}) collective-permute-start(bf16[320,384]{1,0:T(8,128)(2,1)S(1)} %get-tuple-element.23), channel_id=1, source_target_pairs={{0,112},{16,0},{32,16},{48,32},{64,48},{80,64},{96,80},{112,96},{1... | collective-permute-start | bytes 737288 | tf_op jit(solution)/shard_map/ppermute | solution.py:20
  61.3 9.6 %collective-permute-start.2 = (bf16[320,384]{1,0:T(8,128)(2,1)S(1)}, bf16[320,384]{1,0:T(8,128)(2,1)S(1)}, u32[]{:S(2)}, u32[]{:S(2)}) collective-permute-start(bf16[320,384]{1,0:T(8,128)(2,1)S(1)} %get-tuple-element.24), channel_id=1, source_target_pairs={{0,16},{16,32},{32,48},{48,64},{64,80},{80,96},{96,112},{112,0},{1... | collective-permute-start | bytes 737288 | tf_op jit(solution)/shard_map/ppermute | solution.py:20
  68.3 11.5 %collective-permute-start.7 = (bf16[640,384]{1,0:T(8,128)(2,1)S(1)}, bf16[640,384]{1,0:T(8,128)(2,1)S(1)}, u32[]{:S(2)}, u32[]{:S(2)}) collective-permute-start(bf16[640,384]{1,0:T(8,128)(2,1)S(1)} %shard_map.81), channel_id=1, source_target_pairs={{0,112},{16,0},{32,16},{48,32},{64,48},{80,64},{96,80},{112,96},{1... | collective-permute-start | bytes 1474568 | tf_op jit(solution)/shard_map/ppermute | solution.py:20
  71.0 18.0 %copy-start.5 = (f32[1,3,128]{2,0,1:T(1,128)S(1)}, f32[1,3,128]{2,0,1:T(1,128)}, u32[]{:S(2)}) copy-start(f32[1,3,128]{2,0,1:T(1,128)} %param.12) | copy-start | bytes 4612
  71.0 18.0 %copy-start.6 = (f32[1,3,128]{2,0,1:T(1,128)S(1)}, f32[1,3,128]{2,0,1:T(1,128)}, u32[]{:S(2)}) copy-start(f32[1,3,128]{2,0,1:T(1,128)} %param.11) | copy-start | bytes 4612
  71.0 15.1 %collective-permute-start.3 = (bf16[640,384]{1,0:T(8,128)(2,1)S(1)}, bf16[640,384]{1,0:T(8,128)(2,1)S(1)}, u32[]{:S(2)}, u32[]{:S(2)}) collective-permute-start(bf16[640,384]{1,0:T(8,128)(2,1)S(1)} %shard_map.78), channel_id=1, source_target_pairs={{0,16},{16,32},{32,48},{48,64},{64,80},{80,96},{96,112},{112,0},{1... | collective-permute-start | bytes 1474568 | tf_op jit(solution)/shard_map/ppermute | solution.py:20
  80.7 14.2 %collective-permute-start.8 = (bf16[640,384]{1,0:T(8,128)(2,1)}, bf16[640,384]{1,0:T(8,128)(2,1)}, u32[]{:S(2)}, u32[]{:S(2)}) collective-permute-start(bf16[640,384]{1,0:T(8,128)(2,1)} %shard_map.82), channel_id=1, source_target_pairs={{0,112},{16,0},{32,16},{48,32},{64,48},{80,64},{96,80},{112,96},{1... | collective-permute-start | bytes 1474568 | tf_op jit(solution)/shard_map/ppermute | solution.py:20
  87.0 14.2 %collective-permute-start.4 = (bf16[640,384]{1,0:T(8,128)(2,1)}, bf16[640,384]{1,0:T(8,128)(2,1)}, u32[]{:S(2)}, u32[]{:S(2)}) collective-permute-start(bf16[640,384]{1,0:T(8,128)(2,1)} %shard_map.79), channel_id=1, source_target_pairs={{0,16},{16,32},{32,48},{48,64},{64,80},{80,96},{96,112},{112,0},{1... | collective-permute-start | bytes 1474568 | tf_op jit(solution)/shard_map/ppermute | solution.py:20
  89.0 15.5 %collective-permute-start.10 = (f32[2,3,128]{2,0,1:T(2,128)S(1)}, f32[2,3,128]{2,0,1:T(2,128)}, u32[]{:S(2)}, u32[]{:S(2)}) collective-permute-start(f32[2,3,128]{2,0,1:T(2,128)S(1)} %pad_maximum_fusion), channel_id=1, source_target_pairs={{0,1},{1,0},{2,3},{3,2},{4,5},{5,4},{6,7},{7,6},{8,9},{9,8},{10,11... | collective-permute-start | bytes 9224 | tf_op jit(solution)/shard_map/ppermute | solution.py:20
  94.1 0.8 copy-start.2
  94.9 24.6 %copy-start.3 = (bf16[640,384]{1,0:T(8,128)(2,1)S(1)}, bf16[640,384]{1,0:T(8,128)(2,1)}, u32[]{:S(2)}) copy-start(bf16[640,384]{1,0:T(8,128)(2,1)} %copy-done.2) | copy-start | bytes 1474564
  96.1 16.6 %collective-permute-start.9 = (bf16[640,384]{1,0:T(8,128)(2,1)S(1)}, bf16[640,384]{1,0:T(8,128)(2,1)S(1)}, u32[]{:S(2)}, u32[]{:S(2)}) collective-permute-start(bf16[640,384]{1,0:T(8,128)(2,1)S(1)} %shard_map.83), channel_id=1, source_target_pairs={{0,112},{16,0},{32,16},{48,32},{64,48},{80,64},{96,80},{112,96},{1... | collective-permute-start | bytes 1474568 | tf_op jit(solution)/shard_map/ppermute | solution.py:20
  102.4 17.1 %collective-permute-start.5 = (bf16[640,384]{1,0:T(8,128)(2,1)S(1)}, bf16[640,384]{1,0:T(8,128)(2,1)S(1)}, u32[]{:S(2)}, u32[]{:S(2)}) collective-permute-start(bf16[640,384]{1,0:T(8,128)(2,1)S(1)} %shard_map.80), channel_id=1, source_target_pairs={{0,16},{16,32},{32,48},{48,64},{64,80},{80,96},{96,112},{112,0},{1... | collective-permute-start | bytes 1474568 | tf_op jit(solution)/shard_map/ppermute | solution.py:20
  120.0 3.5 %collective-permute-start.11 = (bf16[640,256]{1,0:T(8,128)(2,1)S(1)}, bf16[640,256]{1,0:T(8,128)(2,1)S(1)}, u32[]{:S(2)}, u32[]{:S(2)}) collective-permute-start(bf16[640,256]{1,0:T(8,128)(2,1)S(1)} %get-tuple-element.22), channel_id=1, source_target_pairs={{0,1},{1,0},{2,3},{3,2},{4,5},{5,4},{6,7},{7,6},{8,9},{9,8},{10,11... | collective-permute-start | bytes 983048 | tf_op jit(solution)/shard_map/ppermute | solution.py:20

commit v4 on v3

v4 whole, which is shorter than its diff:
```python
import jax
import jax.numpy as jnp
from jax import lax
from jax.experimental import pallas as pl
from jax.experimental.pallas import tpu as pltpu
from jax.sharding import Mesh
from jax.sharding import PartitionSpec as P

AXES = ("section", "blk", "zlo", "x", "core")
CHIPS = ("zlo", "x")
SMALL = pl.BlockSpec(memory_space=pltpu.SMEM)
WHOLE = pl.BlockSpec(memory_space=pltpu.VMEM)
DISTANT = pl.BlockSpec(memory_space=pltpu.HBM)
LIMIT = pltpu.CompilerParams(vmem_limit_bytes=12 * 2**20)


def shifted(value, axis, steps):
    count = lax.axis_size(axis)
    pairs = [(source, (source + steps) % count) for source in range(count)]
    return lax.ppermute(value, axis, pairs)


def head_norm(values, gain):
    scale = jnp.sqrt(jnp.mean(values * values, axis=-1, keepdims=True) + 1e-06)
    return values / scale * gain


def stack_kernel(q_gain, k_gain, gains):
    heads = q_gain.shape[0]
    for head in range(heads):
        gains[head : head + 1] = q_gain[head]
        gains[heads + head : heads + head + 1] = k_gain[head]


def stacked(q_gain, k_gain):
    return pl.pallas_call(
        stack_kernel,
        out_shape=jax.ShapeDtypeStruct((2 * q_gain.shape[0], q_gain.shape[2]), jnp.float32),
        in_specs=[WHOLE, WHOLE],
        out_specs=WHOLE,
        compiler_params=LIMIT,
        cost_estimate=pl.CostEstimate(flops=0, bytes_accessed=2**14, transcendentals=0),
    )(q_gain, k_gain)


def pack_kernel(counts, place, stale, modul, out):
    rows, width = stale.shape
    blks, padded, slice_width = out.shape
    source = stale[...].astype(jnp.float32)
    spread = jnp.sqrt(jnp.mean(source * source, axis=-1, keepdims=True) + 1e-06)
    normed = source / spread * (1.0 + modul[1:2]) + modul[0:1]
    count = jnp.full((padded - rows, width), counts[0], jnp.int32).astype(jnp.float32)
    normed = jnp.concatenate([normed, count], axis=0).astype(out.dtype)
    for blk in range(blks):
        out[blk] = normed[:, blk * slice_width : (blk + 1) * slice_width]


def packed(counts, place, stale, modul, shape):
    return pl.pallas_call(
        pack_kernel,
        out_shape=jax.ShapeDtypeStruct(shape, jnp.bfloat16),
        in_specs=[SMALL, SMALL, WHOLE, WHOLE],
        out_specs=WHOLE,
        compiler_params=LIMIT,
        cost_estimate=pl.CostEstimate(flops=10**10, bytes_accessed=10**6, transcendentals=0),
    )(counts, place, stale, modul)


def spread_kernel(sliced, weights, out, rows):
    blks = sliced.shape[0]
    count = out.shape[1] // blks
    for blk in range(blks):
        rows[blk * count : (blk + 1) * count] = sliced[blk, :count].astype(jnp.float32)
    block = rows[...].astype(out.dtype)
    for chip in range(out.shape[0]):
        out[chip] = block


def spread(sliced, weights, shape):
    return pl.pallas_call(
        spread_kernel,
        out_shape=jax.ShapeDtypeStruct(shape, jnp.bfloat16),
        in_specs=[WHOLE, DISTANT],
        out_specs=WHOLE,
        scratch_shapes=[pltpu.VMEM(shape[1:], jnp.float32)],
        compiler_params=LIMIT,
        cost_estimate=pl.CostEstimate(flops=0, bytes_accessed=10**6, transcendentals=0),
    )(sliced, weights)


def product_kernel(steps, place, tokens, own, other, *refs):
    outs, block, sems = refs[:-2], refs[-2], refs[-1]
    pieces = len(outs) // len(steps)
    size = tokens.shape[0] // pieces
    row, core = place[0], place[1]
    heads, parts = own.shape[:2]

    def fetch(number):
        owner = lax.rem(row + steps[number], lax.axis_size("blk"))
        head = jnp.minimum(owner, 2 * heads - 1)
        lane = jnp.where(head >= heads, 1, 0)
        slot = number % 2

        @pl.when(lane == core)
        def _():
            pltpu.make_async_copy(own.at[head - lane * heads], block.at[slot], sems.at[slot]).start()

        @pl.when(lane != core)
        def _():
            pltpu.make_async_copy(other.at[head - lane * heads], block.at[slot], sems.at[slot]).start()

    fetch(0)
    for number in range(len(steps)):
        slot = number % 2
        if number + 1 < len(steps):
            fetch(number + 1)
        pltpu.make_async_copy(own.at[0], block.at[slot], sems.at[slot]).wait()
        weights = jnp.concatenate([block[slot, part] for part in range(parts)], axis=1)
        total = jnp.dot(tokens[...], weights, preferred_element_type=jnp.float32)
        for piece in range(pieces):
            out = outs[number * pieces + piece]
            out[...] = total[piece * size : (piece + 1) * size].astype(out.dtype)


def products(steps, place, tokens, own, other, pieces=1):
    rows, depth = tokens.shape
    parts, size = own.shape[1], own.shape[3]
    shape = jax.ShapeDtypeStruct((rows // pieces, parts * size), jnp.bfloat16)
    return pl.pallas_call(
        lambda *refs: product_kernel(steps, *refs),
        out_shape=[shape] * (pieces * len(steps)),
        in_specs=[SMALL, WHOLE, DISTANT, DISTANT],
        out_specs=[WHOLE] * (pieces * len(steps)),
        scratch_shapes=[
            pltpu.VMEM((2,) + own.shape[1:], jnp.bfloat16),
            pltpu.SemaphoreType.DMA((2,)),
        ],
        compiler_params=LIMIT,
        cost_estimate=pl.CostEstimate(
            flops=2 * rows * depth * parts * size * len(steps), bytes_accessed=4 * 2**20, transcendentals=0
        ),
    )(place, tokens, own, other)


def add_kernel(begin, first, second, out):
    rows = second.shape[0]
    total = first[begin : begin + rows].astype(jnp.float32) + second[...].astype(jnp.float32)
    out[begin : begin + rows] = total.astype(out.dtype)
    for low, high in ((0, begin), (begin + rows, out.shape[0])):
        if high > low:
            out[low:high] = first[low:high]


def added(first, second, begin=0):
    return pl.pallas_call(
        lambda *refs: add_kernel(begin, *refs),
        out_shape=jax.ShapeDtypeStruct(first.shape, first.dtype),
        in_specs=[WHOLE, WHOLE],
        out_specs=WHOLE,
        compiler_params=LIMIT,
        cost_estimate=pl.CostEstimate(flops=first.size, bytes_accessed=3 * 2**19, transcendentals=0),
    )(first, second)


def head_kernel(place, first, second, third, gains, theirs, query, pair):
    size = query.shape[1]
    heads = gains.shape[0] // 2
    owned = jnp.minimum(place[0], 2 * heads - 1)
    lane = jnp.where(owned >= heads, 1, 0)
    index = owned - lane * heads
    mine = lane == place[1]
    gain = []
    for part in range(2):
        at = pl.ds(part * heads + index, 1)
        gain.append(jnp.where(mine, gains[at], theirs[at]))
    total = first[...].astype(jnp.float32) + second[...].astype(jnp.float32)
    total = total + third[...].astype(jnp.float32)
    query[...] = head_norm(total[:, :size], gain[0]).astype(query.dtype)
    pair[:, :size] = head_norm(total[:, size : 2 * size], gain[1]).astype(pair.dtype)
    pair[:, size:] = total[:, 2 * size :].astype(pair.dtype)


def headed(place, first, second, third, gains, theirs):
    rows, size = first.shape[0], gains.shape[1]
    return pl.pallas_call(
        head_kernel,
        out_shape=[
            jax.ShapeDtypeStruct((rows, size), jnp.bfloat16),
            jax.ShapeDtypeStruct((rows, 2 * size), jnp.bfloat16),
        ],
        in_specs=[SMALL] + [WHOLE] * 5,
        out_specs=[WHOLE] * 2,
        compiler_params=LIMIT,
        cost_estimate=pl.CostEstimate(flops=10 * first.size, bytes_accessed=4 * 2**19, transcendentals=0),
    )(place, first, second, third, gains, theirs)


def attention_kernel(tok_rows, place, sliced, query, near, far, out):
    rows, size = query.shape
    blks = sliced.shape[0]
    chips = rows // (blks * tok_rows)
    key = lax.broadcasted_iota(jnp.int32, (1, rows), 1)
    chip = sum((key >= i * blks * tok_rows).astype(jnp.int32) for i in range(1, chips))
    rest = key - chip * (blks * tok_rows)
    blk = sum((rest >= i * tok_rows).astype(jnp.int32) for i in range(1, blks))
    begin = chip * (2 * tok_rows) + rest - blk * tok_rows
    limit = jnp.zeros((1, rows), jnp.float32)
    for i in range(blks):
        count = sliced[i, tok_rows : tok_rows + 1, :1].astype(jnp.float32)
        limit = jnp.where(blk == i, count, limit)
    lanes = (place[1], 1 - place[1])
    valid = [(begin + lane * tok_rows).astype(jnp.float32) < limit for lane in lanes]
    pairs = (near, far)
    step = 2 * blks * tok_rows
    for part in range(rows // step):
        block = query[part * step : (part + 1) * step]
        scores = []
        for pair, mask in zip(pairs, valid):
            product = lax.dot_general(
                block, pair[:, :size], (((1,), (1,)), ((), ())), preferred_element_type=jnp.float32
            )
            scores.append(jnp.where(mask, product * (size**-0.5), -1e30))
        top = jnp.maximum(*(jnp.max(score, axis=-1, keepdims=True) for score in scores))
        denom, mixed = 0.0, 0.0
        for score, pair in zip(scores, pairs):
            expo = jnp.exp(score - top)
            denom += jnp.sum(expo, axis=-1, keepdims=True)
            mixed += jnp.dot(
                expo.astype(jnp.bfloat16), pair[:, size:], preferred_element_type=jnp.float32
            )
        mixed = mixed / denom
        for i in range(2):
            for j in range(blks):
                piece = mixed[(i * blks + j) * tok_rows : (i * blks + j + 1) * tok_rows]
                out[j * chips + 2 * part + i] = piece.astype(out.dtype)


def attended(tok_rows, place, sliced, query, near, far):
    rows, size = query.shape
    return pl.pallas_call(
        lambda *refs: attention_kernel(tok_rows, *refs),
        out_shape=jax.ShapeDtypeStruct((rows // tok_rows, tok_rows, size), jnp.bfloat16),
        in_specs=[SMALL] + [WHOLE] * 4,
        out_specs=WHOLE,
        compiler_params=LIMIT,
        cost_estimate=pl.CostEstimate(
            flops=8 * rows * rows * size, bytes_accessed=2**20, transcendentals=2 * rows * rows
        ),
    )(place, sliced, query, near, far)


def merge_kernel(blocks, out):
    blks, chips = blocks.shape[:2]
    size = blocks.shape[3]
    heads = out.shape[2] // (chips * size)
    for chip in range(chips):
        for blk in range(heads):
            begin = (chip * heads + blk) * size
            out[0, :, begin : begin + size] = blocks[blk, chip]


def merged(blocks, shape):
    return pl.pallas_call(
        merge_kernel,
        out_shape=jax.ShapeDtypeStruct(shape, blocks.dtype),
        in_specs=[WHOLE],
        out_specs=WHOLE,
        compiler_params=LIMIT,
        cost_estimate=pl.CostEstimate(flops=0, bytes_accessed=2**19, transcendentals=0),
    )(blocks)


def on_device(stale, layer_of_section, mod_table, w_qkv, q_gain, k_gain, counts):
    tok_rows, width = stale.shape[1:]
    blks = lax.axis_size("blk")
    chips = lax.axis_size("zlo") * lax.axis_size("x")
    slice_width, head_size = w_qkv.shape[1], w_qkv.shape[4]

    received = shifted(stale[0], "section", 1)
    modul = lax.dynamic_index_in_dim(mod_table, layer_of_section[0], 0, keepdims=False)
    place = jnp.stack([lax.axis_index("blk"), lax.axis_index("core")]).astype(jnp.int32)

    own = w_qkv[0].transpose(1, 2, 0, 3)
    gains = stacked(q_gain.transpose(1, 0, 2), k_gain.transpose(1, 0, 2))
    other = shifted(own, "core", 1)
    theirs = shifted(gains, "core", 1)

    sent = packed(counts, place, received, modul, (blks, 16, slice_width))
    sliced = lax.all_to_all(sent, "blk", 0, 0, tiled=False)
    copies = spread(sliced, other, (chips, blks * tok_rows, slice_width))
    tokens = lax.all_to_all(copies, CHIPS, 0, 0, tiled=False)
    tokens = tokens.reshape(chips * blks * tok_rows, slice_width)
    half = tokens.shape[0] // 2

    up, down = products((4,), place, tokens, own, other, 2)
    up, down = shifted(up, "blk", 1), shifted(down, "blk", -1)
    three, five = products((3, 5), place, tokens, own, other)
    up, down = shifted(added(three, up), "blk", 1), shifted(added(five, down, half), "blk", -1)
    two, six, one, seven, zero = products((2, 6, 1, 7, 0), place, tokens, own, other)
    up, down = shifted(added(two, up), "blk", 1), shifted(added(six, down), "blk", -1)
    up, down = shifted(added(one, up), "blk", 1), shifted(added(seven, down), "blk", -1)
    query, near = headed(place, zero, up, down, gains, theirs)
    far = shifted(near, "core", 1)

    mixed = attended(tok_rows, place, sliced, query, near, far)
    returned = lax.all_to_all(mixed, ("blk",) + CHIPS, 0, 0, tiled=False)
    return merged(returned.reshape(blks, chips, tok_rows, head_size), (1, tok_rows, width))


def solution(mesh):
    sizes = mesh.shape
    fine = Mesh(mesh.devices.reshape(sizes["section"], sizes["blk"], 2, 4, 2), AXES)
    uly = CHIPS + ("core",)
    in_specs = (
        P("section", ("blk",) + uly, None),
        P("section"),
        P(),
        P("section", "blk", uly, None, None),
        P("section", uly, None),
        P("section", uly, None),
        P("blk"),
    )
    out_specs = P("section", ("blk",) + uly, None)
    return jax.shard_map(
        on_device, mesh=fine, in_specs=in_specs, out_specs=out_specs, check_vma=False
    )
```

time: 149 us -> 138 us (0.926)
  blocking collectives: 21.2 us -> 62.5 us
  waiting for transfers between devices: 45.6 us -> 21.4 us
  starting transfers between devices: 55.7 us -> 37.7 us
  Pallas kernels: 17.3 us -> 14.1 us
  other arithmetic: 2.59 us -> 0.08 us
  local copies, waits for them, and re-layouts: 2.43 us -> 0.03 us
    all_to_all x0 -> x2, blocking collectives: none -> 38.5 us  [the longest x1 21.7 us: on_device(): tokens = lax.all_to_all(copies, CHIPS, 0, 0, tiled=False)]
    all_to_all x2 -> x0, waiting for transfers between devices: 19.1 us -> none  [the longest x1 11.1 us: on_device(): tokens = lax.all_to_all(copies, CHIPS, 0, 0, tiled=False)]
    all_to_all x2 -> x0, starting transfers between devices: 17.6 us -> none  [the longest x1 10.5 us: on_device(): tokens = lax.all_to_all(copies, CHIPS, 0, 0, tiled=False)]
    ppermute x12, waiting for transfers between devices: 26.5 us -> 21.4 us  [shifted(): return lax.ppermute(value, axis, pairs)]
    pallas_call x6, Pallas kernels: 4.31 us -> 0.65 us  [added(): pl.pallas_call(lambda *refs: add_kernel(begin, *refs), out_shape=jax.Shap...]
    all_to_all x1, blocking collectives: 21.2 us -> 24 us  [on_device(): returned = lax.all_to_all(mixed, ('blk',) + CHIPS, 0, 0, tiled=False)]
    pallas_call x0 -> x3, Pallas kernels: none -> 2.72 us  [the longest x1 2.63 us: attended(): pl.pallas_call(lambda *refs: attention_kernel(tok_rows, *refs), out_shape...]
    pallas_call x4 -> x3, Pallas kernels: 10.9 us -> 8.19 us  [products(): pl.pallas_call(lambda *refs: product_kernel(steps, *refs), out_shape=[sha...]
  transfers between devices with their start and end apart: 14 -> 12, of which waited for: 7 -> 7; matrix products, arithmetic and copies ran while one was open for 2% -> 0% of each run, Pallas kernels for 9% -> 6%
where the time goes in v4:
time: 138 us; the launch traced here: 137 us
  blocking collectives  62.5 us (45%)
  starting transfers between devices  37.7 us (27%)
  waiting for transfers between devices  21.4 us (16%)
  Pallas kernels  14.1 us (10%)
  between operations  1.55 us (1%)
    ppermute x12, starting transfers between devices, shifted(): return lax.ppermute(value, axis, pairs)  37.7 us
    all_to_all x1, blocking collectives, on_device(): returned = lax.all_to_all(mixed, ('blk',) + CHIPS, 0, 0, tiled=False)  24 us
    all_to_all x1, blocking collectives, on_device(): tokens = lax.all_to_all(copies, CHIPS, 0, 0, tiled=False)  21.7 us
    ppermute x12, waiting for transfers between devices, shifted(): return lax.ppermute(value, axis, pairs)  21.4 us
    all_to_all x1, blocking collectives, on_device(): sliced = lax.all_to_all(sent, 'blk', 0, 0, tiled=False)  16.8 us
    pallas_call x3, Pallas kernels, products(): pl.pallas_call(lambda *refs: product_kernel(steps, *refs), out_shape=[sha...  8.19 us
  transfers between devices with their start and end apart: 12, of which 7 were waited for; matrix products, arithmetic and copies ran while one was open for 0% of the time, Pallas kernels for 6%

profile of v4, /device:TPU:6, one launch (start us, length us, event | category | flops | bytes accessed | tf_op | source)
XLA Modules:
  0.0 137.4 jit_solution(14006642558972755281)
XLA Ops:
  0.0 0.0 copy-start
  0.0 6.2 %collective-permute-start = (bf16[10,6144]{1,0:T(8,128)(2,1)}, bf16[10,6144]{1,0:T(8,128)(2,1)S(1)}, u32[]{:S(2)}, u32[]{:S(2)}) collective-permute-start(bf16[10,6144]{1,0:T(8,128)(2,1)} %bitcast.26), channel_id=1, source_target_pairs={{0,128},{128,256},{256,384},{384,0},{1,129},{129,257},{257,385},{3... | collective-permute-start | bytes 368648 | tf_op jit(solution)/shard_map/ppermute | solution.py:20
  6.2 1.9 %collective-permute-start.1 = (bf16[3,3,768,128]{3,2,1,0:T(8,128)(2,1)}, bf16[3,3,768,128]{3,2,1,0:T(8,128)(2,1)S(1)}, u32[]{:S(2)}, u32[]{:S(2)}) collective-permute-start(bf16[3,3,768,128]{3,2,1,0:T(8,128)(2,1)} %bitcast.19), channel_id=1, source_target_pairs={{0,1},{1,0},{2,3},{3,2},{4,5},{5,4},{6,7},{7,6},{8,9},{9,8},{10,11... | collective-permute-start | bytes 5308424 | tf_op jit(solution)/shard_map/ppermute | solution.py:20
  8.8 0.0 copy-done
  9.5 0.1 pad_add_fusion.place.refs_0_
  9.6 6.8 %collective-permute-done.stale = bf16[10,6144]{1,0:T(8,128)(2,1)S(1)} collective-permute-done((bf16[10,6144]{1,0:T(8,128)(2,1)}, bf16[10,6144]{1,0:T(8,128)(2,1)S(1)}, u32[]{:S(2)}, u32[]{:S(2)}) %collective-permute-start) | collective-permute-done | bytes 122912 | tf_op jit(solution)/shard_map/ppermute | solution.py:20
  16.3 0.8 shard_map.73
  17.1 16.8 %all_to_all.15.sliced.refs_1_ = bf16[8,16,768]{2,1,0:T(8,128)(2,1)S(1)} all-to-all(bf16[8,16,768]{2,1,0:T(8,128)(2,1)S(1)} %shard_map.73), channel_id=1, replica_groups=mesh['section'=4,'blk'=8,'zlo'=2,'x'=4,'core'=2] {'blk'}, dimensions={0} | all-to-all | bytes 393216 | tf_op jit(solution)/shard_map/all_to_all | solution.py:289
  33.9 0.0 copy-start.1
  33.9 0.0 collective-permute-done.1.weights.refs_3_
  33.9 0.1 shard_map.74
  34.0 21.7 %all_to_all.16 = bf16[8,80,768]{2,1,0:T(8,128)(2,1)S(1)} all-to-all(bf16[8,80,768]{2,1,0:T(8,128)(2,1)S(1)} %shard_map.74), channel_id=1, replica_groups=mesh['section'=4,'blk'=8,'zlo'=2,'x'=4,'core'=2] {'zlo','x'}, dimensions={0} | all-to-all | bytes 1966080 | tf_op jit(solution)/shard_map/all_to_all | solution.py:291
  55.7 0.0 copy-done.1
  55.7 1.4 %shard_map.77 = (bf16[320,384]{1,0:T(8,128)(2,1)S(1)}, bf16[320,384]{1,0:T(8,128)(2,1)S(1)}) custom-call(s32[2]{0:T(128)S(1)} %pad_add_fusion.place.refs_0_, bf16[640,768]{1,0:T(8,128)(2,1)S(1)} %bitcast.16, bf16[3,3,768,128]{3,2,1,0:T(8,128)(2,1)S(1)} %bitcast.20, bf16[3,3,768,128]{3,2,1,0:T(8,128)(2,1)S(1)} %collective-permute-done.1.weights.refs_3_), custom_call_target="tpu_custom_call" | custom-call | flops 377487360 | bytes 4194304 | tf_op jit(solution)/shard_map/pallas_call | solution.py:129
  57.1 1.9 %collective-permute-start.6 = (bf16[320,384]{1,0:T(8,128)(2,1)S(1)}, bf16[320,384]{1,0:T(8,128)(2,1)S(1)}, u32[]{:S(2)}, u32[]{:S(2)}) collective-permute-start(bf16[320,384]{1,0:T(8,128)(2,1)S(1)} %get-tuple-element.24), channel_id=1, source_target_pairs={{0,112},{16,0},{32,16},{48,32},{64,48},{80,64},{96,80},{112,96},{1... | collective-permute-start | bytes 737288 | tf_op jit(solution)/shard_map/ppermute | solution.py:20
  59.0 3.9 %collective-permute-start.2 = (bf16[320,384]{1,0:T(8,128)(2,1)S(1)}, bf16[320,384]{1,0:T(8,128)(2,1)S(1)}, u32[]{:S(2)}, u32[]{:S(2)}) collective-permute-start(bf16[320,384]{1,0:T(8,128)(2,1)S(1)} %get-tuple-element.20), channel_id=1, source_target_pairs={{0,16},{16,32},{32,48},{48,64},{64,80},{80,96},{96,112},{112,0},{1... | collective-permute-start | bytes 737288 | tf_op jit(solution)/shard_map/ppermute | solution.py:20
  63.0 2.2 %shard_map.76 = (bf16[640,384]{1,0:T(8,128)(2,1)S(1)}, bf16[640,384]{1,0:T(8,128)(2,1)S(1)}) custom-call(s32[2]{0:T(128)S(1)} %pad_add_fusion.place.refs_0_, bf16[640,768]{1,0:T(8,128)(2,1)S(1)} %bitcast.17, bf16[3,3,768,128]{3,2,1,0:T(8,128)(2,1)S(1)} %bitcast.21, bf16[3,3,768,128]{3,2,1,0:T(8,128)(2,1)S(1)} %collective-permute-done.1.weights.refs_3_), custom_call_target="tpu_custom_call" | custom-call | flops 754974720 | bytes 4194304 | tf_op jit(solution)/shard_map/pallas_call | solution.py:129
  65.2 0.0 collective-permute-done.6.refs_1_
  65.2 0.1 shard_map.81
  65.3 3.1 %collective-permute-start.7 = (bf16[640,384]{1,0:T(8,128)(2,1)S(1)}, bf16[640,384]{1,0:T(8,128)(2,1)S(1)}, u32[]{:S(2)}, u32[]{:S(2)}) collective-permute-start(bf16[640,384]{1,0:T(8,128)(2,1)S(1)} %shard_map.81), channel_id=1, source_target_pairs={{0,112},{16,0},{32,16},{48,32},{64,48},{80,64},{96,80},{112,96},{1... | collective-permute-start | bytes 1474568 | tf_op jit(solution)/shard_map/ppermute | solution.py:20
  68.4 0.0 collective-permute-done.2.refs_1_
  68.4 0.1 shard_map.78
  68.5 2.7 %collective-permute-start.3 = (bf16[640,384]{1,0:T(8,128)(2,1)S(1)}, bf16[640,384]{1,0:T(8,128)(2,1)S(1)}, u32[]{:S(2)}, u32[]{:S(2)}) collective-permute-start(bf16[640,384]{1,0:T(8,128)(2,1)S(1)} %shard_map.78), channel_id=1, source_target_pairs={{0,16},{16,32},{32,48},{48,64},{64,80},{80,96},{96,112},{112,0},{1... | collective-permute-start | bytes 1474568 | tf_op jit(solution)/shard_map/ppermute | solution.py:20
  71.2 4.6 %shard_map.75 = (bf16[640,384]{1,0:T(8,128)(2,1)S(1)}, bf16[640,384]{1,0:T(8,128)(2,1)S(1)}, bf16[640,384]{1,0:T(8,128)(2,1)S(1)}, bf16[640,384]{1,0:T(8,128)(2,1)S(1)}, bf16[640,384]{1,0:T(8,128)(2,1)S(1)}) custom-call(s32[2]{0:T(128)S(1)} %pad_add_fusion.place.refs_0_, bf16[640,768]{1,0:T(8,128)(2,1)S(1)} %bitcast.18, ...), custom_call_target="tpu_custom_call" | custom-call | flops 1887436800 | bytes 4194304 | tf_op jit(solution)/shard_map/pallas_call | solution.py:129
  75.8 0.7 collective-permute-done.7.refs_1_
  76.5 0.1 shard_map.82
  76.7 4.6 %collective-permute-start.8 = (bf16[640,384]{1,0:T(8,128)(2,1)S(1)}, bf16[640,384]{1,0:T(8,128)(2,1)S(1)}, u32[]{:S(2)}, u32[]{:S(2)}) collective-permute-start(bf16[640,384]{1,0:T(8,128)(2,1)S(1)} %shard_map.82), channel_id=1, source_target_pairs={{0,112},{16,0},{32,16},{48,32},{64,48},{80,64},{96,80},{112,96},{1... | collective-permute-start | bytes 1474568 | tf_op jit(solution)/shard_map/ppermute | solution.py:20
  81.3 0.0 collective-permute-done.3.refs_1_
  81.3 0.1 shard_map.79
  81.4 0.0 copy-start.2
  81.4 0.0 copy-start.3
  81.5 1.9 %collective-permute-start.4 = (bf16[640,384]{1,0:T(8,128)(2,1)S(1)}, bf16[640,384]{1,0:T(8,128)(2,1)S(1)}, u32[]{:S(2)}, u32[]{:S(2)}) collective-permute-start(bf16[640,384]{1,0:T(8,128)(2,1)S(1)} %shard_map.79), channel_id=1, source_target_pairs={{0,16},{16,32},{32,48},{48,64},{64,80},{80,96},{96,112},{112,0},{1... | collective-permute-start | bytes 1474568 | tf_op jit(solution)/shard_map/ppermute | solution.py:20
  83.4 4.2 %collective-permute-done.8.refs_1_ = bf16[640,384]{1,0:T(8,128)(2,1)S(1)} collective-permute-done((bf16[640,384]{1,0:T(8,128)(2,1)S(1)}, bf16[640,384]{1,0:T(8,128)(2,1)S(1)}, u32[]{:S(2)}, u32[]{:S(2)}) %collective-permute-start.8) | collective-permute-done | bytes 491552 | tf_op jit(solution)/shard_map/ppermute | solution.py:20
  87.6 0.1 shard_map.83
  87.7 5.6 %collective-permute-start.9 = (bf16[640,384]{1,0:T(8,128)(2,1)S(1)}, bf16[640,384]{1,0:T(8,128)(2,1)S(1)}, u32[]{:S(2)}, u32[]{:S(2)}) collective-permute-start(bf16[640,384]{1,0:T(8,128)(2,1)S(1)} %shard_map.83), channel_id=1, source_target_pairs={{0,112},{16,0},{32,16},{48,32},{64,48},{80,64},{96,80},{112,96},{1... | collective-permute-start | bytes 1474568 | tf_op jit(solution)/shard_map/ppermute | solution.py:20
  93.3 0.0 collective-permute-done.4.refs_1_
  93.4 0.1 shard_map.80
  93.5 1.9 %collective-permute-start.5 = (bf16[640,384]{1,0:T(8,128)(2,1)S(1)}, bf16[640,384]{1,0:T(8,128)(2,1)S(1)}, u32[]{:S(2)}, u32[]{:S(2)}) collective-permute-start(bf16[640,384]{1,0:T(8,128)(2,1)S(1)} %shard_map.80), channel_id=1, source_target_pairs={{0,16},{16,32},{32,48},{48,64},{64,80},{80,96},{96,112},{112,0},{1... | collective-permute-start | bytes 1474568 | tf_op jit(solution)/shard_map/ppermute | solution.py:20
  95.4 0.0 copy-done.2
  95.4 0.0 copy-done.3
  95.5 1.9 %collective-permute-start.10 = (f32[6,128]{1,0:T(8,128)S(1)}, f32[6,128]{1,0:T(8,128)S(1)}, u32[]{:S(2)}, u32[]{:S(2)}) collective-permute-start(f32[6,128]{1,0:T(8,128)S(1)} %shard_map.84.gains), channel_id=1, source_target_pairs={{0,1},{1,0},{2,3},{3,2},{4,5},{5,4},{6,7},{7,6},{8,9},{9,8},{10,11... | collective-permute-start | bytes 9224 | tf_op jit(solution)/shard_map/ppermute | solution.py:20
  97.4 1.1 collective-permute-done.10.theirs
  98.5 1.1 collective-permute-done.9.third
  99.7 5.8 %collective-permute-done.5.second = bf16[640,384]{1,0:T(8,128)(2,1)S(1)} collective-permute-done((bf16[640,384]{1,0:T(8,128)(2,1)S(1)}, bf16[640,384]{1,0:T(8,128)(2,1)S(1)}, u32[]{:S(2)}, u32[]{:S(2)}) %collective-permute-start.5) | collective-permute-done | bytes 491552 | tf_op jit(solution)/shard_map/ppermute | solution.py:20
  105.4 1.1 shard_map.85
  106.5 1.9 %collective-permute-start.11 = (bf16[640,256]{1,0:T(8,128)(2,1)S(1)}, bf16[640,256]{1,0:T(8,128)(2,1)S(1)}, u32[]{:S(2)}, u32[]{:S(2)}) collective-permute-start(bf16[640,256]{1,0:T(8,128)(2,1)S(1)} %get-tuple-element.26.refs_3_), channel_id=1, source_target_pairs={{0,1},{1,0},{2,3},{3,2},{4,5},{5,4},{6,7},{7,6},{8,9},{9,8},{10,11... | collective-permute-start | bytes 983048 | tf_op jit(solution)/shard_map/ppermute | solution.py:20
  108.5 1.6 %collective-permute-done.11.refs_4_ = bf16[640,256]{1,0:T(8,128)(2,1)S(1)} collective-permute-done((bf16[640,256]{1,0:T(8,128)(2,1)S(1)}, bf16[640,256]{1,0:T(8,128)(2,1)S(1)}, u32[]{:S(2)}, u32[]{:S(2)}) %collective-permute-start.11) | collective-permute-done | bytes 327712 | tf_op jit(solution)/shard_map/ppermute | solution.py:20
  110.0 2.6 %shard_map.86 = bf16[64,10,128]{2,1,0:T(8,128)(2,1)S(1)} custom-call(s32[2]{0:T(128)S(1)} %pad_add_fusion.place.refs_0_, bf16[8,16,768]{2,1,0:T(8,128)(2,1)S(1)} %all_to_all.15.sliced.refs_1_, bf16[640,128]{1,0:T(8,128)(2,1)S(1)} %get-tuple-element.25.refs_2_, bf16[640,256]{1,0:T(8,128)(2,1)S(1)} %get-tuple-element.26.refs_3_, ...), custom_call_target="tpu_custom_call" | custom-call | flops 419430400 | bytes 1048576 | tf_op jit(solution)/shard_map/pallas_call | solution.py:240
  112.7 24.0 %all_to_all.17 = bf16[64,10,128]{2,1,0:T(8,128)(2,1)S(1)} all-to-all(bf16[64,10,128]{2,1,0:T(8,128)(2,1)S(1)} %shard_map.86), channel_id=1, replica_groups=mesh['section'=4,'blk'=8,'zlo'=2,'x'=4,'core'=2] {'blk','zlo','x'}, dimensions={0} | all-to-all | bytes 327680 | tf_op jit(solution)/shard_map/all_to_all | solution.py:306
  136.7 0.7 shard_map.87
  (2 shorter events, 0.0 us)
Async XLA Ops:
  0.0 8.8 %copy-start = (f32[16,2,6144]{2,1,0:T(2,128)S(1)}, f32[16,2,6144]{2,1,0:T(2,128)}, u32[]{:S(2)}) copy-start(f32[16,2,6144]{2,1,0:T(2,128)} %param.9) | copy-start | bytes 2359300
  0.0 16.3 %collective-permute-start = (bf16[10,6144]{1,0:T(8,128)(2,1)}, bf16[10,6144]{1,0:T(8,128)(2,1)S(1)}, u32[]{:S(2)}, u32[]{:S(2)}) collective-permute-start(bf16[10,6144]{1,0:T(8,128)(2,1)} %bitcast.26), channel_id=1, source_target_pairs={{0,128},{128,256},{256,384},{384,0},{1,129},{129,257},{257,385},{3... | collective-permute-start | bytes 368648 | tf_op jit(solution)/shard_map/ppermute | solution.py:20
  6.2 27.7 %collective-permute-start.1 = (bf16[3,3,768,128]{3,2,1,0:T(8,128)(2,1)}, bf16[3,3,768,128]{3,2,1,0:T(8,128)(2,1)S(1)}, u32[]{:S(2)}, u32[]{:S(2)}) collective-permute-start(bf16[3,3,768,128]{3,2,1,0:T(8,128)(2,1)} %bitcast.19), channel_id=1, source_target_pairs={{0,1},{1,0},{2,3},{3,2},{4,5},{5,4},{6,7},{7,6},{8,9},{9,8},{10,11... | collective-permute-start | bytes 5308424 | tf_op jit(solution)/shard_map/ppermute | solution.py:20
  33.9 21.8 %copy-start.1 = (bf16[1,768,3,3,128]{4,1,3,2,0:T(8,128)(2,1)S(1)}, bf16[1,768,3,3,128]{4,1,3,2,0:T(8,128)(2,1)}, u32[]{:S(2)}) copy-start(bf16[1,768,3,3,128]{4,1,3,2,0:T(8,128)(2,1)} %param.10) | copy-start | bytes 5308420
  57.1 8.1 %collective-permute-start.6 = (bf16[320,384]{1,0:T(8,128)(2,1)S(1)}, bf16[320,384]{1,0:T(8,128)(2,1)S(1)}, u32[]{:S(2)}, u32[]{:S(2)}) collective-permute-start(bf16[320,384]{1,0:T(8,128)(2,1)S(1)} %get-tuple-element.24), channel_id=1, source_target_pairs={{0,112},{16,0},{32,16},{48,32},{64,48},{80,64},{96,80},{112,96},{1... | collective-permute-start | bytes 737288 | tf_op jit(solution)/shard_map/ppermute | solution.py:20
  59.0 9.4 %collective-permute-start.2 = (bf16[320,384]{1,0:T(8,128)(2,1)S(1)}, bf16[320,384]{1,0:T(8,128)(2,1)S(1)}, u32[]{:S(2)}, u32[]{:S(2)}) collective-permute-start(bf16[320,384]{1,0:T(8,128)(2,1)S(1)} %get-tuple-element.20), channel_id=1, source_target_pairs={{0,16},{16,32},{32,48},{48,64},{64,80},{80,96},{96,112},{112,0},{1... | collective-permute-start | bytes 737288 | tf_op jit(solution)/shard_map/ppermute | solution.py:20
  65.3 11.3 %collective-permute-start.7 = (bf16[640,384]{1,0:T(8,128)(2,1)S(1)}, bf16[640,384]{1,0:T(8,128)(2,1)S(1)}, u32[]{:S(2)}, u32[]{:S(2)}) collective-permute-start(bf16[640,384]{1,0:T(8,128)(2,1)S(1)} %shard_map.81), channel_id=1, source_target_pairs={{0,112},{16,0},{32,16},{48,32},{64,48},{80,64},{96,80},{112,96},{1... | collective-permute-start | bytes 1474568 | tf_op jit(solution)/shard_map/ppermute | solution.py:20
  68.5 12.8 %collective-permute-start.3 = (bf16[640,384]{1,0:T(8,128)(2,1)S(1)}, bf16[640,384]{1,0:T(8,128)(2,1)S(1)}, u32[]{:S(2)}, u32[]{:S(2)}) collective-permute-start(bf16[640,384]{1,0:T(8,128)(2,1)S(1)} %shard_map.78), channel_id=1, source_target_pairs={{0,16},{16,32},{32,48},{48,64},{64,80},{80,96},{96,112},{112,0},{1... | collective-permute-start | bytes 1474568 | tf_op jit(solution)/shard_map/ppermute | solution.py:20
  76.7 10.9 %collective-permute-start.8 = (bf16[640,384]{1,0:T(8,128)(2,1)S(1)}, bf16[640,384]{1,0:T(8,128)(2,1)S(1)}, u32[]{:S(2)}, u32[]{:S(2)}) collective-permute-start(bf16[640,384]{1,0:T(8,128)(2,1)S(1)} %shard_map.82), channel_id=1, source_target_pairs={{0,112},{16,0},{32,16},{48,32},{64,48},{80,64},{96,80},{112,96},{1... | collective-permute-start | bytes 1474568 | tf_op jit(solution)/shard_map/ppermute | solution.py:20
  81.4 14.0 %copy-start.2 = (f32[1,3,128]{2,0,1:T(1,128)S(1)}, f32[1,3,128]{2,0,1:T(1,128)}, u32[]{:S(2)}) copy-start(f32[1,3,128]{2,0,1:T(1,128)} %param.11) | copy-start | bytes 4612
  81.4 14.0 %copy-start.3 = (f32[1,3,128]{2,0,1:T(1,128)S(1)}, f32[1,3,128]{2,0,1:T(1,128)}, u32[]{:S(2)}) copy-start(f32[1,3,128]{2,0,1:T(1,128)} %param.12) | copy-start | bytes 4612
  81.5 11.9 %collective-permute-start.4 = (bf16[640,384]{1,0:T(8,128)(2,1)S(1)}, bf16[640,384]{1,0:T(8,128)(2,1)S(1)}, u32[]{:S(2)}, u32[]{:S(2)}) collective-permute-start(bf16[640,384]{1,0:T(8,128)(2,1)S(1)} %shard_map.79), channel_id=1, source_target_pairs={{0,16},{16,32},{32,48},{48,64},{64,80},{80,96},{96,112},{112,0},{1... | collective-permute-start | bytes 1474568 | tf_op jit(solution)/shard_map/ppermute | solution.py:20
  87.7 11.9 %collective-permute-start.9 = (bf16[640,384]{1,0:T(8,128)(2,1)S(1)}, bf16[640,384]{1,0:T(8,128)(2,1)S(1)}, u32[]{:S(2)}, u32[]{:S(2)}) collective-permute-start(bf16[640,384]{1,0:T(8,128)(2,1)S(1)} %shard_map.83), channel_id=1, source_target_pairs={{0,112},{16,0},{32,16},{48,32},{64,48},{80,64},{96,80},{112,96},{1... | collective-permute-start | bytes 1474568 | tf_op jit(solution)/shard_map/ppermute | solution.py:20
  93.5 11.9 %collective-permute-start.5 = (bf16[640,384]{1,0:T(8,128)(2,1)S(1)}, bf16[640,384]{1,0:T(8,128)(2,1)S(1)}, u32[]{:S(2)}, u32[]{:S(2)}) collective-permute-start(bf16[640,384]{1,0:T(8,128)(2,1)S(1)} %shard_map.80), channel_id=1, source_target_pairs={{0,16},{16,32},{32,48},{48,64},{64,80},{80,96},{96,112},{112,0},{1... | collective-permute-start | bytes 1474568 | tf_op jit(solution)/shard_map/ppermute | solution.py:20
  95.5 3.1 %collective-permute-start.10 = (f32[6,128]{1,0:T(8,128)S(1)}, f32[6,128]{1,0:T(8,128)S(1)}, u32[]{:S(2)}, u32[]{:S(2)}) collective-permute-start(f32[6,128]{1,0:T(8,128)S(1)} %shard_map.84.gains), channel_id=1, source_target_pairs={{0,1},{1,0},{2,3},{3,2},{4,5},{5,4},{6,7},{7,6},{8,9},{9,8},{10,11... | collective-permute-start | bytes 9224 | tf_op jit(solution)/shard_map/ppermute | solution.py:20
  106.5 3.5 %collective-permute-start.11 = (bf16[640,256]{1,0:T(8,128)(2,1)S(1)}, bf16[640,256]{1,0:T(8,128)(2,1)S(1)}, u32[]{:S(2)}, u32[]{:S(2)}) collective-permute-start(bf16[640,256]{1,0:T(8,128)(2,1)S(1)} %get-tuple-element.26.refs_3_), channel_id=1, source_target_pairs={{0,1},{1,0},{2,3},{3,2},{4,5},{5,4},{6,7},{7,6},{8,9},{9,8},{10,11... | collective-permute-start | bytes 983048 | tf_op jit(solution)/shard_map/ppermute | solution.py:20

commit v5 on v4

--- a/solution.py
+++ b/solution.py
@@ -21,8 +21,7 @@
 
 
 def head_norm(values, gain):
-    scale = jnp.sqrt(jnp.mean(values * values, axis=-1, keepdims=True) + 1e-06)
-    return values / scale * gain
+    return values * lax.rsqrt(jnp.mean(values * values, axis=-1, keepdims=True) + 1e-06) * gain
 
 
 def stack_kernel(q_gain, k_gain, gains):
@@ -43,22 +42,71 @@
     )(q_gain, k_gain)
 
 
-def pack_kernel(counts, place, stale, modul, out):
-    rows, width = stale.shape
-    blks, padded, slice_width = out.shape
+def dense_kernel(stale, out, buffer):
+    depth = out.shape[2] * 3 // 4
+    piece = depth // 3
+    for blk in range(out.shape[0]):
+        block = stale[0, :, blk * depth : (blk + 1) * depth].astype(jnp.float32)
+        buffer[blk, :, :depth] = block[:8]
+        buffer[blk, 6:, depth:] = jnp.zeros((2, piece), jnp.float32)
+        for token in range(2):
+            for part in range(3):
+                at = 3 * token + part
+                buffer[blk, at : at + 1, depth:] = block[
+                    8 + token : 9 + token, part * piece : (part + 1) * piece
+                ]
+    out[...] = buffer[...].astype(out.dtype)
+
+
+def dense(stale, shape):
+    return pl.pallas_call(
+        dense_kernel,
+        out_shape=jax.ShapeDtypeStruct(shape, jnp.bfloat16),
+        in_specs=[WHOLE],
+        out_specs=WHOLE,
+        scratch_shapes=[pltpu.VMEM(shape, jnp.float32)],
+        compiler_params=LIMIT,
+        cost_estimate=pl.CostEstimate(flops=10**6, bytes_accessed=10**6, transcendentals=0),
+    )(stale)
+
+
+def norm_kernel(counts, place, stale, modul, out):
+    blks, _, lanes = stale.shape
+    depth = lanes * 3 // 4
+    piece = depth // 3
+    width = blks * depth
     source = stale[...].astype(jnp.float32)
-    spread = jnp.sqrt(jnp.mean(source * source, axis=-1, keepdims=True) + 1e-06)
-    normed = source / spread * (1.0 + modul[1:2]) + modul[0:1]
-    count = jnp.full((padded - rows, width), counts[0], jnp.int32).astype(jnp.float32)
-    normed = jnp.concatenate([normed, count], axis=0).astype(out.dtype)
+    square = jnp.sum(source * source, axis=0)
+    row = lax.broadcasted_iota(jnp.int32, (8, 1), 0)
+    first = jnp.sum(square[:, :depth], axis=-1, keepdims=True)
+    rest = jnp.sum(square[:, depth:], axis=-1, keepdims=True)
+    eighth = jnp.sum(jnp.where(row < 3, rest, 0.0), axis=0, keepdims=True)
+    ninth = jnp.sum(jnp.where((row >= 3) & (row < 6), rest, 0.0), axis=0, keepdims=True)
+    spread = jnp.sqrt(first / width + 1e-06)
+    last = jnp.sqrt(jnp.where(row < 3, eighth, ninth) / width + 1e-06)
+    part = jnp.where(row < 3, row, row - 3)
+    count = jnp.full((8, piece), counts[0], jnp.int32).astype(jnp.float32)
     for blk in range(blks):
-        out[blk] = normed[:, blk * slice_width : (blk + 1) * slice_width]
-
-
-def packed(counts, place, stale, modul, shape):
-    return pl.pallas_call(
-        pack_kernel,
-        out_shape=jax.ShapeDtypeStruct(shape, jnp.bfloat16),
+        begin = blk * depth
+        shift, scale = (modul[i : i + 1, begin : begin + depth] for i in (0, 1))
+        normed = source[blk, :, :depth] / spread * (1.0 + scale) + shift
+        out[blk, :, :depth] = normed.astype(out.dtype)
+        shift, scale = (
+            jnp.where(
+                part == 0,
+                values[:, :piece],
+                jnp.where(part == 1, values[:, piece : 2 * piece], values[:, 2 * piece :]),
+            )
+            for values in (shift, scale)
+        )
+        normed = source[blk, :, depth:] / last * (1.0 + scale) + shift
+        out[blk, :, depth:] = jnp.where(row < 6, normed, count).astype(out.dtype)
+
+
+def normed(counts, place, stale, modul):
+    return pl.pallas_call(
+        norm_kernel,
+        out_shape=jax.ShapeDtypeStruct(stale.shape, jnp.bfloat16),
         in_specs=[SMALL, SMALL, WHOLE, WHOLE],
         out_specs=WHOLE,
         compiler_params=LIMIT,
@@ -67,10 +115,20 @@
 
 
 def spread_kernel(sliced, weights, out, rows):
-    blks = sliced.shape[0]
-    count = out.shape[1] // blks
+    blks, _, lanes = sliced.shape
+    depth = lanes * 3 // 4
+    piece = depth // 3
+    tok_rows = rows.shape[0] // blks
     for blk in range(blks):
-        rows[blk * count : (blk + 1) * count] = sliced[blk, :count].astype(jnp.float32)
+        block = sliced[blk].astype(jnp.float32)
+        begin = blk * tok_rows
+        rows[begin : begin + 8] = block[:, :depth]
+        for token in range(2):
+            for part in range(3):
+                at = 3 * token + part
+                rows[begin + 8 + token : begin + 9 + token, part * piece : (part + 1) * piece] = block[
+                    at : at + 1, depth:
+                ]
     block = rows[...].astype(out.dtype)
     for chip in range(out.shape[0]):
         out[chip] = block
@@ -195,7 +253,7 @@
     )(place, first, second, third, gains, theirs)
 
 
-def attention_kernel(tok_rows, place, sliced, query, near, far, out):
+def attention_kernel(tok_rows, place, sliced, query, near, far, out, mixed):
     rows, size = query.shape
     blks = sliced.shape[0]
     chips = rows // (blks * tok_rows)
@@ -206,33 +264,28 @@
     begin = chip * (2 * tok_rows) + rest - blk * tok_rows
     limit = jnp.zeros((1, rows), jnp.float32)
     for i in range(blks):
-        count = sliced[i, tok_rows : tok_rows + 1, :1].astype(jnp.float32)
+        count = sliced[i, -2:, -1:][:1].astype(jnp.float32)
         limit = jnp.where(blk == i, count, limit)
     lanes = (place[1], 1 - place[1])
     valid = [(begin + lane * tok_rows).astype(jnp.float32) < limit for lane in lanes]
     pairs = (near, far)
-    step = 2 * blks * tok_rows
-    for part in range(rows // step):
-        block = query[part * step : (part + 1) * step]
-        scores = []
-        for pair, mask in zip(pairs, valid):
-            product = lax.dot_general(
-                block, pair[:, :size], (((1,), (1,)), ((), ())), preferred_element_type=jnp.float32
-            )
-            scores.append(jnp.where(mask, product * (size**-0.5), -1e30))
-        top = jnp.maximum(*(jnp.max(score, axis=-1, keepdims=True) for score in scores))
-        denom, mixed = 0.0, 0.0
-        for score, pair in zip(scores, pairs):
-            expo = jnp.exp(score - top)
-            denom += jnp.sum(expo, axis=-1, keepdims=True)
-            mixed += jnp.dot(
-                expo.astype(jnp.bfloat16), pair[:, size:], preferred_element_type=jnp.float32
-            )
-        mixed = mixed / denom
-        for i in range(2):
-            for j in range(blks):
-                piece = mixed[(i * blks + j) * tok_rows : (i * blks + j + 1) * tok_rows]
-                out[j * chips + 2 * part + i] = piece.astype(out.dtype)
+    scores = []
+    for pair, mask in zip(pairs, valid):
+        product = lax.dot_general(
+            query[...], pair[:, :size], (((1,), (1,)), ((), ())), preferred_element_type=jnp.float32
+        )
+        scores.append(jnp.where(mask, product * (size**-0.5), -1e30))
+    top = jnp.maximum(*(jnp.max(score, axis=-1, keepdims=True) for score in scores))
+    denom, total = 0.0, 0.0
+    for score, pair in zip(scores, pairs):
+        expo = jnp.exp(score - top)
+        denom += jnp.sum(expo, axis=-1, keepdims=True)
+        total += jnp.dot(expo.astype(jnp.bfloat16), pair[:, size:], preferred_element_type=jnp.float32)
+    mixed[...] = total / denom
+    for i in range(chips):
+        for j in range(blks):
+            begin = (i * blks + j) * tok_rows
+            out[j * chips + i] = mixed[begin : begin + tok_rows].astype(out.dtype)
 
 
 def attended(tok_rows, place, sliced, query, near, far):
@@ -242,6 +295,7 @@
         out_shape=jax.ShapeDtypeStruct((rows // tok_rows, tok_rows, size), jnp.bfloat16),
         in_specs=[SMALL] + [WHOLE] * 4,
         out_specs=WHOLE,
+        scratch_shapes=[pltpu.VMEM((rows, size), jnp.float32)],
         compiler_params=LIMIT,
         cost_estimate=pl.CostEstimate(
             flops=8 * rows * rows * size, bytes_accessed=2**20, transcendentals=2 * rows * rows
@@ -276,7 +330,7 @@
     chips = lax.axis_size("zlo") * lax.axis_size("x")
     slice_width, head_size = w_qkv.shape[1], w_qkv.shape[4]
 
-    received = shifted(stale[0], "section", 1)
+    received = shifted(dense(stale, (blks, 8, slice_width * 4 // 3)), "section", 1)
     modul = lax.dynamic_index_in_dim(mod_table, layer_of_section[0], 0, keepdims=False)
     place = jnp.stack([lax.axis_index("blk"), lax.axis_index("core")]).astype(jnp.int32)
 
@@ -285,7 +339,7 @@
     other = shifted(own, "core", 1)
     theirs = shifted(gains, "core", 1)
 
-    sent = packed(counts, place, received, modul, (blks, 16, slice_width))
+    sent = normed(counts, place, received, modul)
     sliced = lax.all_to_all(sent, "blk", 0, 0, tiled=False)
     copies = spread(sliced, other, (chips, blks * tok_rows, slice_width))
     tokens = lax.all_to_all(copies, CHIPS, 0, 0, tiled=False)

time: 138 us -> 131 us (0.949)
  blocking collectives: 62.5 us -> 57.2 us
  waiting for transfers between devices: 21.4 us -> 19.8 us
    all_to_all x1, blocking collectives: 24 us -> 21.6 us  [on_device(): returned = lax.all_to_all(mixed, ('blk',) + CHIPS, 0, 0, tiled=False)]
    all_to_all x1, blocking collectives: 21.7 us -> 19.6 us  [on_device(): tokens = lax.all_to_all(copies, CHIPS, 0, 0, tiled=False)]
    ppermute x12, waiting for transfers between devices: 21.4 us -> 19.8 us  [shifted(): return lax.ppermute(value, axis, pairs)]
where the time goes in v5:
time: 131 us
  blocking collectives  57.2 us (44%)
  starting transfers between devices  37.6 us (29%)
  waiting for transfers between devices  19.8 us (15%)
  Pallas kernels  13.4 us (10%)
  between operations  1.55 us (1%)
    ppermute x12, starting transfers between devices, shifted(): return lax.ppermute(value, axis, pairs)  37.6 us
    all_to_all x1, blocking collectives, on_device(): returned = lax.all_to_all(mixed, ('blk',) + CHIPS, 0, 0, tiled=False)  21.6 us
    ppermute x12, waiting for transfers between devices, shifted(): return lax.ppermute(value, axis, pairs)  19.8 us
    all_to_all x1, blocking collectives, on_device(): tokens = lax.all_to_all(copies, CHIPS, 0, 0, tiled=False)  19.6 us
    all_to_all x1, blocking collectives, on_device(): sliced = lax.all_to_all(sent, 'blk', 0, 0, tiled=False)  16 us
    pallas_call x3, Pallas kernels, products(): pl.pallas_call(lambda *refs: product_kernel(steps, *refs), out_shape=[sha...  8.19 us
  transfers between devices with their start and end apart: 12, of which 7 were waited for; matrix products, arithmetic and copies ran while one was open for 0% of the time, Pallas kernels for 6%

profile of v5, /device:TPU:6, one launch (start us, length us, event | category | flops | bytes accessed | tf_op | source)
XLA Modules:
  0.0 130.7 jit_solution(15612719927564506801)
XLA Ops:
  0.0 0.0 copy-start
  0.0 0.0 copy-start.2
  0.0 1.0 copy-done.2
  1.0 6.1 %collective-permute-start = (bf16[8,8,1024]{2,1,0:T(8,128)(2,1)S(1)}, bf16[8,8,1024]{2,1,0:T(8,128)(2,1)S(1)}, u32[]{:S(2)}, u32[]{:S(2)}) collective-permute-start(bf16[8,8,1024]{2,1,0:T(8,128)(2,1)S(1)} %shard_map.73), channel_id=1, source_target_pairs={{0,128},{128,256},{256,384},{384,0},{1,129},{129,257},{257,385},{3... | collective-permute-start | bytes 393224 | tf_op jit(solution)/shard_map/ppermute | solution.py:20
  7.1 1.9 %collective-permute-start.1 = (bf16[3,3,768,128]{3,2,1,0:T(8,128)(2,1)}, bf16[3,3,768,128]{3,2,1,0:T(8,128)(2,1)S(1)}, u32[]{:S(2)}, u32[]{:S(2)}) collective-permute-start(bf16[3,3,768,128]{3,2,1,0:T(8,128)(2,1)} %bitcast.18), channel_id=1, source_target_pairs={{0,1},{1,0},{2,3},{3,2},{4,5},{5,4},{6,7},{7,6},{8,9},{9,8},{10,11... | collective-permute-start | bytes 5308424 | tf_op jit(solution)/shard_map/ppermute | solution.py:20
  9.7 0.0 copy-done
  10.4 0.1 pad_add_fusion.place.refs_0_
  10.5 5.1 %collective-permute-done.stale = bf16[8,8,1024]{2,1,0:T(8,128)(2,1)S(1)} collective-permute-done((bf16[8,8,1024]{2,1,0:T(8,128)(2,1)S(1)}, bf16[8,8,1024]{2,1,0:T(8,128)(2,1)S(1)}, u32[]{:S(2)}, u32[]{:S(2)}) %collective-permute-start) | collective-permute-done | bytes 131104 | tf_op jit(solution)/shard_map/ppermute | solution.py:20
  15.6 0.7 shard_map.74
  16.3 16.0 %all_to_all.15.sliced.refs_1_ = bf16[8,8,1024]{2,1,0:T(8,128)(2,1)S(1)} all-to-all(bf16[8,8,1024]{2,1,0:T(8,128)(2,1)S(1)} %shard_map.74), channel_id=1, replica_groups=mesh['section'=4,'blk'=8,'zlo'=2,'x'=4,'core'=2] {'blk'}, dimensions={0} | all-to-all | bytes 262144 | tf_op jit(solution)/shard_map/all_to_all | solution.py:343
  32.3 0.0 copy-start.1
  32.3 0.0 collective-permute-done.1.weights.refs_3_
  32.3 0.1 shard_map.75
  32.4 19.6 %all_to_all.16 = bf16[8,80,768]{2,1,0:T(8,128)(2,1)S(1)} all-to-all(bf16[8,80,768]{2,1,0:T(8,128)(2,1)S(1)} %shard_map.75), channel_id=1, replica_groups=mesh['section'=4,'blk'=8,'zlo'=2,'x'=4,'core'=2] {'zlo','x'}, dimensions={0} | all-to-all | bytes 1966080 | tf_op jit(solution)/shard_map/all_to_all | solution.py:345
  52.0 0.0 copy-done.1
  52.0 1.4 %shard_map.78 = (bf16[320,384]{1,0:T(8,128)(2,1)S(1)}, bf16[320,384]{1,0:T(8,128)(2,1)S(1)}) custom-call(s32[2]{0:T(128)S(1)} %pad_add_fusion.place.refs_0_, bf16[640,768]{1,0:T(8,128)(2,1)S(1)} %bitcast.15, bf16[3,3,768,128]{3,2,1,0:T(8,128)(2,1)S(1)} %bitcast.19, bf16[3,3,768,128]{3,2,1,0:T(8,128)(2,1)S(1)} %collective-permute-done.1.weights.refs_3_), custom_call_target="tpu_custom_call" | custom-call | flops 377487360 | bytes 4194304 | tf_op jit(solution)/shard_map/pallas_call | solution.py:187
  53.4 2.0 %collective-permute-start.6 = (bf16[320,384]{1,0:T(8,128)(2,1)S(1)}, bf16[320,384]{1,0:T(8,128)(2,1)S(1)}, u32[]{:S(2)}, u32[]{:S(2)}) collective-permute-start(bf16[320,384]{1,0:T(8,128)(2,1)S(1)} %get-tuple-element.24), channel_id=1, source_target_pairs={{0,112},{16,0},{32,16},{48,32},{64,48},{80,64},{96,80},{112,96},{1... | collective-permute-start | bytes 737288 | tf_op jit(solution)/shard_map/ppermute | solution.py:20
  55.4 3.8 %collective-permute-start.2 = (bf16[320,384]{1,0:T(8,128)(2,1)S(1)}, bf16[320,384]{1,0:T(8,128)(2,1)S(1)}, u32[]{:S(2)}, u32[]{:S(2)}) collective-permute-start(bf16[320,384]{1,0:T(8,128)(2,1)S(1)} %get-tuple-element.20), channel_id=1, source_target_pairs={{0,16},{16,32},{32,48},{48,64},{64,80},{80,96},{96,112},{112,0},{1... | collective-permute-start | bytes 737288 | tf_op jit(solution)/shard_map/ppermute | solution.py:20
  59.3 2.2 %shard_map.77 = (bf16[640,384]{1,0:T(8,128)(2,1)S(1)}, bf16[640,384]{1,0:T(8,128)(2,1)S(1)}) custom-call(s32[2]{0:T(128)S(1)} %pad_add_fusion.place.refs_0_, bf16[640,768]{1,0:T(8,128)(2,1)S(1)} %bitcast.16, bf16[3,3,768,128]{3,2,1,0:T(8,128)(2,1)S(1)} %bitcast.20, bf16[3,3,768,128]{3,2,1,0:T(8,128)(2,1)S(1)} %collective-permute-done.1.weights.refs_3_), custom_call_target="tpu_custom_call" | custom-call | flops 754974720 | bytes 4194304 | tf_op jit(solution)/shard_map/pallas_call | solution.py:187
  61.5 0.0 collective-permute-done.6.refs_1_
  61.5 0.1 shard_map.82
  61.6 3.2 %collective-permute-start.7 = (bf16[640,384]{1,0:T(8,128)(2,1)S(1)}, bf16[640,384]{1,0:T(8,128)(2,1)S(1)}, u32[]{:S(2)}, u32[]{:S(2)}) collective-permute-start(bf16[640,384]{1,0:T(8,128)(2,1)S(1)} %shard_map.82), channel_id=1, source_target_pairs={{0,112},{16,0},{32,16},{48,32},{64,48},{80,64},{96,80},{112,96},{1... | collective-permute-start | bytes 1474568 | tf_op jit(solution)/shard_map/ppermute | solution.py:20
  64.8 0.0 collective-permute-done.2.refs_1_
  64.8 0.1 shard_map.79
  64.9 2.6 %collective-permute-start.3 = (bf16[640,384]{1,0:T(8,128)(2,1)S(1)}, bf16[640,384]{1,0:T(8,128)(2,1)S(1)}, u32[]{:S(2)}, u32[]{:S(2)}) collective-permute-start(bf16[640,384]{1,0:T(8,128)(2,1)S(1)} %shard_map.79), channel_id=1, source_target_pairs={{0,16},{16,32},{32,48},{48,64},{64,80},{80,96},{96,112},{112,0},{1... | collective-permute-start | bytes 1474568 | tf_op jit(solution)/shard_map/ppermute | solution.py:20
  67.5 4.6 %shard_map.76 = (bf16[640,384]{1,0:T(8,128)(2,1)S(1)}, bf16[640,384]{1,0:T(8,128)(2,1)S(1)}, bf16[640,384]{1,0:T(8,128)(2,1)S(1)}, bf16[640,384]{1,0:T(8,128)(2,1)S(1)}, bf16[640,384]{1,0:T(8,128)(2,1)S(1)}) custom-call(s32[2]{0:T(128)S(1)} %pad_add_fusion.place.refs_0_, bf16[640,768]{1,0:T(8,128)(2,1)S(1)} %bitcast.17, ...), custom_call_target="tpu_custom_call" | custom-call | flops 1887436800 | bytes 4194304 | tf_op jit(solution)/shard_map/pallas_call | solution.py:187
  72.2 0.7 collective-permute-done.7.refs_1_
  72.9 0.1 shard_map.83
  73.0 4.7 %collective-permute-start.8 = (bf16[640,384]{1,0:T(8,128)(2,1)S(1)}, bf16[640,384]{1,0:T(8,128)(2,1)S(1)}, u32[]{:S(2)}, u32[]{:S(2)}) collective-permute-start(bf16[640,384]{1,0:T(8,128)(2,1)S(1)} %shard_map.83), channel_id=1, source_target_pairs={{0,112},{16,0},{32,16},{48,32},{64,48},{80,64},{96,80},{112,96},{1... | collective-permute-start | bytes 1474568 | tf_op jit(solution)/shard_map/ppermute | solution.py:20
  77.7 0.0 collective-permute-done.3.refs_1_
  77.7 0.1 shard_map.80
  77.8 0.0 copy-start.3
  77.8 0.0 copy-start.4
  77.8 1.9 %collective-permute-start.4 = (bf16[640,384]{1,0:T(8,128)(2,1)S(1)}, bf16[640,384]{1,0:T(8,128)(2,1)S(1)}, u32[]{:S(2)}, u32[]{:S(2)}) collective-permute-start(bf16[640,384]{1,0:T(8,128)(2,1)S(1)} %shard_map.80), channel_id=1, source_target_pairs={{0,16},{16,32},{32,48},{48,64},{64,80},{80,96},{96,112},{112,0},{1... | collective-permute-start | bytes 1474568 | tf_op jit(solution)/shard_map/ppermute | solution.py:20
  79.8 4.2 %collective-permute-done.8.refs_1_ = bf16[640,384]{1,0:T(8,128)(2,1)S(1)} collective-permute-done((bf16[640,384]{1,0:T(8,128)(2,1)S(1)}, bf16[640,384]{1,0:T(8,128)(2,1)S(1)}, u32[]{:S(2)}, u32[]{:S(2)}) %collective-permute-start.8) | collective-permute-done | bytes 491552 | tf_op jit(solution)/shard_map/ppermute | solution.py:20
  84.0 0.1 shard_map.84
  84.1 5.6 %collective-permute-start.9 = (bf16[640,384]{1,0:T(8,128)(2,1)S(1)}, bf16[640,384]{1,0:T(8,128)(2,1)S(1)}, u32[]{:S(2)}, u32[]{:S(2)}) collective-permute-start(bf16[640,384]{1,0:T(8,128)(2,1)S(1)} %shard_map.84), channel_id=1, source_target_pairs={{0,112},{16,0},{32,16},{48,32},{64,48},{80,64},{96,80},{112,96},{1... | collective-permute-start | bytes 1474568 | tf_op jit(solution)/shard_map/ppermute | solution.py:20
  89.7 0.0 collective-permute-done.4.refs_1_
  89.8 0.1 shard_map.81
  89.9 1.9 %collective-permute-start.5 = (bf16[640,384]{1,0:T(8,128)(2,1)S(1)}, bf16[640,384]{1,0:T(8,128)(2,1)S(1)}, u32[]{:S(2)}, u32[]{:S(2)}) collective-permute-start(bf16[640,384]{1,0:T(8,128)(2,1)S(1)} %shard_map.81), channel_id=1, source_target_pairs={{0,16},{16,32},{32,48},{48,64},{64,80},{80,96},{96,112},{112,0},{1... | collective-permute-start | bytes 1474568 | tf_op jit(solution)/shard_map/ppermute | solution.py:20
  91.8 0.0 copy-done.3
  91.8 0.0 copy-done.4
  91.8 1.9 %collective-permute-start.10 = (f32[6,128]{1,0:T(8,128)S(1)}, f32[6,128]{1,0:T(8,128)S(1)}, u32[]{:S(2)}, u32[]{:S(2)}) collective-permute-start(f32[6,128]{1,0:T(8,128)S(1)} %shard_map.85.gains), channel_id=1, source_target_pairs={{0,1},{1,0},{2,3},{3,2},{4,5},{5,4},{6,7},{7,6},{8,9},{9,8},{10,11... | collective-permute-start | bytes 9224 | tf_op jit(solution)/shard_map/ppermute | solution.py:20
  93.8 1.1 collective-permute-done.10.theirs
  94.9 1.1 collective-permute-done.9.third
  96.1 5.8 %collective-permute-done.5.second = bf16[640,384]{1,0:T(8,128)(2,1)S(1)} collective-permute-done((bf16[640,384]{1,0:T(8,128)(2,1)S(1)}, bf16[640,384]{1,0:T(8,128)(2,1)S(1)}, u32[]{:S(2)}, u32[]{:S(2)}) %collective-permute-start.5) | collective-permute-done | bytes 491552 | tf_op jit(solution)/shard_map/ppermute | solution.py:20
  101.8 0.9 shard_map.86
  102.8 1.9 %collective-permute-start.11 = (bf16[640,256]{1,0:T(8,128)(2,1)S(1)}, bf16[640,256]{1,0:T(8,128)(2,1)S(1)}, u32[]{:S(2)}, u32[]{:S(2)}) collective-permute-start(bf16[640,256]{1,0:T(8,128)(2,1)S(1)} %get-tuple-element.26.refs_3_), channel_id=1, source_target_pairs={{0,1},{1,0},{2,3},{3,2},{4,5},{5,4},{6,7},{7,6},{8,9},{9,8},{10,11... | collective-permute-start | bytes 983048 | tf_op jit(solution)/shard_map/ppermute | solution.py:20
  104.7 1.6 %collective-permute-done.11.refs_4_ = bf16[640,256]{1,0:T(8,128)(2,1)S(1)} collective-permute-done((bf16[640,256]{1,0:T(8,128)(2,1)S(1)}, bf16[640,256]{1,0:T(8,128)(2,1)S(1)}, u32[]{:S(2)}, u32[]{:S(2)}) %collective-permute-start.11) | collective-permute-done | bytes 327712 | tf_op jit(solution)/shard_map/ppermute | solution.py:20
  106.3 2.1 %shard_map.87 = bf16[64,10,128]{2,1,0:T(8,128)(2,1)S(1)} custom-call(s32[2]{0:T(128)S(1)} %pad_add_fusion.place.refs_0_, bf16[8,8,1024]{2,1,0:T(8,128)(2,1)S(1)} %all_to_all.15.sliced.refs_1_, bf16[640,128]{1,0:T(8,128)(2,1)S(1)} %get-tuple-element.25.refs_2_, bf16[640,256]{1,0:T(8,128)(2,1)S(1)} %get-tuple-element.26.refs_3_, ...), custom_call_target="tpu_custom_call" | custom-call | flops 419430400 | bytes 1048576 | tf_op jit(solution)/shard_map/pallas_call | solution.py:293
  108.4 21.6 %all_to_all.17 = bf16[64,10,128]{2,1,0:T(8,128)(2,1)S(1)} all-to-all(bf16[64,10,128]{2,1,0:T(8,128)(2,1)S(1)} %shard_map.87), channel_id=1, replica_groups=mesh['section'=4,'blk'=8,'zlo'=2,'x'=4,'core'=2] {'blk','zlo','x'}, dimensions={0} | all-to-all | bytes 327680 | tf_op jit(solution)/shard_map/all_to_all | solution.py:360
  130.0 0.7 shard_map.88
  (3 shorter events, 0.1 us)
Async XLA Ops:
  0.0 9.7 %copy-start = (f32[16,2,6144]{2,1,0:T(2,128)S(1)}, f32[16,2,6144]{2,1,0:T(2,128)}, u32[]{:S(2)}) copy-start(f32[16,2,6144]{2,1,0:T(2,128)} %param.9) | copy-start | bytes 2359300
  0.0 1.0 copy-start.2
  1.0 14.6 %collective-permute-start = (bf16[8,8,1024]{2,1,0:T(8,128)(2,1)S(1)}, bf16[8,8,1024]{2,1,0:T(8,128)(2,1)S(1)}, u32[]{:S(2)}, u32[]{:S(2)}) collective-permute-start(bf16[8,8,1024]{2,1,0:T(8,128)(2,1)S(1)} %shard_map.73), channel_id=1, source_target_pairs={{0,128},{128,256},{256,384},{384,0},{1,129},{129,257},{257,385},{3... | collective-permute-start | bytes 393224 | tf_op jit(solution)/shard_map/ppermute | solution.py:20
  7.1 25.1 %collective-permute-start.1 = (bf16[3,3,768,128]{3,2,1,0:T(8,128)(2,1)}, bf16[3,3,768,128]{3,2,1,0:T(8,128)(2,1)S(1)}, u32[]{:S(2)}, u32[]{:S(2)}) collective-permute-start(bf16[3,3,768,128]{3,2,1,0:T(8,128)(2,1)} %bitcast.18), channel_id=1, source_target_pairs={{0,1},{1,0},{2,3},{3,2},{4,5},{5,4},{6,7},{7,6},{8,9},{9,8},{10,11... | collective-permute-start | bytes 5308424 | tf_op jit(solution)/shard_map/ppermute | solution.py:20
  32.3 19.8 %copy-start.1 = (bf16[1,768,3,3,128]{4,1,3,2,0:T(8,128)(2,1)S(1)}, bf16[1,768,3,3,128]{4,1,3,2,0:T(8,128)(2,1)}, u32[]{:S(2)}) copy-start(bf16[1,768,3,3,128]{4,1,3,2,0:T(8,128)(2,1)} %param.10) | copy-start | bytes 5308420
  53.4 8.1 %collective-permute-start.6 = (bf16[320,384]{1,0:T(8,128)(2,1)S(1)}, bf16[320,384]{1,0:T(8,128)(2,1)S(1)}, u32[]{:S(2)}, u32[]{:S(2)}) collective-permute-start(bf16[320,384]{1,0:T(8,128)(2,1)S(1)} %get-tuple-element.24), channel_id=1, source_target_pairs={{0,112},{16,0},{32,16},{48,32},{64,48},{80,64},{96,80},{112,96},{1... | collective-permute-start | bytes 737288 | tf_op jit(solution)/shard_map/ppermute | solution.py:20
  55.4 9.4 %collective-permute-start.2 = (bf16[320,384]{1,0:T(8,128)(2,1)S(1)}, bf16[320,384]{1,0:T(8,128)(2,1)S(1)}, u32[]{:S(2)}, u32[]{:S(2)}) collective-permute-start(bf16[320,384]{1,0:T(8,128)(2,1)S(1)} %get-tuple-element.20), channel_id=1, source_target_pairs={{0,16},{16,32},{32,48},{48,64},{64,80},{80,96},{96,112},{112,0},{1... | collective-permute-start | bytes 737288 | tf_op jit(solution)/shard_map/ppermute | solution.py:20
  61.6 11.3 %collective-permute-start.7 = (bf16[640,384]{1,0:T(8,128)(2,1)S(1)}, bf16[640,384]{1,0:T(8,128)(2,1)S(1)}, u32[]{:S(2)}, u32[]{:S(2)}) collective-permute-start(bf16[640,384]{1,0:T(8,128)(2,1)S(1)} %shard_map.82), channel_id=1, source_target_pairs={{0,112},{16,0},{32,16},{48,32},{64,48},{80,64},{96,80},{112,96},{1... | collective-permute-start | bytes 1474568 | tf_op jit(solution)/shard_map/ppermute | solution.py:20
  64.9 12.8 %collective-permute-start.3 = (bf16[640,384]{1,0:T(8,128)(2,1)S(1)}, bf16[640,384]{1,0:T(8,128)(2,1)S(1)}, u32[]{:S(2)}, u32[]{:S(2)}) collective-permute-start(bf16[640,384]{1,0:T(8,128)(2,1)S(1)} %shard_map.79), channel_id=1, source_target_pairs={{0,16},{16,32},{32,48},{48,64},{64,80},{80,96},{96,112},{112,0},{1... | collective-permute-start | bytes 1474568 | tf_op jit(solution)/shard_map/ppermute | solution.py:20
  73.0 11.0 %collective-permute-start.8 = (bf16[640,384]{1,0:T(8,128)(2,1)S(1)}, bf16[640,384]{1,0:T(8,128)(2,1)S(1)}, u32[]{:S(2)}, u32[]{:S(2)}) collective-permute-start(bf16[640,384]{1,0:T(8,128)(2,1)S(1)} %shard_map.83), channel_id=1, source_target_pairs={{0,112},{16,0},{32,16},{48,32},{64,48},{80,64},{96,80},{112,96},{1... | collective-permute-start | bytes 1474568 | tf_op jit(solution)/shard_map/ppermute | solution.py:20
  77.8 14.0 %copy-start.3 = (f32[1,3,128]{2,0,1:T(1,128)S(1)}, f32[1,3,128]{2,0,1:T(1,128)}, u32[]{:S(2)}) copy-start(f32[1,3,128]{2,0,1:T(1,128)} %param.11) | copy-start | bytes 4612
  77.8 14.0 %copy-start.4 = (f32[1,3,128]{2,0,1:T(1,128)S(1)}, f32[1,3,128]{2,0,1:T(1,128)}, u32[]{:S(2)}) copy-start(f32[1,3,128]{2,0,1:T(1,128)} %param.12) | copy-start | bytes 4612
  77.8 11.9 %collective-permute-start.4 = (bf16[640,384]{1,0:T(8,128)(2,1)S(1)}, bf16[640,384]{1,0:T(8,128)(2,1)S(1)}, u32[]{:S(2)}, u32[]{:S(2)}) collective-permute-start(bf16[640,384]{1,0:T(8,128)(2,1)S(1)} %shard_map.80), channel_id=1, source_target_pairs={{0,16},{16,32},{32,48},{48,64},{64,80},{80,96},{96,112},{112,0},{1... | collective-permute-start | bytes 1474568 | tf_op jit(solution)/shard_map/ppermute | solution.py:20
  84.1 11.9 %collective-permute-start.9 = (bf16[640,384]{1,0:T(8,128)(2,1)S(1)}, bf16[640,384]{1,0:T(8,128)(2,1)S(1)}, u32[]{:S(2)}, u32[]{:S(2)}) collective-permute-start(bf16[640,384]{1,0:T(8,128)(2,1)S(1)} %shard_map.84), channel_id=1, source_target_pairs={{0,112},{16,0},{32,16},{48,32},{64,48},{80,64},{96,80},{112,96},{1... | collective-permute-start | bytes 1474568 | tf_op jit(solution)/shard_map/ppermute | solution.py:20
  89.9 11.9 %collective-permute-start.5 = (bf16[640,384]{1,0:T(8,128)(2,1)S(1)}, bf16[640,384]{1,0:T(8,128)(2,1)S(1)}, u32[]{:S(2)}, u32[]{:S(2)}) collective-permute-start(bf16[640,384]{1,0:T(8,128)(2,1)S(1)} %shard_map.81), channel_id=1, source_target_pairs={{0,16},{16,32},{32,48},{48,64},{64,80},{80,96},{96,112},{112,0},{1... | collective-permute-start | bytes 1474568 | tf_op jit(solution)/shard_map/ppermute | solution.py:20
  91.8 3.1 %collective-permute-start.10 = (f32[6,128]{1,0:T(8,128)S(1)}, f32[6,128]{1,0:T(8,128)S(1)}, u32[]{:S(2)}, u32[]{:S(2)}) collective-permute-start(f32[6,128]{1,0:T(8,128)S(1)} %shard_map.85.gains), channel_id=1, source_target_pairs={{0,1},{1,0},{2,3},{3,2},{4,5},{5,4},{6,7},{7,6},{8,9},{9,8},{10,11... | collective-permute-start | bytes 9224 | tf_op jit(solution)/shard_map/ppermute | solution.py:20
  102.8 3.5 %collective-permute-start.11 = (bf16[640,256]{1,0:T(8,128)(2,1)S(1)}, bf16[640,256]{1,0:T(8,128)(2,1)S(1)}, u32[]{:S(2)}, u32[]{:S(2)}) collective-permute-start(bf16[640,256]{1,0:T(8,128)(2,1)S(1)} %get-tuple-element.26.refs_3_), channel_id=1, source_target_pairs={{0,1},{1,0},{2,3},{3,2},{4,5},{5,4},{6,7},{7,6},{8,9},{9,8},{10,11... | collective-permute-start | bytes 983048 | tf_op jit(solution)/shard_map/ppermute | solution.py:20

commit v6 on v5

--- a/solution.py
+++ b/solution.py
@@ -18,6 +18,12 @@
     count = lax.axis_size(axis)
     pairs = [(source, (source + steps) % count) for source in range(count)]
     return lax.ppermute(value, axis, pairs)
+
+
+def passed(value, steps, ahead, owners):
+    blks = lax.axis_size("blk")
+    pairs = [(row, (row + steps) % blks) for row in range(blks) if (row + steps * ahead) % blks < owners]
+    return lax.ppermute(value, "blk", pairs)
 
 
 def head_norm(values, gain):
@@ -346,13 +352,14 @@
     tokens = tokens.reshape(chips * blks * tok_rows, slice_width)
     half = tokens.shape[0] // 2
 
+    owners = 2 * own.shape[0]
     up, down = products((4,), place, tokens, own, other, 2)
-    up, down = shifted(up, "blk", 1), shifted(down, "blk", -1)
+    up, down = passed(up, 1, 4, owners), passed(down, -1, 4, owners)
     three, five = products((3, 5), place, tokens, own, other)
-    up, down = shifted(added(three, up), "blk", 1), shifted(added(five, down, half), "blk", -1)
+    up, down = passed(added(three, up), 1, 3, owners), passed(added(five, down, half), -1, 3, owners)
     two, six, one, seven, zero = products((2, 6, 1, 7, 0), place, tokens, own, other)
-    up, down = shifted(added(two, up), "blk", 1), shifted(added(six, down), "blk", -1)
-    up, down = shifted(added(one, up), "blk", 1), shifted(added(seven, down), "blk", -1)
+    up, down = passed(added(two, up), 1, 2, owners), passed(added(six, down), -1, 2, owners)
+    up, down = passed(added(one, up), 1, 1, owners), passed(added(seven, down), -1, 1, owners)
     query, near = headed(place, zero, up, down, gains, theirs)
     far = shifted(near, "core", 1)
 

time: 131 us -> 130 us (level)
  starting transfers between devices: 37.6 us -> 29.3 us
  waiting for transfers between devices: 19.8 us -> 27.8 us
    ppermute x12 -> x4, starting transfers between devices: 37.6 us -> 11.9 us  [shifted(): return lax.ppermute(value, axis, pairs)]
    ppermute x0 -> x8, waiting for transfers between devices: none -> 20 us  [passed(): return lax.ppermute(value, 'blk', pairs)]
    ppermute x0 -> x8, starting transfers between devices: none -> 17.4 us  [passed(): return lax.ppermute(value, 'blk', pairs)]
    ppermute x12 -> x4, waiting for transfers between devices: 19.8 us -> 7.85 us  [shifted(): return lax.ppermute(value, axis, pairs)]
  transfers between devices with their start and end apart: 12 -> 12, of which waited for: 7 -> 6; matrix products, arithmetic and copies ran while one was open for 0% -> 0% of each run, Pallas kernels for 6% -> 6%
where the time goes in v6:
time: 130 us
  blocking collectives  56.5 us (43%)
  starting transfers between devices  29.3 us (23%)
  waiting for transfers between devices  27.8 us (21%)
  Pallas kernels  13.4 us (10%)
  between operations  1.56 us (1%)
    all_to_all x1, blocking collectives, on_device(): returned = lax.all_to_all(mixed, ('blk',) + CHIPS, 0, 0, tiled=False)  20.9 us
    ppermute x8, waiting for transfers between devices, passed(): return lax.ppermute(value, 'blk', pairs)  20 us
    all_to_all x1, blocking collectives, on_device(): tokens = lax.all_to_all(copies, CHIPS, 0, 0, tiled=False)  19.6 us
    ppermute x8, starting transfers between devices, passed(): return lax.ppermute(value, 'blk', pairs)  17.4 us
    all_to_all x1, blocking collectives, on_device(): sliced = lax.all_to_all(sent, 'blk', 0, 0, tiled=False)  16 us
    ppermute x4, starting transfers between devices, shifted(): return lax.ppermute(value, axis, pairs)  11.9 us
    pallas_call x3, Pallas kernels, products(): pl.pallas_call(lambda *refs: product_kernel(steps, *refs), out_shape=[sha...  8.18 us
    ppermute x4, waiting for transfers between devices, shifted(): return lax.ppermute(value, axis, pairs)  7.85 us
  transfers between devices with their start and end apart: 12, of which 6 were waited for; matrix products, arithmetic and copies ran while one was open for 0% of the time, Pallas kernels for 6%

profile of v6, /device:TPU:6, one launch (start us, length us, event | category | flops | bytes accessed | tf_op | source)
XLA Modules:
  0.0 129.7 jit_solution(17888306753694852370)
XLA Ops:
  0.0 0.0 copy-start
  0.0 0.0 copy-start.2
  0.0 1.0 copy-done.2
  1.0 6.1 %collective-permute-start = (bf16[8,8,1024]{2,1,0:T(8,128)(2,1)S(1)}, bf16[8,8,1024]{2,1,0:T(8,128)(2,1)S(1)}, u32[]{:S(2)}, u32[]{:S(2)}) collective-permute-start(bf16[8,8,1024]{2,1,0:T(8,128)(2,1)S(1)} %shard_map.73), channel_id=1, source_target_pairs={{0,128},{128,256},{256,384},{384,0},{1,129},{129,257},{257,385},{3... | collective-permute-start | bytes 393224 | tf_op jit(solution)/shard_map/ppermute | solution.py:20
  7.1 1.9 %collective-permute-start.1 = (bf16[3,3,768,128]{3,2,1,0:T(8,128)(2,1)}, bf16[3,3,768,128]{3,2,1,0:T(8,128)(2,1)S(1)}, u32[]{:S(2)}, u32[]{:S(2)}) collective-permute-start(bf16[3,3,768,128]{3,2,1,0:T(8,128)(2,1)} %bitcast.18), channel_id=1, source_target_pairs={{0,1},{1,0},{2,3},{3,2},{4,5},{5,4},{6,7},{7,6},{8,9},{9,8},{10,11... | collective-permute-start | bytes 5308424 | tf_op jit(solution)/shard_map/ppermute | solution.py:20
  9.7 0.0 copy-done
  10.4 0.1 pad_add_fusion.place.refs_0_
  10.5 5.1 %collective-permute-done.stale = bf16[8,8,1024]{2,1,0:T(8,128)(2,1)S(1)} collective-permute-done((bf16[8,8,1024]{2,1,0:T(8,128)(2,1)S(1)}, bf16[8,8,1024]{2,1,0:T(8,128)(2,1)S(1)}, u32[]{:S(2)}, u32[]{:S(2)}) %collective-permute-start) | collective-permute-done | bytes 131104 | tf_op jit(solution)/shard_map/ppermute | solution.py:20
  15.6 0.7 shard_map.74
  16.3 16.0 %all_to_all.15.sliced.refs_1_ = bf16[8,8,1024]{2,1,0:T(8,128)(2,1)S(1)} all-to-all(bf16[8,8,1024]{2,1,0:T(8,128)(2,1)S(1)} %shard_map.74), channel_id=1, replica_groups=mesh['section'=4,'blk'=8,'zlo'=2,'x'=4,'core'=2] {'blk'}, dimensions={0} | all-to-all | bytes 262144 | tf_op jit(solution)/shard_map/all_to_all | solution.py:349
  32.3 0.0 copy-start.1
  32.3 0.0 collective-permute-done.1.weights.refs_3_
  32.3 0.1 shard_map.75
  32.4 19.6 %all_to_all.16 = bf16[8,80,768]{2,1,0:T(8,128)(2,1)S(1)} all-to-all(bf16[8,80,768]{2,1,0:T(8,128)(2,1)S(1)} %shard_map.75), channel_id=1, replica_groups=mesh['section'=4,'blk'=8,'zlo'=2,'x'=4,'core'=2] {'zlo','x'}, dimensions={0} | all-to-all | bytes 1966080 | tf_op jit(solution)/shard_map/all_to_all | solution.py:351
  52.0 0.0 copy-done.1
  52.0 1.4 %shard_map.78 = (bf16[320,384]{1,0:T(8,128)(2,1)S(1)}, bf16[320,384]{1,0:T(8,128)(2,1)S(1)}) custom-call(s32[2]{0:T(128)S(1)} %pad_add_fusion.place.refs_0_, bf16[640,768]{1,0:T(8,128)(2,1)S(1)} %bitcast.15, bf16[3,3,768,128]{3,2,1,0:T(8,128)(2,1)S(1)} %bitcast.19, bf16[3,3,768,128]{3,2,1,0:T(8,128)(2,1)S(1)} %collective-permute-done.1.weights.refs_3_), custom_call_target="tpu_custom_call" | custom-call | flops 377487360 | bytes 4194304 | tf_op jit(solution)/shard_map/pallas_call | solution.py:193
  53.4 2.0 %collective-permute-start.6 = (bf16[320,384]{1,0:T(8,128)(2,1)S(1)}, bf16[320,384]{1,0:T(8,128)(2,1)S(1)}, u32[]{:S(2)}, u32[]{:S(2)}) collective-permute-start(bf16[320,384]{1,0:T(8,128)(2,1)S(1)} %get-tuple-element.24), channel_id=1, source_target_pairs={{0,112},{16,0},{64,48},{80,64},{96,80},{112,96},{1,113},{17,1},{65... | collective-permute-start | bytes 737288 | tf_op jit(solution)/shard_map/ppermute | solution.py:26
  55.4 3.8 %collective-permute-start.2 = (bf16[320,384]{1,0:T(8,128)(2,1)S(1)}, bf16[320,384]{1,0:T(8,128)(2,1)S(1)}, u32[]{:S(2)}, u32[]{:S(2)}) collective-permute-start(bf16[320,384]{1,0:T(8,128)(2,1)S(1)} %get-tuple-element.20), channel_id=1, source_target_pairs={{0,16},{16,32},{64,80},{80,96},{96,112},{112,0},{1,17},{17,33},{65... | collective-permute-start | bytes 737288 | tf_op jit(solution)/shard_map/ppermute | solution.py:26
  59.3 2.2 %shard_map.77 = (bf16[640,384]{1,0:T(8,128)(2,1)S(1)}, bf16[640,384]{1,0:T(8,128)(2,1)S(1)}) custom-call(s32[2]{0:T(128)S(1)} %pad_add_fusion.place.refs_0_, bf16[640,768]{1,0:T(8,128)(2,1)S(1)} %bitcast.16, bf16[3,3,768,128]{3,2,1,0:T(8,128)(2,1)S(1)} %bitcast.20, bf16[3,3,768,128]{3,2,1,0:T(8,128)(2,1)S(1)} %collective-permute-done.1.weights.refs_3_), custom_call_target="tpu_custom_call" | custom-call | flops 754974720 | bytes 4194304 | tf_op jit(solution)/shard_map/pallas_call | solution.py:193
  61.5 0.0 collective-permute-done.6.refs_1_
  61.5 0.1 shard_map.82
  61.6 3.2 %collective-permute-start.7 = (bf16[640,384]{1,0:T(8,128)(2,1)S(1)}, bf16[640,384]{1,0:T(8,128)(2,1)S(1)}, u32[]{:S(2)}, u32[]{:S(2)}) collective-permute-start(bf16[640,384]{1,0:T(8,128)(2,1)S(1)} %shard_map.82), channel_id=1, source_target_pairs={{0,112},{48,32},{64,48},{80,64},{96,80},{112,96},{1,113},{49,33},{... | collective-permute-start | bytes 1474568 | tf_op jit(solution)/shard_map/ppermute | solution.py:26
  64.8 0.0 collective-permute-done.2.refs_1_
  64.9 0.1 shard_map.79
  64.9 2.5 %collective-permute-start.3 = (bf16[640,384]{1,0:T(8,128)(2,1)S(1)}, bf16[640,384]{1,0:T(8,128)(2,1)S(1)}, u32[]{:S(2)}, u32[]{:S(2)}) collective-permute-start(bf16[640,384]{1,0:T(8,128)(2,1)S(1)} %shard_map.79), channel_id=1, source_target_pairs={{0,16},{16,32},{32,48},{80,96},{96,112},{112,0},{1,17},{17,33},{33... | collective-permute-start | bytes 1474568 | tf_op jit(solution)/shard_map/ppermute | solution.py:26
  67.4 4.6 %shard_map.76 = (bf16[640,384]{1,0:T(8,128)(2,1)S(1)}, bf16[640,384]{1,0:T(8,128)(2,1)S(1)}, bf16[640,384]{1,0:T(8,128)(2,1)S(1)}, bf16[640,384]{1,0:T(8,128)(2,1)S(1)}, bf16[640,384]{1,0:T(8,128)(2,1)S(1)}) custom-call(s32[2]{0:T(128)S(1)} %pad_add_fusion.place.refs_0_, bf16[640,768]{1,0:T(8,128)(2,1)S(1)} %bitcast.17, ...), custom_call_target="tpu_custom_call" | custom-call | flops 1887436800 | bytes 4194304 | tf_op jit(solution)/shard_map/pallas_call | solution.py:193
  72.1 0.0 collective-permute-done.7.refs_1_
  72.1 0.1 shard_map.83
  72.2 0.7 collective-permute-start.8
  72.9 4.5 %collective-permute-done.3.refs_1_ = bf16[640,384]{1,0:T(8,128)(2,1)S(1)} collective-permute-done((bf16[640,384]{1,0:T(8,128)(2,1)S(1)}, bf16[640,384]{1,0:T(8,128)(2,1)S(1)}, u32[]{:S(2)}, u32[]{:S(2)}) %collective-permute-start.3) | collective-permute-done | bytes 491552 | tf_op jit(solution)/shard_map/ppermute | solution.py:26
  77.4 0.1 shard_map.80
  77.5 0.0 copy-start.3
  77.5 0.0 copy-start.4
  77.5 1.9 %collective-permute-start.4 = (bf16[640,384]{1,0:T(8,128)(2,1)S(1)}, bf16[640,384]{1,0:T(8,128)(2,1)S(1)}, u32[]{:S(2)}, u32[]{:S(2)}) collective-permute-start(bf16[640,384]{1,0:T(8,128)(2,1)S(1)} %shard_map.80), channel_id=1, source_target_pairs={{0,16},{16,32},{32,48},{48,64},{96,112},{112,0},{1,17},{17,33},{33... | collective-permute-start | bytes 1474568 | tf_op jit(solution)/shard_map/ppermute | solution.py:26
  79.5 0.0 collective-permute-done.8.refs_1_
  79.5 0.1 shard_map.84
  79.6 1.3 collective-permute-start.9
  80.9 8.6 %collective-permute-done.4.refs_1_ = bf16[640,384]{1,0:T(8,128)(2,1)S(1)} collective-permute-done((bf16[640,384]{1,0:T(8,128)(2,1)S(1)}, bf16[640,384]{1,0:T(8,128)(2,1)S(1)}, u32[]{:S(2)}, u32[]{:S(2)}) %collective-permute-start.4) | collective-permute-done | bytes 491552 | tf_op jit(solution)/shard_map/ppermute | solution.py:26
  89.5 0.1 shard_map.81
  89.6 1.9 %collective-permute-start.5 = (bf16[640,384]{1,0:T(8,128)(2,1)S(1)}, bf16[640,384]{1,0:T(8,128)(2,1)S(1)}, u32[]{:S(2)}, u32[]{:S(2)}) collective-permute-start(bf16[640,384]{1,0:T(8,128)(2,1)S(1)} %shard_map.81), channel_id=1, source_target_pairs={{0,16},{16,32},{32,48},{48,64},{64,80},{112,0},{1,17},{17,33},{33,... | collective-permute-start | bytes 1474568 | tf_op jit(solution)/shard_map/ppermute | solution.py:26
  91.5 0.0 copy-done.3
  91.5 0.0 copy-done.4
  91.5 1.9 %collective-permute-start.10 = (f32[6,128]{1,0:T(8,128)S(1)}, f32[6,128]{1,0:T(8,128)S(1)}, u32[]{:S(2)}, u32[]{:S(2)}) collective-permute-start(f32[6,128]{1,0:T(8,128)S(1)} %shard_map.85.gains), channel_id=1, source_target_pairs={{0,1},{1,0},{2,3},{3,2},{4,5},{5,4},{6,7},{7,6},{8,9},{9,8},{10,11... | collective-permute-start | bytes 9224 | tf_op jit(solution)/shard_map/ppermute | solution.py:20
  93.5 1.1 collective-permute-done.10.theirs
  94.6 0.0 collective-permute-done.9.third
  94.6 6.9 %collective-permute-done.5.second = bf16[640,384]{1,0:T(8,128)(2,1)S(1)} collective-permute-done((bf16[640,384]{1,0:T(8,128)(2,1)S(1)}, bf16[640,384]{1,0:T(8,128)(2,1)S(1)}, u32[]{:S(2)}, u32[]{:S(2)}) %collective-permute-start.5) | collective-permute-done | bytes 491552 | tf_op jit(solution)/shard_map/ppermute | solution.py:26
  101.5 0.9 shard_map.86
  102.5 1.9 %collective-permute-start.11 = (bf16[640,256]{1,0:T(8,128)(2,1)S(1)}, bf16[640,256]{1,0:T(8,128)(2,1)S(1)}, u32[]{:S(2)}, u32[]{:S(2)}) collective-permute-start(bf16[640,256]{1,0:T(8,128)(2,1)S(1)} %get-tuple-element.26.refs_3_), channel_id=1, source_target_pairs={{0,1},{1,0},{2,3},{3,2},{4,5},{5,4},{6,7},{7,6},{8,9},{9,8},{10,11... | collective-permute-start | bytes 983048 | tf_op jit(solution)/shard_map/ppermute | solution.py:20
  104.4 1.6 %collective-permute-done.11.refs_4_ = bf16[640,256]{1,0:T(8,128)(2,1)S(1)} collective-permute-done((bf16[640,256]{1,0:T(8,128)(2,1)S(1)}, bf16[640,256]{1,0:T(8,128)(2,1)S(1)}, u32[]{:S(2)}, u32[]{:S(2)}) %collective-permute-start.11) | collective-permute-done | bytes 327712 | tf_op jit(solution)/shard_map/ppermute | solution.py:20
  106.0 2.1 %shard_map.87 = bf16[64,10,128]{2,1,0:T(8,128)(2,1)S(1)} custom-call(s32[2]{0:T(128)S(1)} %pad_add_fusion.place.refs_0_, bf16[8,8,1024]{2,1,0:T(8,128)(2,1)S(1)} %all_to_all.15.sliced.refs_1_, bf16[640,128]{1,0:T(8,128)(2,1)S(1)} %get-tuple-element.25.refs_2_, bf16[640,256]{1,0:T(8,128)(2,1)S(1)} %get-tuple-element.26.refs_3_, ...), custom_call_target="tpu_custom_call" | custom-call | flops 419430400 | bytes 1048576 | tf_op jit(solution)/shard_map/pallas_call | solution.py:299
  108.1 20.9 %all_to_all.17 = bf16[64,10,128]{2,1,0:T(8,128)(2,1)S(1)} all-to-all(bf16[64,10,128]{2,1,0:T(8,128)(2,1)S(1)} %shard_map.87), channel_id=1, replica_groups=mesh['section'=4,'blk'=8,'zlo'=2,'x'=4,'core'=2] {'blk','zlo','x'}, dimensions={0} | all-to-all | bytes 327680 | tf_op jit(solution)/shard_map/all_to_all | solution.py:367
  129.0 0.7 shard_map.88
  (3 shorter events, 0.1 us)
Async XLA Ops:
  0.0 9.7 %copy-start = (f32[16,2,6144]{2,1,0:T(2,128)S(1)}, f32[16,2,6144]{2,1,0:T(2,128)}, u32[]{:S(2)}) copy-start(f32[16,2,6144]{2,1,0:T(2,128)} %param.9) | copy-start | bytes 2359300
  0.0 1.0 copy-start.2
  1.0 14.6 %collective-permute-start = (bf16[8,8,1024]{2,1,0:T(8,128)(2,1)S(1)}, bf16[8,8,1024]{2,1,0:T(8,128)(2,1)S(1)}, u32[]{:S(2)}, u32[]{:S(2)}) collective-permute-start(bf16[8,8,1024]{2,1,0:T(8,128)(2,1)S(1)} %shard_map.73), channel_id=1, source_target_pairs={{0,128},{128,256},{256,384},{384,0},{1,129},{129,257},{257,385},{3... | collective-permute-start | bytes 393224 | tf_op jit(solution)/shard_map/ppermute | solution.py:20
  7.1 25.1 %collective-permute-start.1 = (bf16[3,3,768,128]{3,2,1,0:T(8,128)(2,1)}, bf16[3,3,768,128]{3,2,1,0:T(8,128)(2,1)S(1)}, u32[]{:S(2)}, u32[]{:S(2)}) collective-permute-start(bf16[3,3,768,128]{3,2,1,0:T(8,128)(2,1)} %bitcast.18), channel_id=1, source_target_pairs={{0,1},{1,0},{2,3},{3,2},{4,5},{5,4},{6,7},{7,6},{8,9},{9,8},{10,11... | collective-permute-start | bytes 5308424 | tf_op jit(solution)/shard_map/ppermute | solution.py:20
  32.3 19.8 %copy-start.1 = (bf16[1,768,3,3,128]{4,1,3,2,0:T(8,128)(2,1)S(1)}, bf16[1,768,3,3,128]{4,1,3,2,0:T(8,128)(2,1)}, u32[]{:S(2)}) copy-start(bf16[1,768,3,3,128]{4,1,3,2,0:T(8,128)(2,1)} %param.10) | copy-start | bytes 5308420
  53.4 8.1 %collective-permute-start.6 = (bf16[320,384]{1,0:T(8,128)(2,1)S(1)}, bf16[320,384]{1,0:T(8,128)(2,1)S(1)}, u32[]{:S(2)}, u32[]{:S(2)}) collective-permute-start(bf16[320,384]{1,0:T(8,128)(2,1)S(1)} %get-tuple-element.24), channel_id=1, source_target_pairs={{0,112},{16,0},{64,48},{80,64},{96,80},{112,96},{1,113},{17,1},{65... | collective-permute-start | bytes 737288 | tf_op jit(solution)/shard_map/ppermute | solution.py:26
  55.4 9.4 %collective-permute-start.2 = (bf16[320,384]{1,0:T(8,128)(2,1)S(1)}, bf16[320,384]{1,0:T(8,128)(2,1)S(1)}, u32[]{:S(2)}, u32[]{:S(2)}) collective-permute-start(bf16[320,384]{1,0:T(8,128)(2,1)S(1)} %get-tuple-element.20), channel_id=1, source_target_pairs={{0,16},{16,32},{64,80},{80,96},{96,112},{112,0},{1,17},{17,33},{65... | collective-permute-start | bytes 737288 | tf_op jit(solution)/shard_map/ppermute | solution.py:26
  61.6 10.5 %collective-permute-start.7 = (bf16[640,384]{1,0:T(8,128)(2,1)S(1)}, bf16[640,384]{1,0:T(8,128)(2,1)S(1)}, u32[]{:S(2)}, u32[]{:S(2)}) collective-permute-start(bf16[640,384]{1,0:T(8,128)(2,1)S(1)} %shard_map.82), channel_id=1, source_target_pairs={{0,112},{48,32},{64,48},{80,64},{96,80},{112,96},{1,113},{49,33},{... | collective-permute-start | bytes 1474568 | tf_op jit(solution)/shard_map/ppermute | solution.py:26
  64.9 12.4 %collective-permute-start.3 = (bf16[640,384]{1,0:T(8,128)(2,1)S(1)}, bf16[640,384]{1,0:T(8,128)(2,1)S(1)}, u32[]{:S(2)}, u32[]{:S(2)}) collective-permute-start(bf16[640,384]{1,0:T(8,128)(2,1)S(1)} %shard_map.79), channel_id=1, source_target_pairs={{0,16},{16,32},{32,48},{80,96},{96,112},{112,0},{1,17},{17,33},{33... | collective-permute-start | bytes 1474568 | tf_op jit(solution)/shard_map/ppermute | solution.py:26
  72.2 7.3 %collective-permute-start.8 = (bf16[640,384]{1,0:T(8,128)(2,1)S(1)}, bf16[640,384]{1,0:T(8,128)(2,1)S(1)}, u32[]{:S(2)}, u32[]{:S(2)}) collective-permute-start(bf16[640,384]{1,0:T(8,128)(2,1)S(1)} %shard_map.83), channel_id=1, source_target_pairs={{32,16},{48,32},{64,48},{80,64},{96,80},{112,96},{33,17},{49,33},{... | collective-permute-start | bytes 1474568 | tf_op jit(solution)/shard_map/ppermute | solution.py:26
  77.5 14.0 %copy-start.3 = (f32[1,3,128]{2,0,1:T(1,128)S(1)}, f32[1,3,128]{2,0,1:T(1,128)}, u32[]{:S(2)}) copy-start(f32[1,3,128]{2,0,1:T(1,128)} %param.11) | copy-start | bytes 4612
  77.5 14.0 %copy-start.4 = (f32[1,3,128]{2,0,1:T(1,128)S(1)}, f32[1,3,128]{2,0,1:T(1,128)}, u32[]{:S(2)}) copy-start(f32[1,3,128]{2,0,1:T(1,128)} %param.12) | copy-start | bytes 4612
  77.5 11.9 %collective-permute-start.4 = (bf16[640,384]{1,0:T(8,128)(2,1)S(1)}, bf16[640,384]{1,0:T(8,128)(2,1)S(1)}, u32[]{:S(2)}, u32[]{:S(2)}) collective-permute-start(bf16[640,384]{1,0:T(8,128)(2,1)S(1)} %shard_map.80), channel_id=1, source_target_pairs={{0,16},{16,32},{32,48},{48,64},{96,112},{112,0},{1,17},{17,33},{33... | collective-permute-start | bytes 1474568 | tf_op jit(solution)/shard_map/ppermute | solution.py:26
  79.6 15.0 %collective-permute-start.9 = (bf16[640,384]{1,0:T(8,128)(2,1)S(1)}, bf16[640,384]{1,0:T(8,128)(2,1)S(1)}, u32[]{:S(2)}, u32[]{:S(2)}) collective-permute-start(bf16[640,384]{1,0:T(8,128)(2,1)S(1)} %shard_map.84), channel_id=1, source_target_pairs={{16,0},{32,16},{48,32},{64,48},{80,64},{96,80},{17,1},{33,17},{49,... | collective-permute-start | bytes 1474568 | tf_op jit(solution)/shard_map/ppermute | solution.py:26
  89.6 11.9 %collective-permute-start.5 = (bf16[640,384]{1,0:T(8,128)(2,1)S(1)}, bf16[640,384]{1,0:T(8,128)(2,1)S(1)}, u32[]{:S(2)}, u32[]{:S(2)}) collective-permute-start(bf16[640,384]{1,0:T(8,128)(2,1)S(1)} %shard_map.81), channel_id=1, source_target_pairs={{0,16},{16,32},{32,48},{48,64},{64,80},{112,0},{1,17},{17,33},{33,... | collective-permute-start | bytes 1474568 | tf_op jit(solution)/shard_map/ppermute | solution.py:26
  91.5 3.1 %collective-permute-start.10 = (f32[6,128]{1,0:T(8,128)S(1)}, f32[6,128]{1,0:T(8,128)S(1)}, u32[]{:S(2)}, u32[]{:S(2)}) collective-permute-start(f32[6,128]{1,0:T(8,128)S(1)} %shard_map.85.gains), channel_id=1, source_target_pairs={{0,1},{1,0},{2,3},{3,2},{4,5},{5,4},{6,7},{7,6},{8,9},{9,8},{10,11... | collective-permute-start | bytes 9224 | tf_op jit(solution)/shard_map/ppermute | solution.py:20
  102.5 3.5 %collective-permute-start.11 = (bf16[640,256]{1,0:T(8,128)(2,1)S(1)}, bf16[640,256]{1,0:T(8,128)(2,1)S(1)}, u32[]{:S(2)}, u32[]{:S(2)}) collective-permute-start(bf16[640,256]{1,0:T(8,128)(2,1)S(1)} %get-tuple-element.26.refs_3_), channel_id=1, source_target_pairs={{0,1},{1,0},{2,3},{3,2},{4,5},{5,4},{6,7},{7,6},{8,9},{9,8},{10,11... | collective-permute-start | bytes 983048 | tf_op jit(solution)/shard_map/ppermute | solution.py:20

commit v7 on v6

--- a/solution.py
+++ b/solution.py
@@ -155,7 +155,6 @@
 def product_kernel(steps, place, tokens, own, other, *refs):
     outs, block, sems = refs[:-2], refs[-2], refs[-1]
     pieces = len(outs) // len(steps)
-    size = tokens.shape[0] // pieces
     row, core = place[0], place[1]
     heads, parts = own.shape[:2]
 
@@ -181,20 +180,22 @@
         pltpu.make_async_copy(own.at[0], block.at[slot], sems.at[slot]).wait()
         weights = jnp.concatenate([block[slot, part] for part in range(parts)], axis=1)
         total = jnp.dot(tokens[...], weights, preferred_element_type=jnp.float32)
-        for piece in range(pieces):
-            out = outs[number * pieces + piece]
-            out[...] = total[piece * size : (piece + 1) * size].astype(out.dtype)
-
-
-def products(steps, place, tokens, own, other, pieces=1):
+        begin = 0
+        for out in outs[number * pieces : (number + 1) * pieces]:
+            out[...] = total[begin : begin + out.shape[0]].astype(out.dtype)
+            begin += out.shape[0]
+
+
+def products(steps, place, tokens, own, other, pieces=None):
     rows, depth = tokens.shape
     parts, size = own.shape[1], own.shape[3]
-    shape = jax.ShapeDtypeStruct((rows // pieces, parts * size), jnp.bfloat16)
+    pieces = pieces or (rows,)
+    shapes = [jax.ShapeDtypeStruct((piece, parts * size), jnp.bfloat16) for piece in pieces]
     return pl.pallas_call(
         lambda *refs: product_kernel(steps, *refs),
-        out_shape=[shape] * (pieces * len(steps)),
+        out_shape=shapes * len(steps),
         in_specs=[SMALL, WHOLE, DISTANT, DISTANT],
-        out_specs=[WHOLE] * (pieces * len(steps)),
+        out_specs=[WHOLE] * (len(pieces) * len(steps)),
         scratch_shapes=[
             pltpu.VMEM((2,) + own.shape[1:], jnp.bfloat16),
             pltpu.SemaphoreType.DMA((2,)),
@@ -350,13 +351,14 @@
     copies = spread(sliced, other, (chips, blks * tok_rows, slice_width))
     tokens = lax.all_to_all(copies, CHIPS, 0, 0, tiled=False)
     tokens = tokens.reshape(chips * blks * tok_rows, slice_width)
-    half = tokens.shape[0] // 2
+    rows = tokens.shape[0]
+    cut = rows // 4
 
     owners = 2 * own.shape[0]
-    up, down = products((4,), place, tokens, own, other, 2)
+    up, down = products((4,), place, tokens, own, other, (cut, rows - cut))
     up, down = passed(up, 1, 4, owners), passed(down, -1, 4, owners)
     three, five = products((3, 5), place, tokens, own, other)
-    up, down = passed(added(three, up), 1, 3, owners), passed(added(five, down, half), -1, 3, owners)
+    up, down = passed(added(three, up), 1, 3, owners), passed(added(five, down, cut), -1, 3, owners)
     two, six, one, seven, zero = products((2, 6, 1, 7, 0), place, tokens, own, other)
     up, down = passed(added(two, up), 1, 2, owners), passed(added(six, down), -1, 2, owners)
     up, down = passed(added(one, up), 1, 1, owners), passed(added(seven, down), -1, 1, owners)

time: 130 us -> 128 us (0.985)
  waiting for transfers between devices: 27.8 us -> 25.6 us
  blocking collectives: 56.5 us -> 55 us
  starting transfers between devices: 29.3 us -> 30.6 us
    ppermute x8, waiting for transfers between devices: 20 us -> 17.8 us  [passed(): return lax.ppermute(value, 'blk', pairs)]
    all_to_all x1, blocking collectives: 20.9 us -> 19.4 us  [on_device(): returned = lax.all_to_all(mixed, ('blk',) + CHIPS, 0, 0, tiled=False)]
    ppermute x8, starting transfers between devices: 17.4 us -> 18.8 us  [passed(): return lax.ppermute(value, 'blk', pairs)]
  transfers between devices with their start and end apart: 12 -> 12, of which waited for: 6 -> 8; matrix products, arithmetic and copies ran while one was open for 0% -> 0% of each run, Pallas kernels for 6% -> 6%
where the time goes in v7:
time: 128 us; the launch traced here: 127 us
  blocking collectives  55 us (43%)
  starting transfers between devices  30.6 us (24%)
  waiting for transfers between devices  25.6 us (20%)
  Pallas kernels  13.4 us (10%)
  between operations  1.56 us (1%)
    all_to_all x1, blocking collectives, on_device(): tokens = lax.all_to_all(copies, CHIPS, 0, 0, tiled=False)  19.6 us
    all_to_all x1, blocking collectives, on_device(): returned = lax.all_to_all(mixed, ('blk',) + CHIPS, 0, 0, tiled=False)  19.4 us
    ppermute x8, starting transfers between devices, passed(): return lax.ppermute(value, 'blk', pairs)  18.8 us
    ppermute x8, waiting for transfers between devices, passed(): return lax.ppermute(value, 'blk', pairs)  17.8 us
    all_to_all x1, blocking collectives, on_device(): sliced = lax.all_to_all(sent, 'blk', 0, 0, tiled=False)  16 us
    ppermute x4, starting transfers between devices, shifted(): return lax.ppermute(value, axis, pairs)  11.9 us
    pallas_call x3, Pallas kernels, products(): pl.pallas_call(lambda *refs: product_kernel(steps, *refs), out_shape=shap...  8.18 us
    ppermute x4, waiting for transfers between devices, shifted(): return lax.ppermute(value, axis, pairs)  7.85 us
  transfers between devices with their start and end apart: 12, of which 8 were waited for; matrix products, arithmetic and copies ran while one was open for 0% of the time, Pallas kernels for 6%

profile of v7, /device:TPU:6, one launch (start us, length us, event | category | flops | bytes accessed | tf_op | source)
XLA Modules:
  0.0 127.4 jit_solution(5018375498345674014)
XLA Ops:
  0.0 0.0 copy-start
  0.0 0.0 copy-start.2
  0.0 1.0 copy-done.2
  1.0 6.1 %collective-permute-start = (bf16[8,8,1024]{2,1,0:T(8,128)(2,1)S(1)}, bf16[8,8,1024]{2,1,0:T(8,128)(2,1)S(1)}, u32[]{:S(2)}, u32[]{:S(2)}) collective-permute-start(bf16[8,8,1024]{2,1,0:T(8,128)(2,1)S(1)} %shard_map.73), channel_id=1, source_target_pairs={{0,128},{128,256},{256,384},{384,0},{1,129},{129,257},{257,385},{3... | collective-permute-start | bytes 393224 | tf_op jit(solution)/shard_map/ppermute | solution.py:20
  7.1 1.9 %collective-permute-start.1 = (bf16[3,3,768,128]{3,2,1,0:T(8,128)(2,1)}, bf16[3,3,768,128]{3,2,1,0:T(8,128)(2,1)S(1)}, u32[]{:S(2)}, u32[]{:S(2)}) collective-permute-start(bf16[3,3,768,128]{3,2,1,0:T(8,128)(2,1)} %bitcast.18), channel_id=1, source_target_pairs={{0,1},{1,0},{2,3},{3,2},{4,5},{5,4},{6,7},{7,6},{8,9},{9,8},{10,11... | collective-permute-start | bytes 5308424 | tf_op jit(solution)/shard_map/ppermute | solution.py:20
  9.7 0.0 copy-done
  10.4 0.1 pad_add_fusion.place.refs_0_
  10.5 5.1 %collective-permute-done.stale = bf16[8,8,1024]{2,1,0:T(8,128)(2,1)S(1)} collective-permute-done((bf16[8,8,1024]{2,1,0:T(8,128)(2,1)S(1)}, bf16[8,8,1024]{2,1,0:T(8,128)(2,1)S(1)}, u32[]{:S(2)}, u32[]{:S(2)}) %collective-permute-start) | collective-permute-done | bytes 131104 | tf_op jit(solution)/shard_map/ppermute | solution.py:20
  15.6 0.7 shard_map.74
  16.3 16.0 %all_to_all.15.sliced.refs_1_ = bf16[8,8,1024]{2,1,0:T(8,128)(2,1)S(1)} all-to-all(bf16[8,8,1024]{2,1,0:T(8,128)(2,1)S(1)} %shard_map.74), channel_id=1, replica_groups=mesh['section'=4,'blk'=8,'zlo'=2,'x'=4,'core'=2] {'blk'}, dimensions={0} | all-to-all | bytes 262144 | tf_op jit(solution)/shard_map/all_to_all | solution.py:350
  32.3 0.0 copy-start.1
  32.3 0.0 collective-permute-done.1.weights.refs_3_
  32.3 0.1 shard_map.75
  32.4 19.6 %all_to_all.16 = bf16[8,80,768]{2,1,0:T(8,128)(2,1)S(1)} all-to-all(bf16[8,80,768]{2,1,0:T(8,128)(2,1)S(1)} %shard_map.75), channel_id=1, replica_groups=mesh['section'=4,'blk'=8,'zlo'=2,'x'=4,'core'=2] {'zlo','x'}, dimensions={0} | all-to-all | bytes 1966080 | tf_op jit(solution)/shard_map/all_to_all | solution.py:352
  52.0 0.0 copy-done.1
  52.0 1.4 %shard_map.78 = (bf16[160,384]{1,0:T(8,128)(2,1)S(1)}, bf16[480,384]{1,0:T(8,128)(2,1)S(1)}) custom-call(s32[2]{0:T(128)S(1)} %pad_add_fusion.place.refs_0_, bf16[640,768]{1,0:T(8,128)(2,1)S(1)} %bitcast.15, bf16[3,3,768,128]{3,2,1,0:T(8,128)(2,1)S(1)} %bitcast.19, bf16[3,3,768,128]{3,2,1,0:T(8,128)(2,1)S(1)} %collective-permute-done.1.weights.refs_3_), custom_call_target="tpu_custom_call" | custom-call | flops 377487360 | bytes 4194304 | tf_op jit(solution)/shard_map/pallas_call | solution.py:194
  53.4 2.0 %collective-permute-start.6 = (bf16[480,384]{1,0:T(8,128)(2,1)S(1)}, bf16[480,384]{1,0:T(8,128)(2,1)S(1)}, u32[]{:S(2)}, u32[]{:S(2)}) collective-permute-start(bf16[480,384]{1,0:T(8,128)(2,1)S(1)} %get-tuple-element.24), channel_id=1, source_target_pairs={{0,112},{16,0},{64,48},{80,64},{96,80},{112,96},{1,113},{17,1},{65... | collective-permute-start | bytes 1105928 | tf_op jit(solution)/shard_map/ppermute | solution.py:26
  55.4 3.9 %collective-permute-start.2 = (bf16[160,384]{1,0:T(8,128)(2,1)S(1)}, bf16[160,384]{1,0:T(8,128)(2,1)S(1)}, u32[]{:S(2)}, u32[]{:S(2)}) collective-permute-start(bf16[160,384]{1,0:T(8,128)(2,1)S(1)} %get-tuple-element.20), channel_id=1, source_target_pairs={{0,16},{16,32},{64,80},{80,96},{96,112},{112,0},{1,17},{17,33},{65... | collective-permute-start | bytes 368648 | tf_op jit(solution)/shard_map/ppermute | solution.py:26
  59.3 2.2 %shard_map.77 = (bf16[640,384]{1,0:T(8,128)(2,1)S(1)}, bf16[640,384]{1,0:T(8,128)(2,1)S(1)}) custom-call(s32[2]{0:T(128)S(1)} %pad_add_fusion.place.refs_0_, bf16[640,768]{1,0:T(8,128)(2,1)S(1)} %bitcast.16, bf16[3,3,768,128]{3,2,1,0:T(8,128)(2,1)S(1)} %bitcast.20, bf16[3,3,768,128]{3,2,1,0:T(8,128)(2,1)S(1)} %collective-permute-done.1.weights.refs_3_), custom_call_target="tpu_custom_call" | custom-call | flops 754974720 | bytes 4194304 | tf_op jit(solution)/shard_map/pallas_call | solution.py:194
  61.5 1.9 %collective-permute-done.2.refs_1_ = bf16[160,384]{1,0:T(8,128)(2,1)S(1)} collective-permute-done((bf16[160,384]{1,0:T(8,128)(2,1)S(1)}, bf16[160,384]{1,0:T(8,128)(2,1)S(1)}, u32[]{:S(2)}, u32[]{:S(2)}) %collective-permute-start.2) | collective-permute-done | bytes 122912 | tf_op jit(solution)/shard_map/ppermute | solution.py:26
  63.4 0.1 shard_map.79
  63.5 2.8 %collective-permute-start.3 = (bf16[640,384]{1,0:T(8,128)(2,1)S(1)}, bf16[640,384]{1,0:T(8,128)(2,1)S(1)}, u32[]{:S(2)}, u32[]{:S(2)}) collective-permute-start(bf16[640,384]{1,0:T(8,128)(2,1)S(1)} %shard_map.79), channel_id=1, source_target_pairs={{0,16},{16,32},{32,48},{80,96},{96,112},{112,0},{1,17},{17,33},{33... | collective-permute-start | bytes 1474568 | tf_op jit(solution)/shard_map/ppermute | solution.py:26
  66.3 0.0 collective-permute-done.6.refs_1_
  66.3 0.1 shard_map.82
  66.4 4.3 %collective-permute-start.7 = (bf16[640,384]{1,0:T(8,128)(2,1)S(1)}, bf16[640,384]{1,0:T(8,128)(2,1)S(1)}, u32[]{:S(2)}, u32[]{:S(2)}) collective-permute-start(bf16[640,384]{1,0:T(8,128)(2,1)S(1)} %shard_map.82), channel_id=1, source_target_pairs={{0,112},{48,32},{64,48},{80,64},{96,80},{112,96},{1,113},{49,33},{... | collective-permute-start | bytes 1474568 | tf_op jit(solution)/shard_map/ppermute | solution.py:26
  70.7 4.6 %shard_map.76 = (bf16[640,384]{1,0:T(8,128)(2,1)S(1)}, bf16[640,384]{1,0:T(8,128)(2,1)S(1)}, bf16[640,384]{1,0:T(8,128)(2,1)S(1)}, bf16[640,384]{1,0:T(8,128)(2,1)S(1)}, bf16[640,384]{1,0:T(8,128)(2,1)S(1)}) custom-call(s32[2]{0:T(128)S(1)} %pad_add_fusion.place.refs_0_, bf16[640,768]{1,0:T(8,128)(2,1)S(1)} %bitcast.17, ...), custom_call_target="tpu_custom_call" | custom-call | flops 1887436800 | bytes 4194304 | tf_op jit(solution)/shard_map/pallas_call | solution.py:194
  75.3 0.1 collective-permute-done.3.refs_1_
  75.4 0.1 shard_map.80
  75.5 1.9 %collective-permute-start.4 = (bf16[640,384]{1,0:T(8,128)(2,1)S(1)}, bf16[640,384]{1,0:T(8,128)(2,1)S(1)}, u32[]{:S(2)}, u32[]{:S(2)}) collective-permute-start(bf16[640,384]{1,0:T(8,128)(2,1)S(1)} %shard_map.80), channel_id=1, source_target_pairs={{0,16},{16,32},{32,48},{48,64},{96,112},{112,0},{1,17},{17,33},{33... | collective-permute-start | bytes 1474568 | tf_op jit(solution)/shard_map/ppermute | solution.py:26
  77.5 0.0 collective-permute-done.7.refs_1_
  77.5 0.1 shard_map.83
  77.6 0.0 copy-start.3
  77.6 0.0 copy-start.4
  77.6 0.7 collective-permute-start.8
  78.3 9.4 %collective-permute-done.4.refs_1_ = bf16[640,384]{1,0:T(8,128)(2,1)S(1)} collective-permute-done((bf16[640,384]{1,0:T(8,128)(2,1)S(1)}, bf16[640,384]{1,0:T(8,128)(2,1)S(1)}, u32[]{:S(2)}, u32[]{:S(2)}) %collective-permute-start.4) | collective-permute-done | bytes 491552 | tf_op jit(solution)/shard_map/ppermute | solution.py:26
  87.7 0.1 shard_map.81
  87.9 1.9 %collective-permute-start.5 = (bf16[640,384]{1,0:T(8,128)(2,1)S(1)}, bf16[640,384]{1,0:T(8,128)(2,1)S(1)}, u32[]{:S(2)}, u32[]{:S(2)}) collective-permute-start(bf16[640,384]{1,0:T(8,128)(2,1)S(1)} %shard_map.81), channel_id=1, source_target_pairs={{0,16},{16,32},{32,48},{48,64},{64,80},{112,0},{1,17},{17,33},{33,... | collective-permute-start | bytes 1474568 | tf_op jit(solution)/shard_map/ppermute | solution.py:26
  89.8 0.0 collective-permute-done.8.refs_1_
  89.8 0.1 shard_map.84
  89.9 1.3 %collective-permute-start.9 = (bf16[640,384]{1,0:T(8,128)(2,1)S(1)}, bf16[640,384]{1,0:T(8,128)(2,1)S(1)}, u32[]{:S(2)}, u32[]{:S(2)}) collective-permute-start(bf16[640,384]{1,0:T(8,128)(2,1)S(1)} %shard_map.84), channel_id=1, source_target_pairs={{16,0},{32,16},{48,32},{64,48},{80,64},{96,80},{17,1},{33,17},{49,... | collective-permute-start | bytes 1474568 | tf_op jit(solution)/shard_map/ppermute | solution.py:26
  91.2 0.0 copy-done.3
  91.3 0.0 copy-done.4
  91.3 1.9 %collective-permute-start.10 = (f32[6,128]{1,0:T(8,128)S(1)}, f32[6,128]{1,0:T(8,128)S(1)}, u32[]{:S(2)}, u32[]{:S(2)}) collective-permute-start(f32[6,128]{1,0:T(8,128)S(1)} %shard_map.85.gains), channel_id=1, source_target_pairs={{0,1},{1,0},{2,3},{3,2},{4,5},{5,4},{6,7},{7,6},{8,9},{9,8},{10,11... | collective-permute-start | bytes 9224 | tf_op jit(solution)/shard_map/ppermute | solution.py:20
  93.2 1.1 collective-permute-done.10.theirs
  94.3 5.5 %collective-permute-done.5.second = bf16[640,384]{1,0:T(8,128)(2,1)S(1)} collective-permute-done((bf16[640,384]{1,0:T(8,128)(2,1)S(1)}, bf16[640,384]{1,0:T(8,128)(2,1)S(1)}, u32[]{:S(2)}, u32[]{:S(2)}) %collective-permute-start.5) | collective-permute-done | bytes 491552 | tf_op jit(solution)/shard_map/ppermute | solution.py:26
  99.8 0.9 collective-permute-done.9.third
  100.7 0.9 shard_map.86
  101.6 1.9 %collective-permute-start.11 = (bf16[640,256]{1,0:T(8,128)(2,1)S(1)}, bf16[640,256]{1,0:T(8,128)(2,1)S(1)}, u32[]{:S(2)}, u32[]{:S(2)}) collective-permute-start(bf16[640,256]{1,0:T(8,128)(2,1)S(1)} %get-tuple-element.26.refs_3_), channel_id=1, source_target_pairs={{0,1},{1,0},{2,3},{3,2},{4,5},{5,4},{6,7},{7,6},{8,9},{9,8},{10,11... | collective-permute-start | bytes 983048 | tf_op jit(solution)/shard_map/ppermute | solution.py:20
  103.5 1.6 %collective-permute-done.11.refs_4_ = bf16[640,256]{1,0:T(8,128)(2,1)S(1)} collective-permute-done((bf16[640,256]{1,0:T(8,128)(2,1)S(1)}, bf16[640,256]{1,0:T(8,128)(2,1)S(1)}, u32[]{:S(2)}, u32[]{:S(2)}) %collective-permute-start.11) | collective-permute-done | bytes 327712 | tf_op jit(solution)/shard_map/ppermute | solution.py:20
  105.1 2.1 %shard_map.87 = bf16[64,10,128]{2,1,0:T(8,128)(2,1)S(1)} custom-call(s32[2]{0:T(128)S(1)} %pad_add_fusion.place.refs_0_, bf16[8,8,1024]{2,1,0:T(8,128)(2,1)S(1)} %all_to_all.15.sliced.refs_1_, bf16[640,128]{1,0:T(8,128)(2,1)S(1)} %get-tuple-element.25.refs_2_, bf16[640,256]{1,0:T(8,128)(2,1)S(1)} %get-tuple-element.26.refs_3_, ...), custom_call_target="tpu_custom_call" | custom-call | flops 419430400 | bytes 1048576 | tf_op jit(solution)/shard_map/pallas_call | solution.py:300
  107.2 19.4 %all_to_all.17 = bf16[64,10,128]{2,1,0:T(8,128)(2,1)S(1)} all-to-all(bf16[64,10,128]{2,1,0:T(8,128)(2,1)S(1)} %shard_map.87), channel_id=1, replica_groups=mesh['section'=4,'blk'=8,'zlo'=2,'x'=4,'core'=2] {'blk','zlo','x'}, dimensions={0} | all-to-all | bytes 327680 | tf_op jit(solution)/shard_map/all_to_all | solution.py:369
  126.7 0.7 shard_map.88
  (3 shorter events, 0.1 us)
Async XLA Ops:
  0.0 9.7 %copy-start = (f32[16,2,6144]{2,1,0:T(2,128)S(1)}, f32[16,2,6144]{2,1,0:T(2,128)}, u32[]{:S(2)}) copy-start(f32[16,2,6144]{2,1,0:T(2,128)} %param.9) | copy-start | bytes 2359300
  0.0 1.0 copy-start.2
  1.0 14.6 %collective-permute-start = (bf16[8,8,1024]{2,1,0:T(8,128)(2,1)S(1)}, bf16[8,8,1024]{2,1,0:T(8,128)(2,1)S(1)}, u32[]{:S(2)}, u32[]{:S(2)}) collective-permute-start(bf16[8,8,1024]{2,1,0:T(8,128)(2,1)S(1)} %shard_map.73), channel_id=1, source_target_pairs={{0,128},{128,256},{256,384},{384,0},{1,129},{129,257},{257,385},{3... | collective-permute-start | bytes 393224 | tf_op jit(solution)/shard_map/ppermute | solution.py:20
  7.1 25.1 %collective-permute-start.1 = (bf16[3,3,768,128]{3,2,1,0:T(8,128)(2,1)}, bf16[3,3,768,128]{3,2,1,0:T(8,128)(2,1)S(1)}, u32[]{:S(2)}, u32[]{:S(2)}) collective-permute-start(bf16[3,3,768,128]{3,2,1,0:T(8,128)(2,1)} %bitcast.18), channel_id=1, source_target_pairs={{0,1},{1,0},{2,3},{3,2},{4,5},{5,4},{6,7},{7,6},{8,9},{9,8},{10,11... | collective-permute-start | bytes 5308424 | tf_op jit(solution)/shard_map/ppermute | solution.py:20
  32.3 19.8 %copy-start.1 = (bf16[1,768,3,3,128]{4,1,3,2,0:T(8,128)(2,1)S(1)}, bf16[1,768,3,3,128]{4,1,3,2,0:T(8,128)(2,1)}, u32[]{:S(2)}) copy-start(bf16[1,768,3,3,128]{4,1,3,2,0:T(8,128)(2,1)} %param.10) | copy-start | bytes 5308420
  53.4 12.9 %collective-permute-start.6 = (bf16[480,384]{1,0:T(8,128)(2,1)S(1)}, bf16[480,384]{1,0:T(8,128)(2,1)S(1)}, u32[]{:S(2)}, u32[]{:S(2)}) collective-permute-start(bf16[480,384]{1,0:T(8,128)(2,1)S(1)} %get-tuple-element.24), channel_id=1, source_target_pairs={{0,112},{16,0},{64,48},{80,64},{96,80},{112,96},{1,113},{17,1},{65... | collective-permute-start | bytes 1105928 | tf_op jit(solution)/shard_map/ppermute | solution.py:26
  55.4 8.0 %collective-permute-start.2 = (bf16[160,384]{1,0:T(8,128)(2,1)S(1)}, bf16[160,384]{1,0:T(8,128)(2,1)S(1)}, u32[]{:S(2)}, u32[]{:S(2)}) collective-permute-start(bf16[160,384]{1,0:T(8,128)(2,1)S(1)} %get-tuple-element.20), channel_id=1, source_target_pairs={{0,16},{16,32},{64,80},{80,96},{96,112},{112,0},{1,17},{17,33},{65... | collective-permute-start | bytes 368648 | tf_op jit(solution)/shard_map/ppermute | solution.py:26
  63.5 11.9 %collective-permute-start.3 = (bf16[640,384]{1,0:T(8,128)(2,1)S(1)}, bf16[640,384]{1,0:T(8,128)(2,1)S(1)}, u32[]{:S(2)}, u32[]{:S(2)}) collective-permute-start(bf16[640,384]{1,0:T(8,128)(2,1)S(1)} %shard_map.79), channel_id=1, source_target_pairs={{0,16},{16,32},{32,48},{80,96},{96,112},{112,0},{1,17},{17,33},{33... | collective-permute-start | bytes 1474568 | tf_op jit(solution)/shard_map/ppermute | solution.py:26
  66.4 11.1 %collective-permute-start.7 = (bf16[640,384]{1,0:T(8,128)(2,1)S(1)}, bf16[640,384]{1,0:T(8,128)(2,1)S(1)}, u32[]{:S(2)}, u32[]{:S(2)}) collective-permute-start(bf16[640,384]{1,0:T(8,128)(2,1)S(1)} %shard_map.82), channel_id=1, source_target_pairs={{0,112},{48,32},{64,48},{80,64},{96,80},{112,96},{1,113},{49,33},{... | collective-permute-start | bytes 1474568 | tf_op jit(solution)/shard_map/ppermute | solution.py:26
  75.5 12.2 %collective-permute-start.4 = (bf16[640,384]{1,0:T(8,128)(2,1)S(1)}, bf16[640,384]{1,0:T(8,128)(2,1)S(1)}, u32[]{:S(2)}, u32[]{:S(2)}) collective-permute-start(bf16[640,384]{1,0:T(8,128)(2,1)S(1)} %shard_map.80), channel_id=1, source_target_pairs={{0,16},{16,32},{32,48},{48,64},{96,112},{112,0},{1,17},{17,33},{33... | collective-permute-start | bytes 1474568 | tf_op jit(solution)/shard_map/ppermute | solution.py:26
  77.6 13.6 %copy-start.3 = (f32[1,3,128]{2,0,1:T(1,128)S(1)}, f32[1,3,128]{2,0,1:T(1,128)}, u32[]{:S(2)}) copy-start(f32[1,3,128]{2,0,1:T(1,128)} %param.11) | copy-start | bytes 4612
  77.6 13.6 %copy-start.4 = (f32[1,3,128]{2,0,1:T(1,128)S(1)}, f32[1,3,128]{2,0,1:T(1,128)}, u32[]{:S(2)}) copy-start(f32[1,3,128]{2,0,1:T(1,128)} %param.12) | copy-start | bytes 4612
  77.6 12.2 %collective-permute-start.8 = (bf16[640,384]{1,0:T(8,128)(2,1)S(1)}, bf16[640,384]{1,0:T(8,128)(2,1)S(1)}, u32[]{:S(2)}, u32[]{:S(2)}) collective-permute-start(bf16[640,384]{1,0:T(8,128)(2,1)S(1)} %shard_map.83), channel_id=1, source_target_pairs={{32,16},{48,32},{64,48},{80,64},{96,80},{112,96},{33,17},{49,33},{... | collective-permute-start | bytes 1474568 | tf_op jit(solution)/shard_map/ppermute | solution.py:26
  87.9 11.9 %collective-permute-start.5 = (bf16[640,384]{1,0:T(8,128)(2,1)S(1)}, bf16[640,384]{1,0:T(8,128)(2,1)S(1)}, u32[]{:S(2)}, u32[]{:S(2)}) collective-permute-start(bf16[640,384]{1,0:T(8,128)(2,1)S(1)} %shard_map.81), channel_id=1, source_target_pairs={{0,16},{16,32},{32,48},{48,64},{64,80},{112,0},{1,17},{17,33},{33,... | collective-permute-start | bytes 1474568 | tf_op jit(solution)/shard_map/ppermute | solution.py:26
  89.9 10.7 %collective-permute-start.9 = (bf16[640,384]{1,0:T(8,128)(2,1)S(1)}, bf16[640,384]{1,0:T(8,128)(2,1)S(1)}, u32[]{:S(2)}, u32[]{:S(2)}) collective-permute-start(bf16[640,384]{1,0:T(8,128)(2,1)S(1)} %shard_map.84), channel_id=1, source_target_pairs={{16,0},{32,16},{48,32},{64,48},{80,64},{96,80},{17,1},{33,17},{49,... | collective-permute-start | bytes 1474568 | tf_op jit(solution)/shard_map/ppermute | solution.py:26
  91.3 3.1 %collective-permute-start.10 = (f32[6,128]{1,0:T(8,128)S(1)}, f32[6,128]{1,0:T(8,128)S(1)}, u32[]{:S(2)}, u32[]{:S(2)}) collective-permute-start(f32[6,128]{1,0:T(8,128)S(1)} %shard_map.85.gains), channel_id=1, source_target_pairs={{0,1},{1,0},{2,3},{3,2},{4,5},{5,4},{6,7},{7,6},{8,9},{9,8},{10,11... | collective-permute-start | bytes 9224 | tf_op jit(solution)/shard_map/ppermute | solution.py:20
  101.6 3.5 %collective-permute-start.11 = (bf16[640,256]{1,0:T(8,128)(2,1)S(1)}, bf16[640,256]{1,0:T(8,128)(2,1)S(1)}, u32[]{:S(2)}, u32[]{:S(2)}) collective-permute-start(bf16[640,256]{1,0:T(8,128)(2,1)S(1)} %get-tuple-element.26.refs_3_), channel_id=1, source_target_pairs={{0,1},{1,0},{2,3},{3,2},{4,5},{5,4},{6,7},{7,6},{8,9},{9,8},{10,11... | collective-permute-start | bytes 983048 | tf_op jit(solution)/shard_map/ppermute | solution.py:20

commit v8 on v7

--- a/solution.py
+++ b/solution.py
@@ -20,9 +20,19 @@
     return lax.ppermute(value, axis, pairs)
 
 
-def passed(value, steps, ahead, owners):
+def owns(row, blks):
+    return (row + 1) % (blks // 2) != 0
+
+
+def head_at(row, blks, heads):
+    return jnp.minimum(jnp.where(row >= blks // 2, row - 1, row), heads - 1)
+
+
+def passed(value, steps, ahead):
     blks = lax.axis_size("blk")
-    pairs = [(row, (row + steps) % blks) for row in range(blks) if (row + steps * ahead) % blks < owners]
+    pairs = [
+        (row, (row + steps) % blks) for row in range(blks) if owns((row + steps * ahead) % blks, blks)
+    ]
     return lax.ppermute(value, "blk", pairs)
 
 
@@ -159,8 +169,8 @@
     heads, parts = own.shape[:2]
 
     def fetch(number):
-        owner = lax.rem(row + steps[number], lax.axis_size("blk"))
-        head = jnp.minimum(owner, 2 * heads - 1)
+        blks = lax.axis_size("blk")
+        head = head_at(lax.rem(row + steps[number], blks), blks, 2 * heads)
         lane = jnp.where(head >= heads, 1, 0)
         slot = number % 2
 
@@ -227,36 +237,53 @@
     )(first, second)
 
 
-def head_kernel(place, first, second, third, gains, theirs, query, pair):
+def head_gain(place, gains, theirs, part):
+    heads = gains.shape[0] // 2
+    owned = head_at(place[0], lax.axis_size("blk"), 2 * heads)
+    lane = jnp.where(owned >= heads, 1, 0)
+    at = pl.ds(part * heads + owned - lane * heads, 1)
+    return jnp.where(lane == place[1], gains[at], theirs[at])
+
+
+def summed(refs, begin, end):
+    return sum(ref[:, begin:end].astype(jnp.float32) for ref in refs)
+
+
+def pair_kernel(place, first, second, third, gains, theirs, pair):
+    size = pair.shape[1] // 2
+    refs = (first, second, third)
+    keys = head_norm(summed(refs, size, 2 * size), head_gain(place, gains, theirs, 1))
+    pair[:, :size] = keys.astype(pair.dtype)
+    pair[:, size:] = summed(refs, 2 * size, 3 * size).astype(pair.dtype)
+
+
+def paired(place, first, second, third, gains, theirs):
+    rows, size = first.shape[0], gains.shape[1]
+    return pl.pallas_call(
+        pair_kernel,
+        out_shape=jax.ShapeDtypeStruct((rows, 2 * size), jnp.bfloat16),
+        in_specs=[SMALL] + [WHOLE] * 5,
+        out_specs=WHOLE,
+        compiler_params=LIMIT,
+        cost_estimate=pl.CostEstimate(flops=10 * first.size, bytes_accessed=4 * 2**19, transcendentals=0),
+    )(place, first, second, third, gains, theirs)
+
+
+def query_kernel(place, first, second, third, gains, theirs, query):
     size = query.shape[1]
-    heads = gains.shape[0] // 2
-    owned = jnp.minimum(place[0], 2 * heads - 1)
-    lane = jnp.where(owned >= heads, 1, 0)
-    index = owned - lane * heads
-    mine = lane == place[1]
-    gain = []
-    for part in range(2):
-        at = pl.ds(part * heads + index, 1)
-        gain.append(jnp.where(mine, gains[at], theirs[at]))
-    total = first[...].astype(jnp.float32) + second[...].astype(jnp.float32)
-    total = total + third[...].astype(jnp.float32)
-    query[...] = head_norm(total[:, :size], gain[0]).astype(query.dtype)
-    pair[:, :size] = head_norm(total[:, size : 2 * size], gain[1]).astype(pair.dtype)
-    pair[:, size:] = total[:, 2 * size :].astype(pair.dtype)
-
-
-def headed(place, first, second, third, gains, theirs):
+    total = summed((first, second, third), 0, size)
+    query[...] = head_norm(total, head_gain(place, gains, theirs, 0)).astype(query.dtype)
+
+
+def queried(place, first, second, third, gains, theirs):
     rows, size = first.shape[0], gains.shape[1]
     return pl.pallas_call(
-        head_kernel,
-        out_shape=[
-            jax.ShapeDtypeStruct((rows, size), jnp.bfloat16),
-            jax.ShapeDtypeStruct((rows, 2 * size), jnp.bfloat16),
-        ],
+        query_kernel,
+        out_shape=jax.ShapeDtypeStruct((rows, size), jnp.bfloat16),
         in_specs=[SMALL] + [WHOLE] * 5,
-        out_specs=[WHOLE] * 2,
-        compiler_params=LIMIT,
-        cost_estimate=pl.CostEstimate(flops=10 * first.size, bytes_accessed=4 * 2**19, transcendentals=0),
+        out_specs=WHOLE,
+        compiler_params=LIMIT,
+        cost_estimate=pl.CostEstimate(flops=5 * first.size, bytes_accessed=2 * 2**19, transcendentals=0),
     )(place, first, second, third, gains, theirs)
 
 
@@ -313,11 +340,12 @@
 def merge_kernel(blocks, out):
     blks, chips = blocks.shape[:2]
     size = blocks.shape[3]
-    heads = out.shape[2] // (chips * size)
+    begin = 0
     for chip in range(chips):
-        for blk in range(heads):
-            begin = (chip * heads + blk) * size
-            out[0, :, begin : begin + size] = blocks[blk, chip]
+        for blk in range(blks):
+            if owns(blk, blks):
+                out[0, :, begin : begin + size] = blocks[blk, chip]
+                begin += size
 
 
 def merged(blocks, shape):
@@ -354,16 +382,16 @@
     rows = tokens.shape[0]
     cut = rows // 4
 
-    owners = 2 * own.shape[0]
     up, down = products((4,), place, tokens, own, other, (cut, rows - cut))
-    up, down = passed(up, 1, 4, owners), passed(down, -1, 4, owners)
+    up, down = passed(up, 1, 4), passed(down, -1, 4)
     three, five = products((3, 5), place, tokens, own, other)
-    up, down = passed(added(three, up), 1, 3, owners), passed(added(five, down, cut), -1, 3, owners)
+    up, down = passed(added(three, up), 1, 3), passed(added(five, down, cut), -1, 3)
     two, six, one, seven, zero = products((2, 6, 1, 7, 0), place, tokens, own, other)
-    up, down = passed(added(two, up), 1, 2, owners), passed(added(six, down), -1, 2, owners)
-    up, down = passed(added(one, up), 1, 1, owners), passed(added(seven, down), -1, 1, owners)
-    query, near = headed(place, zero, up, down, gains, theirs)
+    up, down = passed(added(two, up), 1, 2), passed(added(six, down), -1, 2)
+    up, down = passed(added(one, up), 1, 1), passed(added(seven, down), -1, 1)
+    near = paired(place, zero, up, down, gains, theirs)
     far = shifted(near, "core", 1)
+    query = queried(place, zero, up, down, gains, theirs)
 
     mixed = attended(tok_rows, place, sliced, query, near, far)
     returned = lax.all_to_all(mixed, ("blk",) + CHIPS, 0, 0, tiled=False)

time: 128 us -> 127 us (level)
  waiting for transfers between devices: 25.6 us -> 18.9 us
  starting transfers between devices: 30.6 us -> 35 us
    ppermute x8, waiting for transfers between devices: 17.8 us -> 11.8 us  [passed(): return lax.ppermute(value, 'blk', pairs)]
    ppermute x8, starting transfers between devices: 18.8 us -> 23.2 us  [passed(): return lax.ppermute(value, 'blk', pairs)]
  transfers between devices with their start and end apart: 12 -> 12, of which waited for: 8 -> 8; matrix products, arithmetic and copies ran while one was open for 0% -> 0% of each run, Pallas kernels for 6% -> 7%
where the time goes in v8:
time: 127 us
  blocking collectives  56.1 us (44%)
  starting transfers between devices  35 us (28%)
  waiting for transfers between devices  18.9 us (15%)
  Pallas kernels  14 us (11%)
  between operations  1.56 us (1%)
    ppermute x8, starting transfers between devices, passed(): return lax.ppermute(value, 'blk', pairs)  23.2 us
    all_to_all x1, blocking collectives, on_device(): returned = lax.all_to_all(mixed, ('blk',) + CHIPS, 0, 0, tiled=False)  20.5 us
    all_to_all x1, blocking collectives, on_device(): tokens = lax.all_to_all(copies, CHIPS, 0, 0, tiled=False)  19.6 us
    all_to_all x1, blocking collectives, on_device(): sliced = lax.all_to_all(sent, 'blk', 0, 0, tiled=False)  16 us
    ppermute x4, starting transfers between devices, shifted(): return lax.ppermute(value, axis, pairs)  11.9 us
    ppermute x8, waiting for transfers between devices, passed(): return lax.ppermute(value, 'blk', pairs)  11.8 us
    pallas_call x3, Pallas kernels, products(): pl.pallas_call(lambda *refs: product_kernel(steps, *refs), out_shape=shap...  8.18 us
    ppermute x4, waiting for transfers between devices, shifted(): return lax.ppermute(value, axis, pairs)  7.12 us
  transfers between devices with their start and end apart: 12, of which 8 were waited for; matrix products, arithmetic and copies ran while one was open for 0% of the time, Pallas kernels for 7%

profile of v8, /device:TPU:6, one launch (start us, length us, event | category | flops | bytes accessed | tf_op | source)
XLA Modules:
  0.0 126.8 jit_solution(858875706568390612)
XLA Ops:
  0.0 0.0 copy-start
  0.0 0.0 copy-start.2
  0.0 1.0 copy-done.2
  1.0 6.1 %collective-permute-start = (bf16[8,8,1024]{2,1,0:T(8,128)(2,1)S(1)}, bf16[8,8,1024]{2,1,0:T(8,128)(2,1)S(1)}, u32[]{:S(2)}, u32[]{:S(2)}) collective-permute-start(bf16[8,8,1024]{2,1,0:T(8,128)(2,1)S(1)} %shard_map.73), channel_id=1, source_target_pairs={{0,128},{128,256},{256,384},{384,0},{1,129},{129,257},{257,385},{3... | collective-permute-start | bytes 393224 | tf_op jit(solution)/shard_map/ppermute | solution.py:20
  7.1 1.9 %collective-permute-start.1 = (bf16[3,3,768,128]{3,2,1,0:T(8,128)(2,1)}, bf16[3,3,768,128]{3,2,1,0:T(8,128)(2,1)S(1)}, u32[]{:S(2)}, u32[]{:S(2)}) collective-permute-start(bf16[3,3,768,128]{3,2,1,0:T(8,128)(2,1)} %bitcast.18), channel_id=1, source_target_pairs={{0,1},{1,0},{2,3},{3,2},{4,5},{5,4},{6,7},{7,6},{8,9},{9,8},{10,11... | collective-permute-start | bytes 5308424 | tf_op jit(solution)/shard_map/ppermute | solution.py:20
  9.7 0.0 copy-done
  10.4 0.1 pad_add_fusion.place.refs_0_
  10.5 5.1 %collective-permute-done.stale = bf16[8,8,1024]{2,1,0:T(8,128)(2,1)S(1)} collective-permute-done((bf16[8,8,1024]{2,1,0:T(8,128)(2,1)S(1)}, bf16[8,8,1024]{2,1,0:T(8,128)(2,1)S(1)}, u32[]{:S(2)}, u32[]{:S(2)}) %collective-permute-start) | collective-permute-done | bytes 131104 | tf_op jit(solution)/shard_map/ppermute | solution.py:20
  15.6 0.7 shard_map.74
  16.3 16.0 %all_to_all.15.sliced.refs_1_ = bf16[8,8,1024]{2,1,0:T(8,128)(2,1)S(1)} all-to-all(bf16[8,8,1024]{2,1,0:T(8,128)(2,1)S(1)} %shard_map.74), channel_id=1, replica_groups=mesh['section'=4,'blk'=8,'zlo'=2,'x'=4,'core'=2] {'blk'}, dimensions={0} | all-to-all | bytes 262144 | tf_op jit(solution)/shard_map/all_to_all | solution.py:378
  32.3 0.0 copy-start.1
  32.3 0.0 collective-permute-done.1.weights.refs_3_
  32.3 0.1 shard_map.75
  32.4 19.6 %all_to_all.16 = bf16[8,80,768]{2,1,0:T(8,128)(2,1)S(1)} all-to-all(bf16[8,80,768]{2,1,0:T(8,128)(2,1)S(1)} %shard_map.75), channel_id=1, replica_groups=mesh['section'=4,'blk'=8,'zlo'=2,'x'=4,'core'=2] {'zlo','x'}, dimensions={0} | all-to-all | bytes 1966080 | tf_op jit(solution)/shard_map/all_to_all | solution.py:380
  52.0 0.0 copy-done.1
  52.0 1.4 %shard_map.78 = (bf16[160,384]{1,0:T(8,128)(2,1)S(1)}, bf16[480,384]{1,0:T(8,128)(2,1)S(1)}) custom-call(s32[2]{0:T(128)S(1)} %pad_add_fusion.place.refs_0_, bf16[640,768]{1,0:T(8,128)(2,1)S(1)} %bitcast.15, bf16[3,3,768,128]{3,2,1,0:T(8,128)(2,1)S(1)} %bitcast.19, bf16[3,3,768,128]{3,2,1,0:T(8,128)(2,1)S(1)} %collective-permute-done.1.weights.refs_3_), custom_call_target="tpu_custom_call" | custom-call | flops 377487360 | bytes 4194304 | tf_op jit(solution)/shard_map/pallas_call | solution.py:204
  53.4 2.0 %collective-permute-start.6 = (bf16[480,384]{1,0:T(8,128)(2,1)S(1)}, bf16[480,384]{1,0:T(8,128)(2,1)S(1)}, u32[]{:S(2)}, u32[]{:S(2)}) collective-permute-start(bf16[480,384]{1,0:T(8,128)(2,1)S(1)} %get-tuple-element.22), channel_id=1, source_target_pairs={{0,112},{16,0},{32,16},{64,48},{80,64},{96,80},{1,113},{17,1},{33,... | collective-permute-start | bytes 1105928 | tf_op jit(solution)/shard_map/ppermute | solution.py:36
  55.4 3.8 %collective-permute-start.2 = (bf16[160,384]{1,0:T(8,128)(2,1)S(1)}, bf16[160,384]{1,0:T(8,128)(2,1)S(1)}, u32[]{:S(2)}, u32[]{:S(2)}) collective-permute-start(bf16[160,384]{1,0:T(8,128)(2,1)S(1)} %get-tuple-element.18), channel_id=1, source_target_pairs={{0,16},{16,32},{32,48},{64,80},{80,96},{96,112},{1,17},{17,33},{33... | collective-permute-start | bytes 368648 | tf_op jit(solution)/shard_map/ppermute | solution.py:36
  59.3 2.2 %shard_map.77 = (bf16[640,384]{1,0:T(8,128)(2,1)S(1)}, bf16[640,384]{1,0:T(8,128)(2,1)S(1)}) custom-call(s32[2]{0:T(128)S(1)} %pad_add_fusion.place.refs_0_, bf16[640,768]{1,0:T(8,128)(2,1)S(1)} %bitcast.16, bf16[3,3,768,128]{3,2,1,0:T(8,128)(2,1)S(1)} %bitcast.20, bf16[3,3,768,128]{3,2,1,0:T(8,128)(2,1)S(1)} %collective-permute-done.1.weights.refs_3_), custom_call_target="tpu_custom_call" | custom-call | flops 754974720 | bytes 4194304 | tf_op jit(solution)/shard_map/pallas_call | solution.py:204
  61.5 0.2 collective-permute-done.2.refs_1_
  61.7 0.1 shard_map.79
  61.8 1.3 %collective-permute-start.3 = (bf16[640,384]{1,0:T(8,128)(2,1)S(1)}, bf16[640,384]{1,0:T(8,128)(2,1)S(1)}, u32[]{:S(2)}, u32[]{:S(2)}) collective-permute-start(bf16[640,384]{1,0:T(8,128)(2,1)S(1)} %shard_map.79), channel_id=1, source_target_pairs={{16,32},{32,48},{48,64},{80,96},{96,112},{112,0},{17,33},{33,49},{... | collective-permute-start | bytes 1474568 | tf_op jit(solution)/shard_map/ppermute | solution.py:36
  63.1 0.0 collective-permute-done.6.refs_1_
  63.1 0.1 shard_map.82
  63.2 5.8 %collective-permute-start.7 = (bf16[640,384]{1,0:T(8,128)(2,1)S(1)}, bf16[640,384]{1,0:T(8,128)(2,1)S(1)}, u32[]{:S(2)}, u32[]{:S(2)}) collective-permute-start(bf16[640,384]{1,0:T(8,128)(2,1)S(1)} %shard_map.82), channel_id=1, source_target_pairs={{0,112},{16,0},{48,32},{64,48},{80,64},{112,96},{1,113},{17,1},{49... | collective-permute-start | bytes 1474568 | tf_op jit(solution)/shard_map/ppermute | solution.py:36
  68.9 4.6 %shard_map.76 = (bf16[640,384]{1,0:T(8,128)(2,1)S(1)}, bf16[640,384]{1,0:T(8,128)(2,1)S(1)}, bf16[640,384]{1,0:T(8,128)(2,1)S(1)}, bf16[640,384]{1,0:T(8,128)(2,1)S(1)}, bf16[640,384]{1,0:T(8,128)(2,1)S(1)}) custom-call(s32[2]{0:T(128)S(1)} %pad_add_fusion.place.refs_0_, bf16[640,768]{1,0:T(8,128)(2,1)S(1)} %bitcast.17, ...), custom_call_target="tpu_custom_call" | custom-call | flops 1887436800 | bytes 4194304 | tf_op jit(solution)/shard_map/pallas_call | solution.py:204
  73.5 0.4 collective-permute-done.3.refs_1_
  73.9 0.1 shard_map.80
  74.0 1.9 %collective-permute-start.4 = (bf16[640,384]{1,0:T(8,128)(2,1)S(1)}, bf16[640,384]{1,0:T(8,128)(2,1)S(1)}, u32[]{:S(2)}, u32[]{:S(2)}) collective-permute-start(bf16[640,384]{1,0:T(8,128)(2,1)S(1)} %shard_map.80), channel_id=1, source_target_pairs={{0,16},{32,48},{48,64},{64,80},{96,112},{112,0},{1,17},{33,49},{49... | collective-permute-start | bytes 1474568 | tf_op jit(solution)/shard_map/ppermute | solution.py:36
  76.0 0.0 collective-permute-done.7.refs_1_
  76.0 0.1 shard_map.83
  76.1 0.0 copy-start.3
  76.1 0.0 copy-start.4
  76.1 5.2 %collective-permute-start.8 = (bf16[640,384]{1,0:T(8,128)(2,1)S(1)}, bf16[640,384]{1,0:T(8,128)(2,1)S(1)}, u32[]{:S(2)}, u32[]{:S(2)}) collective-permute-start(bf16[640,384]{1,0:T(8,128)(2,1)S(1)} %shard_map.83), channel_id=1, source_target_pairs={{0,112},{32,16},{48,32},{64,48},{96,80},{112,96},{1,113},{33,17},{... | collective-permute-start | bytes 1474568 | tf_op jit(solution)/shard_map/ppermute | solution.py:36
  81.3 4.9 %collective-permute-done.4.refs_1_ = bf16[640,384]{1,0:T(8,128)(2,1)S(1)} collective-permute-done((bf16[640,384]{1,0:T(8,128)(2,1)S(1)}, bf16[640,384]{1,0:T(8,128)(2,1)S(1)}, u32[]{:S(2)}, u32[]{:S(2)}) %collective-permute-start.4) | collective-permute-done | bytes 491552 | tf_op jit(solution)/shard_map/ppermute | solution.py:36
  86.2 0.1 shard_map.81
  86.3 1.9 %collective-permute-start.5 = (bf16[640,384]{1,0:T(8,128)(2,1)S(1)}, bf16[640,384]{1,0:T(8,128)(2,1)S(1)}, u32[]{:S(2)}, u32[]{:S(2)}) collective-permute-start(bf16[640,384]{1,0:T(8,128)(2,1)S(1)} %shard_map.81), channel_id=1, source_target_pairs={{0,16},{16,32},{48,64},{64,80},{80,96},{112,0},{1,17},{17,33},{49,... | collective-permute-start | bytes 1474568 | tf_op jit(solution)/shard_map/ppermute | solution.py:36
  88.3 0.0 collective-permute-done.8.refs_1_
  88.3 0.1 shard_map.84
  88.4 1.3 %collective-permute-start.9 = (bf16[640,384]{1,0:T(8,128)(2,1)S(1)}, bf16[640,384]{1,0:T(8,128)(2,1)S(1)}, u32[]{:S(2)}, u32[]{:S(2)}) collective-permute-start(bf16[640,384]{1,0:T(8,128)(2,1)S(1)} %shard_map.84), channel_id=1, source_target_pairs={{16,0},{32,16},{48,32},{80,64},{96,80},{112,96},{17,1},{33,17},{49... | collective-permute-start | bytes 1474568 | tf_op jit(solution)/shard_map/ppermute | solution.py:36
  89.7 0.0 copy-done.3
  89.7 0.0 copy-done.4
  89.7 1.9 %collective-permute-start.10 = (f32[6,128]{1,0:T(8,128)S(1)}, f32[6,128]{1,0:T(8,128)S(1)}, u32[]{:S(2)}, u32[]{:S(2)}) collective-permute-start(f32[6,128]{1,0:T(8,128)S(1)} %shard_map.85.gains), channel_id=1, source_target_pairs={{0,1},{1,0},{2,3},{3,2},{4,5},{5,4},{6,7},{7,6},{8,9},{9,8},{10,11... | collective-permute-start | bytes 9224 | tf_op jit(solution)/shard_map/ppermute | solution.py:20
  91.7 1.1 collective-permute-done.10.theirs
  92.8 5.5 %collective-permute-done.5.second = bf16[640,384]{1,0:T(8,128)(2,1)S(1)} collective-permute-done((bf16[640,384]{1,0:T(8,128)(2,1)S(1)}, bf16[640,384]{1,0:T(8,128)(2,1)S(1)}, u32[]{:S(2)}, u32[]{:S(2)}) %collective-permute-start.5) | collective-permute-done | bytes 491552 | tf_op jit(solution)/shard_map/ppermute | solution.py:36
  98.3 0.9 collective-permute-done.9.third
  99.1 0.8 shard_map.87.refs_3_
  99.9 1.9 %collective-permute-start.11 = (bf16[640,256]{1,0:T(8,128)(2,1)S(1)}, bf16[640,256]{1,0:T(8,128)(2,1)S(1)}, u32[]{:S(2)}, u32[]{:S(2)}) collective-permute-start(bf16[640,256]{1,0:T(8,128)(2,1)S(1)} %shard_map.87.refs_3_), channel_id=1, source_target_pairs={{0,1},{1,0},{2,3},{3,2},{4,5},{5,4},{6,7},{7,6},{8,9},{9,8},{10,11... | collective-permute-start | bytes 983048 | tf_op jit(solution)/shard_map/ppermute | solution.py:20
  101.9 0.7 shard_map.86.refs_2_
  102.6 0.9 collective-permute-done.11.refs_4_
  103.5 2.1 %shard_map.88 = bf16[64,10,128]{2,1,0:T(8,128)(2,1)S(1)} custom-call(s32[2]{0:T(128)S(1)} %pad_add_fusion.place.refs_0_, bf16[8,8,1024]{2,1,0:T(8,128)(2,1)S(1)} %all_to_all.15.sliced.refs_1_, bf16[640,128]{1,0:T(8,128)(2,1)S(1)} %shard_map.86.refs_2_, bf16[640,256]{1,0:T(8,128)(2,1)S(1)} %shard_map.87.refs_3_, ...), custom_call_target="tpu_custom_call" | custom-call | flops 419430400 | bytes 1048576 | tf_op jit(solution)/shard_map/pallas_call | solution.py:327
  105.6 20.5 %all_to_all.17 = bf16[64,10,128]{2,1,0:T(8,128)(2,1)S(1)} all-to-all(bf16[64,10,128]{2,1,0:T(8,128)(2,1)S(1)} %shard_map.88), channel_id=1, replica_groups=mesh['section'=4,'blk'=8,'zlo'=2,'x'=4,'core'=2] {'blk','zlo','x'}, dimensions={0} | all-to-all | bytes 327680 | tf_op jit(solution)/shard_map/all_to_all | solution.py:397
  126.1 0.7 shard_map.89
  (3 shorter events, 0.1 us)
Async XLA Ops:
  0.0 9.7 %copy-start = (f32[16,2,6144]{2,1,0:T(2,128)S(1)}, f32[16,2,6144]{2,1,0:T(2,128)}, u32[]{:S(2)}) copy-start(f32[16,2,6144]{2,1,0:T(2,128)} %param.9) | copy-start | bytes 2359300
  0.0 1.0 copy-start.2
  1.0 14.6 %collective-permute-start = (bf16[8,8,1024]{2,1,0:T(8,128)(2,1)S(1)}, bf16[8,8,1024]{2,1,0:T(8,128)(2,1)S(1)}, u32[]{:S(2)}, u32[]{:S(2)}) collective-permute-start(bf16[8,8,1024]{2,1,0:T(8,128)(2,1)S(1)} %shard_map.73), channel_id=1, source_target_pairs={{0,128},{128,256},{256,384},{384,0},{1,129},{129,257},{257,385},{3... | collective-permute-start | bytes 393224 | tf_op jit(solution)/shard_map/ppermute | solution.py:20
  7.1 25.1 %collective-permute-start.1 = (bf16[3,3,768,128]{3,2,1,0:T(8,128)(2,1)}, bf16[3,3,768,128]{3,2,1,0:T(8,128)(2,1)S(1)}, u32[]{:S(2)}, u32[]{:S(2)}) collective-permute-start(bf16[3,3,768,128]{3,2,1,0:T(8,128)(2,1)} %bitcast.18), channel_id=1, source_target_pairs={{0,1},{1,0},{2,3},{3,2},{4,5},{5,4},{6,7},{7,6},{8,9},{9,8},{10,11... | collective-permute-start | bytes 5308424 | tf_op jit(solution)/shard_map/ppermute | solution.py:20
  32.3 19.8 %copy-start.1 = (bf16[1,768,3,3,128]{4,1,3,2,0:T(8,128)(2,1)S(1)}, bf16[1,768,3,3,128]{4,1,3,2,0:T(8,128)(2,1)}, u32[]{:S(2)}) copy-start(bf16[1,768,3,3,128]{4,1,3,2,0:T(8,128)(2,1)} %param.10) | copy-start | bytes 5308420
  53.4 9.6 %collective-permute-start.6 = (bf16[480,384]{1,0:T(8,128)(2,1)S(1)}, bf16[480,384]{1,0:T(8,128)(2,1)S(1)}, u32[]{:S(2)}, u32[]{:S(2)}) collective-permute-start(bf16[480,384]{1,0:T(8,128)(2,1)S(1)} %get-tuple-element.22), channel_id=1, source_target_pairs={{0,112},{16,0},{32,16},{64,48},{80,64},{96,80},{1,113},{17,1},{33,... | collective-permute-start | bytes 1105928 | tf_op jit(solution)/shard_map/ppermute | solution.py:36
  55.4 6.3 %collective-permute-start.2 = (bf16[160,384]{1,0:T(8,128)(2,1)S(1)}, bf16[160,384]{1,0:T(8,128)(2,1)S(1)}, u32[]{:S(2)}, u32[]{:S(2)}) collective-permute-start(bf16[160,384]{1,0:T(8,128)(2,1)S(1)} %get-tuple-element.18), channel_id=1, source_target_pairs={{0,16},{16,32},{32,48},{64,80},{80,96},{96,112},{1,17},{17,33},{33... | collective-permute-start | bytes 368648 | tf_op jit(solution)/shard_map/ppermute | solution.py:36
  61.8 12.2 %collective-permute-start.3 = (bf16[640,384]{1,0:T(8,128)(2,1)S(1)}, bf16[640,384]{1,0:T(8,128)(2,1)S(1)}, u32[]{:S(2)}, u32[]{:S(2)}) collective-permute-start(bf16[640,384]{1,0:T(8,128)(2,1)S(1)} %shard_map.79), channel_id=1, source_target_pairs={{16,32},{32,48},{48,64},{80,96},{96,112},{112,0},{17,33},{33,49},{... | collective-permute-start | bytes 1474568 | tf_op jit(solution)/shard_map/ppermute | solution.py:36
  63.2 12.8 %collective-permute-start.7 = (bf16[640,384]{1,0:T(8,128)(2,1)S(1)}, bf16[640,384]{1,0:T(8,128)(2,1)S(1)}, u32[]{:S(2)}, u32[]{:S(2)}) collective-permute-start(bf16[640,384]{1,0:T(8,128)(2,1)S(1)} %shard_map.82), channel_id=1, source_target_pairs={{0,112},{16,0},{48,32},{64,48},{80,64},{112,96},{1,113},{17,1},{49... | collective-permute-start | bytes 1474568 | tf_op jit(solution)/shard_map/ppermute | solution.py:36
  74.0 12.2 %collective-permute-start.4 = (bf16[640,384]{1,0:T(8,128)(2,1)S(1)}, bf16[640,384]{1,0:T(8,128)(2,1)S(1)}, u32[]{:S(2)}, u32[]{:S(2)}) collective-permute-start(bf16[640,384]{1,0:T(8,128)(2,1)S(1)} %shard_map.80), channel_id=1, source_target_pairs={{0,16},{32,48},{48,64},{64,80},{96,112},{112,0},{1,17},{33,49},{49... | collective-permute-start | bytes 1474568 | tf_op jit(solution)/shard_map/ppermute | solution.py:36
  76.1 13.6 %copy-start.3 = (f32[1,3,128]{2,0,1:T(1,128)S(1)}, f32[1,3,128]{2,0,1:T(1,128)}, u32[]{:S(2)}) copy-start(f32[1,3,128]{2,0,1:T(1,128)} %param.11) | copy-start | bytes 4612
  76.1 13.6 %copy-start.4 = (f32[1,3,128]{2,0,1:T(1,128)S(1)}, f32[1,3,128]{2,0,1:T(1,128)}, u32[]{:S(2)}) copy-start(f32[1,3,128]{2,0,1:T(1,128)} %param.12) | copy-start | bytes 4612
  76.1 12.1 %collective-permute-start.8 = (bf16[640,384]{1,0:T(8,128)(2,1)S(1)}, bf16[640,384]{1,0:T(8,128)(2,1)S(1)}, u32[]{:S(2)}, u32[]{:S(2)}) collective-permute-start(bf16[640,384]{1,0:T(8,128)(2,1)S(1)} %shard_map.83), channel_id=1, source_target_pairs={{0,112},{32,16},{48,32},{64,48},{96,80},{112,96},{1,113},{33,17},{... | collective-permute-start | bytes 1474568 | tf_op jit(solution)/shard_map/ppermute | solution.py:36
  86.3 11.9 %collective-permute-start.5 = (bf16[640,384]{1,0:T(8,128)(2,1)S(1)}, bf16[640,384]{1,0:T(8,128)(2,1)S(1)}, u32[]{:S(2)}, u32[]{:S(2)}) collective-permute-start(bf16[640,384]{1,0:T(8,128)(2,1)S(1)} %shard_map.81), channel_id=1, source_target_pairs={{0,16},{16,32},{48,64},{64,80},{80,96},{112,0},{1,17},{17,33},{49,... | collective-permute-start | bytes 1474568 | tf_op jit(solution)/shard_map/ppermute | solution.py:36
  88.4 10.7 %collective-permute-start.9 = (bf16[640,384]{1,0:T(8,128)(2,1)S(1)}, bf16[640,384]{1,0:T(8,128)(2,1)S(1)}, u32[]{:S(2)}, u32[]{:S(2)}) collective-permute-start(bf16[640,384]{1,0:T(8,128)(2,1)S(1)} %shard_map.84), channel_id=1, source_target_pairs={{16,0},{32,16},{48,32},{80,64},{96,80},{112,96},{17,1},{33,17},{49... | collective-permute-start | bytes 1474568 | tf_op jit(solution)/shard_map/ppermute | solution.py:36
  89.7 3.1 %collective-permute-start.10 = (f32[6,128]{1,0:T(8,128)S(1)}, f32[6,128]{1,0:T(8,128)S(1)}, u32[]{:S(2)}, u32[]{:S(2)}) collective-permute-start(f32[6,128]{1,0:T(8,128)S(1)} %shard_map.85.gains), channel_id=1, source_target_pairs={{0,1},{1,0},{2,3},{3,2},{4,5},{5,4},{6,7},{7,6},{8,9},{9,8},{10,11... | collective-permute-start | bytes 9224 | tf_op jit(solution)/shard_map/ppermute | solution.py:20
  99.9 3.5 %collective-permute-start.11 = (bf16[640,256]{1,0:T(8,128)(2,1)S(1)}, bf16[640,256]{1,0:T(8,128)(2,1)S(1)}, u32[]{:S(2)}, u32[]{:S(2)}) collective-permute-start(bf16[640,256]{1,0:T(8,128)(2,1)S(1)} %shard_map.87.refs_3_), channel_id=1, source_target_pairs={{0,1},{1,0},{2,3},{3,2},{4,5},{5,4},{6,7},{7,6},{8,9},{9,8},{10,11... | collective-permute-start | bytes 983048 | tf_op jit(solution)/shard_map/ppermute | solution.py:20

commit v9 on v8

--- a/solution.py
+++ b/solution.py
@@ -380,7 +380,7 @@
     tokens = lax.all_to_all(copies, CHIPS, 0, 0, tiled=False)
     tokens = tokens.reshape(chips * blks * tok_rows, slice_width)
     rows = tokens.shape[0]
-    cut = rows // 4
+    cut = rows // 5
 
     up, down = products((4,), place, tokens, own, other, (cut, rows - cut))
     up, down = passed(up, 1, 4), passed(down, -1, 4)

time: 127 us -> 128 us (level)
  no operation moved by 1% of the time
where the time goes in v9:
time: 128 us; the launch traced here: 127 us
  blocking collectives  56.5 us (44%)
  starting transfers between devices  34.8 us (27%)
  waiting for transfers between devices  19 us (15%)
  Pallas kernels  14 us (11%)
  between operations  1.56 us (1%)
    ppermute x8, starting transfers between devices, passed(): return lax.ppermute(value, 'blk', pairs)  23 us
    all_to_all x1, blocking collectives, on_device(): returned = lax.all_to_all(mixed, ('blk',) + CHIPS, 0, 0, tiled=False)  20.9 us
    all_to_all x1, blocking collectives, on_device(): tokens = lax.all_to_all(copies, CHIPS, 0, 0, tiled=False)  19.6 us
    all_to_all x1, blocking collectives, on_device(): sliced = lax.all_to_all(sent, 'blk', 0, 0, tiled=False)  16 us
    ppermute x4, starting transfers between devices, shifted(): return lax.ppermute(value, axis, pairs)  11.9 us
    ppermute x8, waiting for transfers between devices, passed(): return lax.ppermute(value, 'blk', pairs)  11.8 us
    pallas_call x3, Pallas kernels, products(): pl.pallas_call(lambda *refs: product_kernel(steps, *refs), out_shape=shap...  8.19 us
    ppermute x4, waiting for transfers between devices, shifted(): return lax.ppermute(value, axis, pairs)  7.12 us
  transfers between devices with their start and end apart: 12, of which 8 were waited for; matrix products, arithmetic and copies ran while one was open for 0% of the time, Pallas kernels for 7%

profile of v9, /device:TPU:6, one launch (start us, length us, event | category | flops | bytes accessed | tf_op | source)
XLA Modules:
  0.0 127.0 jit_solution(6187716135708905317)
XLA Ops:
  0.0 0.0 copy-start
  0.0 0.0 copy-start.2
  0.0 1.0 copy-done.2
  1.0 6.1 %collective-permute-start = (bf16[8,8,1024]{2,1,0:T(8,128)(2,1)S(1)}, bf16[8,8,1024]{2,1,0:T(8,128)(2,1)S(1)}, u32[]{:S(2)}, u32[]{:S(2)}) collective-permute-start(bf16[8,8,1024]{2,1,0:T(8,128)(2,1)S(1)} %shard_map.73), channel_id=1, source_target_pairs={{0,128},{128,256},{256,384},{384,0},{1,129},{129,257},{257,385},{3... | collective-permute-start | bytes 393224 | tf_op jit(solution)/shard_map/ppermute | solution.py:20
  7.1 1.9 %collective-permute-start.1 = (bf16[3,3,768,128]{3,2,1,0:T(8,128)(2,1)}, bf16[3,3,768,128]{3,2,1,0:T(8,128)(2,1)S(1)}, u32[]{:S(2)}, u32[]{:S(2)}) collective-permute-start(bf16[3,3,768,128]{3,2,1,0:T(8,128)(2,1)} %bitcast.18), channel_id=1, source_target_pairs={{0,1},{1,0},{2,3},{3,2},{4,5},{5,4},{6,7},{7,6},{8,9},{9,8},{10,11... | collective-permute-start | bytes 5308424 | tf_op jit(solution)/shard_map/ppermute | solution.py:20
  9.7 0.0 copy-done
  10.4 0.1 pad_add_fusion.place.refs_0_
  10.5 5.1 %collective-permute-done.stale = bf16[8,8,1024]{2,1,0:T(8,128)(2,1)S(1)} collective-permute-done((bf16[8,8,1024]{2,1,0:T(8,128)(2,1)S(1)}, bf16[8,8,1024]{2,1,0:T(8,128)(2,1)S(1)}, u32[]{:S(2)}, u32[]{:S(2)}) %collective-permute-start) | collective-permute-done | bytes 131104 | tf_op jit(solution)/shard_map/ppermute | solution.py:20
  15.6 0.7 shard_map.74
  16.3 16.0 %all_to_all.15.sliced.refs_1_ = bf16[8,8,1024]{2,1,0:T(8,128)(2,1)S(1)} all-to-all(bf16[8,8,1024]{2,1,0:T(8,128)(2,1)S(1)} %shard_map.74), channel_id=1, replica_groups=mesh['section'=4,'blk'=8,'zlo'=2,'x'=4,'core'=2] {'blk'}, dimensions={0} | all-to-all | bytes 262144 | tf_op jit(solution)/shard_map/all_to_all | solution.py:378
  32.3 0.0 copy-start.1
  32.3 0.0 collective-permute-done.1.weights.refs_3_
  32.3 0.1 shard_map.75
  32.4 19.6 %all_to_all.16 = bf16[8,80,768]{2,1,0:T(8,128)(2,1)S(1)} all-to-all(bf16[8,80,768]{2,1,0:T(8,128)(2,1)S(1)} %shard_map.75), channel_id=1, replica_groups=mesh['section'=4,'blk'=8,'zlo'=2,'x'=4,'core'=2] {'zlo','x'}, dimensions={0} | all-to-all | bytes 1966080 | tf_op jit(solution)/shard_map/all_to_all | solution.py:380
  52.0 0.0 copy-done.1
  52.0 1.4 %shard_map.78 = (bf16[128,384]{1,0:T(8,128)(2,1)S(1)}, bf16[512,384]{1,0:T(8,128)(2,1)S(1)}) custom-call(s32[2]{0:T(128)S(1)} %pad_add_fusion.place.refs_0_, bf16[640,768]{1,0:T(8,128)(2,1)S(1)} %bitcast.15, bf16[3,3,768,128]{3,2,1,0:T(8,128)(2,1)S(1)} %bitcast.19, bf16[3,3,768,128]{3,2,1,0:T(8,128)(2,1)S(1)} %collective-permute-done.1.weights.refs_3_), custom_call_target="tpu_custom_call" | custom-call | flops 377487360 | bytes 4194304 | tf_op jit(solution)/shard_map/pallas_call | solution.py:204
  53.4 2.0 %collective-permute-start.6 = (bf16[512,384]{1,0:T(8,128)(2,1)S(1)}, bf16[512,384]{1,0:T(8,128)(2,1)S(1)}, u32[]{:S(2)}, u32[]{:S(2)}) collective-permute-start(bf16[512,384]{1,0:T(8,128)(2,1)S(1)} %get-tuple-element.22), channel_id=1, source_target_pairs={{0,112},{16,0},{32,16},{64,48},{80,64},{96,80},{1,113},{17,1},{33,... | collective-permute-start | bytes 1179656 | tf_op jit(solution)/shard_map/ppermute | solution.py:36
  55.4 3.8 %collective-permute-start.2 = (bf16[128,384]{1,0:T(8,128)(2,1)S(1)}, bf16[128,384]{1,0:T(8,128)(2,1)S(1)}, u32[]{:S(2)}, u32[]{:S(2)}) collective-permute-start(bf16[128,384]{1,0:T(8,128)(2,1)S(1)} %get-tuple-element.18), channel_id=1, source_target_pairs={{0,16},{16,32},{32,48},{64,80},{80,96},{96,112},{1,17},{17,33},{33... | collective-permute-start | bytes 294920 | tf_op jit(solution)/shard_map/ppermute | solution.py:36
  59.3 2.2 %shard_map.77 = (bf16[640,384]{1,0:T(8,128)(2,1)S(1)}, bf16[640,384]{1,0:T(8,128)(2,1)S(1)}) custom-call(s32[2]{0:T(128)S(1)} %pad_add_fusion.place.refs_0_, bf16[640,768]{1,0:T(8,128)(2,1)S(1)} %bitcast.16, bf16[3,3,768,128]{3,2,1,0:T(8,128)(2,1)S(1)} %bitcast.20, bf16[3,3,768,128]{3,2,1,0:T(8,128)(2,1)S(1)} %collective-permute-done.1.weights.refs_3_), custom_call_target="tpu_custom_call" | custom-call | flops 754974720 | bytes 4194304 | tf_op jit(solution)/shard_map/pallas_call | solution.py:204
  61.5 0.0 collective-permute-done.2.refs_1_
  61.6 1.3 %collective-permute-start.3 = (bf16[640,384]{1,0:T(8,128)(2,1)S(1)}, bf16[640,384]{1,0:T(8,128)(2,1)S(1)}, u32[]{:S(2)}, u32[]{:S(2)}) collective-permute-start(bf16[640,384]{1,0:T(8,128)(2,1)S(1)} %shard_map.79), channel_id=1, source_target_pairs={{16,32},{32,48},{48,64},{80,96},{96,112},{112,0},{17,33},{33,49},{... | collective-permute-start | bytes 1474568 | tf_op jit(solution)/shard_map/ppermute | solution.py:36
  62.9 0.2 collective-permute-done.6.refs_1_
  63.1 0.1 shard_map.82
  63.2 5.5 %collective-permute-start.7 = (bf16[640,384]{1,0:T(8,128)(2,1)S(1)}, bf16[640,384]{1,0:T(8,128)(2,1)S(1)}, u32[]{:S(2)}, u32[]{:S(2)}) collective-permute-start(bf16[640,384]{1,0:T(8,128)(2,1)S(1)} %shard_map.82), channel_id=1, source_target_pairs={{0,112},{16,0},{48,32},{64,48},{80,64},{112,96},{1,113},{17,1},{49... | collective-permute-start | bytes 1474568 | tf_op jit(solution)/shard_map/ppermute | solution.py:36
  68.7 4.6 %shard_map.76 = (bf16[640,384]{1,0:T(8,128)(2,1)S(1)}, bf16[640,384]{1,0:T(8,128)(2,1)S(1)}, bf16[640,384]{1,0:T(8,128)(2,1)S(1)}, bf16[640,384]{1,0:T(8,128)(2,1)S(1)}, bf16[640,384]{1,0:T(8,128)(2,1)S(1)}) custom-call(s32[2]{0:T(128)S(1)} %pad_add_fusion.place.refs_0_, bf16[640,768]{1,0:T(8,128)(2,1)S(1)} %bitcast.17, ...), custom_call_target="tpu_custom_call" | custom-call | flops 1887436800 | bytes 4194304 | tf_op jit(solution)/shard_map/pallas_call | solution.py:204
  73.4 0.6 collective-permute-done.3.refs_1_
  73.9 0.1 shard_map.80
  74.0 1.9 %collective-permute-start.4 = (bf16[640,384]{1,0:T(8,128)(2,1)S(1)}, bf16[640,384]{1,0:T(8,128)(2,1)S(1)}, u32[]{:S(2)}, u32[]{:S(2)}) collective-permute-start(bf16[640,384]{1,0:T(8,128)(2,1)S(1)} %shard_map.80), channel_id=1, source_target_pairs={{0,16},{32,48},{48,64},{64,80},{96,112},{112,0},{1,17},{33,49},{49... | collective-permute-start | bytes 1474568 | tf_op jit(solution)/shard_map/ppermute | solution.py:36
  76.0 0.0 collective-permute-done.7.refs_1_
  76.0 0.1 shard_map.83
  76.1 0.0 copy-start.3
  76.1 0.0 copy-start.4
  76.1 5.2 %collective-permute-start.8 = (bf16[640,384]{1,0:T(8,128)(2,1)S(1)}, bf16[640,384]{1,0:T(8,128)(2,1)S(1)}, u32[]{:S(2)}, u32[]{:S(2)}) collective-permute-start(bf16[640,384]{1,0:T(8,128)(2,1)S(1)} %shard_map.83), channel_id=1, source_target_pairs={{0,112},{32,16},{48,32},{64,48},{96,80},{112,96},{1,113},{33,17},{... | collective-permute-start | bytes 1474568 | tf_op jit(solution)/shard_map/ppermute | solution.py:36
  81.3 4.7 %collective-permute-done.4.refs_1_ = bf16[640,384]{1,0:T(8,128)(2,1)S(1)} collective-permute-done((bf16[640,384]{1,0:T(8,128)(2,1)S(1)}, bf16[640,384]{1,0:T(8,128)(2,1)S(1)}, u32[]{:S(2)}, u32[]{:S(2)}) %collective-permute-start.4) | collective-permute-done | bytes 491552 | tf_op jit(solution)/shard_map/ppermute | solution.py:36
  86.0 0.1 shard_map.81
  86.2 1.9 %collective-permute-start.5 = (bf16[640,384]{1,0:T(8,128)(2,1)S(1)}, bf16[640,384]{1,0:T(8,128)(2,1)S(1)}, u32[]{:S(2)}, u32[]{:S(2)}) collective-permute-start(bf16[640,384]{1,0:T(8,128)(2,1)S(1)} %shard_map.81), channel_id=1, source_target_pairs={{0,16},{16,32},{48,64},{64,80},{80,96},{112,0},{1,17},{17,33},{49,... | collective-permute-start | bytes 1474568 | tf_op jit(solution)/shard_map/ppermute | solution.py:36
  88.1 0.0 collective-permute-done.8.refs_1_
  88.1 0.1 shard_map.84
  88.2 1.3 %collective-permute-start.9 = (bf16[640,384]{1,0:T(8,128)(2,1)S(1)}, bf16[640,384]{1,0:T(8,128)(2,1)S(1)}, u32[]{:S(2)}, u32[]{:S(2)}) collective-permute-start(bf16[640,384]{1,0:T(8,128)(2,1)S(1)} %shard_map.84), channel_id=1, source_target_pairs={{16,0},{32,16},{48,32},{80,64},{96,80},{112,96},{17,1},{33,17},{49... | collective-permute-start | bytes 1474568 | tf_op jit(solution)/shard_map/ppermute | solution.py:36
  89.5 0.0 copy-done.3
  89.5 0.0 copy-done.4
  89.6 1.9 %collective-permute-start.10 = (f32[6,128]{1,0:T(8,128)S(1)}, f32[6,128]{1,0:T(8,128)S(1)}, u32[]{:S(2)}, u32[]{:S(2)}) collective-permute-start(f32[6,128]{1,0:T(8,128)S(1)} %shard_map.85.gains), channel_id=1, source_target_pairs={{0,1},{1,0},{2,3},{3,2},{4,5},{5,4},{6,7},{7,6},{8,9},{9,8},{10,11... | collective-permute-start | bytes 9224 | tf_op jit(solution)/shard_map/ppermute | solution.py:20
  91.5 1.1 collective-permute-done.10.theirs
  92.6 5.5 %collective-permute-done.5.second = bf16[640,384]{1,0:T(8,128)(2,1)S(1)} collective-permute-done((bf16[640,384]{1,0:T(8,128)(2,1)S(1)}, bf16[640,384]{1,0:T(8,128)(2,1)S(1)}, u32[]{:S(2)}, u32[]{:S(2)}) %collective-permute-start.5) | collective-permute-done | bytes 491552 | tf_op jit(solution)/shard_map/ppermute | solution.py:36
  98.1 0.9 collective-permute-done.9.third
  98.9 0.8 shard_map.87.refs_3_
  99.8 1.9 %collective-permute-start.11 = (bf16[640,256]{1,0:T(8,128)(2,1)S(1)}, bf16[640,256]{1,0:T(8,128)(2,1)S(1)}, u32[]{:S(2)}, u32[]{:S(2)}) collective-permute-start(bf16[640,256]{1,0:T(8,128)(2,1)S(1)} %shard_map.87.refs_3_), channel_id=1, source_target_pairs={{0,1},{1,0},{2,3},{3,2},{4,5},{5,4},{6,7},{7,6},{8,9},{9,8},{10,11... | collective-permute-start | bytes 983048 | tf_op jit(solution)/shard_map/ppermute | solution.py:20
  101.7 0.7 shard_map.86.refs_2_
  102.4 0.9 collective-permute-done.11.refs_4_
  103.3 2.1 %shard_map.88 = bf16[64,10,128]{2,1,0:T(8,128)(2,1)S(1)} custom-call(s32[2]{0:T(128)S(1)} %pad_add_fusion.place.refs_0_, bf16[8,8,1024]{2,1,0:T(8,128)(2,1)S(1)} %all_to_all.15.sliced.refs_1_, bf16[640,128]{1,0:T(8,128)(2,1)S(1)} %shard_map.86.refs_2_, bf16[640,256]{1,0:T(8,128)(2,1)S(1)} %shard_map.87.refs_3_, ...), custom_call_target="tpu_custom_call" | custom-call | flops 419430400 | bytes 1048576 | tf_op jit(solution)/shard_map/pallas_call | solution.py:327
  105.4 20.9 %all_to_all.17 = bf16[64,10,128]{2,1,0:T(8,128)(2,1)S(1)} all-to-all(bf16[64,10,128]{2,1,0:T(8,128)(2,1)S(1)} %shard_map.88), channel_id=1, replica_groups=mesh['section'=4,'blk'=8,'zlo'=2,'x'=4,'core'=2] {'blk','zlo','x'}, dimensions={0} | all-to-all | bytes 327680 | tf_op jit(solution)/shard_map/all_to_all | solution.py:397
  126.3 0.7 shard_map.89
  (4 shorter events, 0.1 us)
Async XLA Ops:
  0.0 9.7 %copy-start = (f32[16,2,6144]{2,1,0:T(2,128)S(1)}, f32[16,2,6144]{2,1,0:T(2,128)}, u32[]{:S(2)}) copy-start(f32[16,2,6144]{2,1,0:T(2,128)} %param.9) | copy-start | bytes 2359300
  0.0 1.0 copy-start.2
  1.0 14.6 %collective-permute-start = (bf16[8,8,1024]{2,1,0:T(8,128)(2,1)S(1)}, bf16[8,8,1024]{2,1,0:T(8,128)(2,1)S(1)}, u32[]{:S(2)}, u32[]{:S(2)}) collective-permute-start(bf16[8,8,1024]{2,1,0:T(8,128)(2,1)S(1)} %shard_map.73), channel_id=1, source_target_pairs={{0,128},{128,256},{256,384},{384,0},{1,129},{129,257},{257,385},{3... | collective-permute-start | bytes 393224 | tf_op jit(solution)/shard_map/ppermute | solution.py:20
  7.1 25.1 %collective-permute-start.1 = (bf16[3,3,768,128]{3,2,1,0:T(8,128)(2,1)}, bf16[3,3,768,128]{3,2,1,0:T(8,128)(2,1)S(1)}, u32[]{:S(2)}, u32[]{:S(2)}) collective-permute-start(bf16[3,3,768,128]{3,2,1,0:T(8,128)(2,1)} %bitcast.18), channel_id=1, source_target_pairs={{0,1},{1,0},{2,3},{3,2},{4,5},{5,4},{6,7},{7,6},{8,9},{9,8},{10,11... | collective-permute-start | bytes 5308424 | tf_op jit(solution)/shard_map/ppermute | solution.py:20
  32.3 19.8 %copy-start.1 = (bf16[1,768,3,3,128]{4,1,3,2,0:T(8,128)(2,1)S(1)}, bf16[1,768,3,3,128]{4,1,3,2,0:T(8,128)(2,1)}, u32[]{:S(2)}) copy-start(bf16[1,768,3,3,128]{4,1,3,2,0:T(8,128)(2,1)} %param.10) | copy-start | bytes 5308420
  53.4 9.7 %collective-permute-start.6 = (bf16[512,384]{1,0:T(8,128)(2,1)S(1)}, bf16[512,384]{1,0:T(8,128)(2,1)S(1)}, u32[]{:S(2)}, u32[]{:S(2)}) collective-permute-start(bf16[512,384]{1,0:T(8,128)(2,1)S(1)} %get-tuple-element.22), channel_id=1, source_target_pairs={{0,112},{16,0},{32,16},{64,48},{80,64},{96,80},{1,113},{17,1},{33,... | collective-permute-start | bytes 1179656 | tf_op jit(solution)/shard_map/ppermute | solution.py:36
  55.4 6.1 %collective-permute-start.2 = (bf16[128,384]{1,0:T(8,128)(2,1)S(1)}, bf16[128,384]{1,0:T(8,128)(2,1)S(1)}, u32[]{:S(2)}, u32[]{:S(2)}) collective-permute-start(bf16[128,384]{1,0:T(8,128)(2,1)S(1)} %get-tuple-element.18), channel_id=1, source_target_pairs={{0,16},{16,32},{32,48},{64,80},{80,96},{96,112},{1,17},{17,33},{33... | collective-permute-start | bytes 294920 | tf_op jit(solution)/shard_map/ppermute | solution.py:36
  61.6 12.4 %collective-permute-start.3 = (bf16[640,384]{1,0:T(8,128)(2,1)S(1)}, bf16[640,384]{1,0:T(8,128)(2,1)S(1)}, u32[]{:S(2)}, u32[]{:S(2)}) collective-permute-start(bf16[640,384]{1,0:T(8,128)(2,1)S(1)} %shard_map.79), channel_id=1, source_target_pairs={{16,32},{32,48},{48,64},{80,96},{96,112},{112,0},{17,33},{33,49},{... | collective-permute-start | bytes 1474568 | tf_op jit(solution)/shard_map/ppermute | solution.py:36
  63.2 12.8 %collective-permute-start.7 = (bf16[640,384]{1,0:T(8,128)(2,1)S(1)}, bf16[640,384]{1,0:T(8,128)(2,1)S(1)}, u32[]{:S(2)}, u32[]{:S(2)}) collective-permute-start(bf16[640,384]{1,0:T(8,128)(2,1)S(1)} %shard_map.82), channel_id=1, source_target_pairs={{0,112},{16,0},{48,32},{64,48},{80,64},{112,96},{1,113},{17,1},{49... | collective-permute-start | bytes 1474568 | tf_op jit(solution)/shard_map/ppermute | solution.py:36
  74.0 12.0 %collective-permute-start.4 = (bf16[640,384]{1,0:T(8,128)(2,1)S(1)}, bf16[640,384]{1,0:T(8,128)(2,1)S(1)}, u32[]{:S(2)}, u32[]{:S(2)}) collective-permute-start(bf16[640,384]{1,0:T(8,128)(2,1)S(1)} %shard_map.80), channel_id=1, source_target_pairs={{0,16},{32,48},{48,64},{64,80},{96,112},{112,0},{1,17},{33,49},{49... | collective-permute-start | bytes 1474568 | tf_op jit(solution)/shard_map/ppermute | solution.py:36
  76.1 13.4 %copy-start.3 = (f32[1,3,128]{2,0,1:T(1,128)S(1)}, f32[1,3,128]{2,0,1:T(1,128)}, u32[]{:S(2)}) copy-start(f32[1,3,128]{2,0,1:T(1,128)} %param.11) | copy-start | bytes 4612
  76.1 13.4 %copy-start.4 = (f32[1,3,128]{2,0,1:T(1,128)S(1)}, f32[1,3,128]{2,0,1:T(1,128)}, u32[]{:S(2)}) copy-start(f32[1,3,128]{2,0,1:T(1,128)} %param.12) | copy-start | bytes 4612
  76.1 12.0 %collective-permute-start.8 = (bf16[640,384]{1,0:T(8,128)(2,1)S(1)}, bf16[640,384]{1,0:T(8,128)(2,1)S(1)}, u32[]{:S(2)}, u32[]{:S(2)}) collective-permute-start(bf16[640,384]{1,0:T(8,128)(2,1)S(1)} %shard_map.83), channel_id=1, source_target_pairs={{0,112},{32,16},{48,32},{64,48},{96,80},{112,96},{1,113},{33,17},{... | collective-permute-start | bytes 1474568 | tf_op jit(solution)/shard_map/ppermute | solution.py:36
  86.2 11.9 %collective-permute-start.5 = (bf16[640,384]{1,0:T(8,128)(2,1)S(1)}, bf16[640,384]{1,0:T(8,128)(2,1)S(1)}, u32[]{:S(2)}, u32[]{:S(2)}) collective-permute-start(bf16[640,384]{1,0:T(8,128)(2,1)S(1)} %shard_map.81), channel_id=1, source_target_pairs={{0,16},{16,32},{48,64},{64,80},{80,96},{112,0},{1,17},{17,33},{49,... | collective-permute-start | bytes 1474568 | tf_op jit(solution)/shard_map/ppermute | solution.py:36
  88.2 10.7 %collective-permute-start.9 = (bf16[640,384]{1,0:T(8,128)(2,1)S(1)}, bf16[640,384]{1,0:T(8,128)(2,1)S(1)}, u32[]{:S(2)}, u32[]{:S(2)}) collective-permute-start(bf16[640,384]{1,0:T(8,128)(2,1)S(1)} %shard_map.84), channel_id=1, source_target_pairs={{16,0},{32,16},{48,32},{80,64},{96,80},{112,96},{17,1},{33,17},{49... | collective-permute-start | bytes 1474568 | tf_op jit(solution)/shard_map/ppermute | solution.py:36
  89.6 3.1 %collective-permute-start.10 = (f32[6,128]{1,0:T(8,128)S(1)}, f32[6,128]{1,0:T(8,128)S(1)}, u32[]{:S(2)}, u32[]{:S(2)}) collective-permute-start(f32[6,128]{1,0:T(8,128)S(1)} %shard_map.85.gains), channel_id=1, source_target_pairs={{0,1},{1,0},{2,3},{3,2},{4,5},{5,4},{6,7},{7,6},{8,9},{9,8},{10,11... | collective-permute-start | bytes 9224 | tf_op jit(solution)/shard_map/ppermute | solution.py:20
  99.8 3.5 %collective-permute-start.11 = (bf16[640,256]{1,0:T(8,128)(2,1)S(1)}, bf16[640,256]{1,0:T(8,128)(2,1)S(1)}, u32[]{:S(2)}, u32[]{:S(2)}) collective-permute-start(bf16[640,256]{1,0:T(8,128)(2,1)S(1)} %shard_map.87.refs_3_), channel_id=1, source_target_pairs={{0,1},{1,0},{2,3},{3,2},{4,5},{5,4},{6,7},{7,6},{8,9},{9,8},{10,11... | collective-permute-start | bytes 983048 | tf_op jit(solution)/shard_map/ppermute | solution.py:20
